TPU v7x, 32 devices: a whole 2x2x4 slice. The times are simulated.
32 devices in a mesh: task: 4 (over x, core), row: 8 (over z, y).
Axes of the slice: x: 2, y: 2, z: 4, core: 2. Of those that a mesh axis runs over, the one named last changes fastest.
Arguments:
- task_delta: bfloat16 [4, 28672, 4096], P('task', 'row'), may hold values from -16 to 16
- start_block: float32 [4, 4096, 32], P('task'), may hold values from -6 to 6
Outputs:
- merged: bfloat16 [28672, 4096], P(('row', 'task'))
All inputs are finite; a program needn't handle non-finite values.
Results may differ from a plain program's by a relative error of at most 0.013.
Values may be sent and summed in bfloat16 or wider, within the bound.
No kernel may reach another device: no remote copies, remote signals or barrier semaphores. Data moves between devices by JAX's collectives and lax.ppermute only.
A program may use at most 128 MiB of HBM per device.

v0:
```python
import functools

import jax
import jax.numpy as jnp
from jax import lax
from jax.experimental import pallas as pl
from jax.experimental.pallas import tpu as pltpu
from jax.sharding import PartitionSpec as P

ITERS = 4
ROOT_STEPS = 12
LANES = 128
TILE = 8
F32 = jnp.float32
BF16 = jnp.bfloat16
ROWS_BY_ROWS = (((1,), (1,)), ((), ()))
VMEM_BYTES = 16 * 1024 * 1024
IN_VMEM = pl.BlockSpec(memory_space=pltpu.VMEM)
ANYWHERE = pl.BlockSpec(memory_space=pl.ANY)


def shape_of(shape, kind):
    return jax.ShapeDtypeStruct(shape, kind)


def call(kernel, name, operands, shapes, scratch=(), held=None, idle=(), flops=10**8):
    operands = [*operands, *idle]
    specs = [IN_VMEM] * (len(operands) - len(idle)) + [ANYWHERE] * len(idle)
    if held is not None:
        operands, specs = [held, *operands], [IN_VMEM, *specs]
    return pl.pallas_call(
        kernel,
        out_shape=tuple(shapes),
        in_specs=specs,
        out_specs=(IN_VMEM,) * len(shapes),
        scratch_shapes=list(scratch),
        cost_estimate=pl.CostEstimate(flops=flops, bytes_accessed=10**6, transcendentals=0),
        compiler_params=pltpu.CompilerParams(vmem_limit_bytes=VMEM_BYTES),
        name=name,
    )(*operands)


def split_two(value):
    high = value.astype(BF16)
    return high, (value - high.astype(F32)).astype(BF16)


def split_three(value):
    high = value.astype(BF16)
    rest = value - high.astype(F32)
    middle = rest.astype(BF16)
    return high, middle, (rest - middle.astype(F32)).astype(BF16)


def spread(value, order, axis):
    pieces = split_three(value)
    return jnp.concatenate([pieces[at] for at in order], axis=axis)


def square(left, right):
    return jnp.dot(
        spread(left, (0, 0, 1, 0, 2, 1), 1), spread(right, (0, 1, 0, 2, 0, 1), 0), preferred_element_type=F32
    )


def eye_of(size):
    return lax.broadcasted_iota(jnp.int32, (size, size), 0) == lax.broadcasted_iota(jnp.int32, (size, size), 1)


def tree_sum(values):
    while len(values) > 1:
        values = [values[at] + values[at + 1] for at in range(0, len(values), 2)]
    return values[0]


def lower_inverse(grams):
    size = grams[0].shape[0]
    tiles = size // TILE
    rows = lax.broadcasted_iota(jnp.int32, (TILE, LANES), 0)
    lanes = lax.broadcasted_iota(jnp.int32, (TILE, LANES), 1)
    columns, inverses, scales = [], [], []
    for gram in grams:
        wide = [jnp.broadcast_to(gram[:, at : at + 1], (size, LANES)) for at in range(size)]
        columns.append([[one[TILE * tile : TILE * (tile + 1)] for tile in range(tiles)] for one in wide])
        inverses.append([(rows + TILE * tile == lanes).astype(F32) for tile in range(tiles)])
        scales.append([jnp.zeros((TILE, LANES), F32) for _ in range(tiles)])
    for step in range(size):
        top, place = divmod(step, TILE)
        for cols, inverse, scale in zip(columns, inverses, scales):
            pivot = cols[step][top][place : place + 1]
            reciprocal = 1.0 / pivot
            ratio = [None] * top + [cols[step][tile] * reciprocal for tile in range(top, tiles)]
            for later in range(step + 1, size):
                first, inner = divmod(later, TILE)
                factor = ratio[first][inner : inner + 1]
                for tile in range(first, tiles):
                    cols[later][tile] = cols[later][tile] - cols[step][tile] * factor
            own = inverse[top][place : place + 1]
            for tile in range(top, tiles):
                factor = jnp.where(rows > place, ratio[tile], 0.0) if tile == top else ratio[tile]
                inverse[tile] = inverse[tile] - factor * own
            scale[top] = jnp.where(rows == place, lax.rsqrt(pivot), scale[top])
    return [
        jnp.concatenate([one * down for one, down in zip(inverse, scale)], axis=0)[:, :size]
        for inverse, scale in zip(inverses, scales)
    ]


def gram_pieces(images):
    return with_pieces(lax.dot_general(images, images, ROWS_BY_ROWS, preferred_element_type=F32))


def tall_of(rows, *sizes):
    return next(size for size in (*sizes, rows) if rows % size == 0)


def partner(axis, mask):
    return lax.bitwise_xor(lax.axis_index(axis).astype(jnp.int32), jnp.int32(mask))


def block_at(index, size):
    return pl.ds(pl.multiple_of(index * size, size), size)


def first_kernel(tall, d_ref, x_ref, out_ref, gram_ref, wide):
    wide[...] = x_ref[...].astype(BF16)

    def body(at, carry):
        rows = block_at(at, tall)
        product = lax.dot_general(d_ref[rows, :], wide[...], ROWS_BY_ROWS, preferred_element_type=F32)
        out_ref[:, rows] = product.T.astype(BF16)
        return carry

    lax.fori_loop(0, d_ref.shape[0] // tall, body, 0)
    gram_ref[...] = gram_pieces(out_ref[...])


def first(held, start):
    rows, cols = held.shape
    rank = start.shape[0]
    return call(
        functools.partial(first_kernel, tall_of(rows, 896, 512, 256, 128)),
        "first",
        [start],
        [shape_of((rank, rows), BF16), shape_of((rank, LANES), BF16)],
        [pltpu.VMEM((rank, cols), BF16)],
        held=held,
        flops=2 * rows * cols * 384,
    )


def with_pieces(gram):
    rank = gram.shape[0]
    return jnp.concatenate([*split_three(gram), jnp.zeros((rank, LANES - 3 * rank), BF16)], axis=1)


def from_pieces(pieces):
    rank = pieces.shape[0]
    pieces = pieces.astype(F32)
    return pieces[:, :rank] + pieces[:, rank : 2 * rank] + pieces[:, 2 * rank : 3 * rank]


def backs_kernel(mask, d_ref, images_ref, gram_ref, *refs):
    out_ref = refs[-1]
    chunk = out_ref.shape[1] - LANES
    across = tall_of(chunk, 512)
    out_ref[:, :LANES] = gram_ref[...].astype(out_ref.dtype)
    for at in range(0, chunk, across):
        span = block_at(lax.div(partner("row", mask), 2) * (chunk // across) + at // across, across)
        out_ref[:, LANES + at : LANES + at + across] = jnp.dot(
            images_ref[...], d_ref[:, span], preferred_element_type=F32
        ).astype(out_ref.dtype)


def backs(held, panel, gram, mask, count, *after):
    rows, cols = held.shape
    rank = panel.shape[0]
    return call(
        functools.partial(backs_kernel, mask),
        "backs",
        [panel, gram],
        [shape_of((rank, LANES + cols // count), BF16 if mask else F32)],
        held=held,
        idle=after,
        flops=10**6,
    )[0]


def combine_kernel(_, *refs):
    *in_refs, out_ref = refs
    gram = tree_sum([from_pieces(ref[:, :LANES]) for ref in in_refs])
    out_ref[:, :LANES] = with_pieces(gram)
    out_ref[:, LANES:] = tree_sum([ref[:, LANES:].astype(F32) for ref in in_refs]).astype(BF16)


def settle_kernel(_, one_ref, other_ref, out_ref):
    rank = one_ref.shape[0]
    gram = from_pieces(one_ref[:, :LANES]) + from_pieces(other_ref[:, :LANES])
    total = one_ref[:, LANES:].astype(F32) + other_ref[:, LANES:].astype(F32)
    out_ref[...] = square(lower_inverse([gram])[0], total).astype(BF16)


def combine(held, pieces):
    return call(combine_kernel, "combine", pieces, [shape_of(pieces[0].shape, BF16)], held=held)[0]


def settle(held, one, other):
    rank, wide = one.shape
    return call(settle_kernel, "settle", [one, other], [shape_of((rank, wide - LANES), BF16)], held=held)[0]


def images_kernel(masks, tall, partial, tasks, d_ref, *refs):
    x_refs, refs = refs[: len(masks)], refs[len(masks) :]
    if partial:
        sum_ref, refs = refs[0], refs[1:]
    target = refs[1] if tasks else refs[0]
    chunk = x_refs[0].shape[1]

    def body(at, carry):
        rows = block_at(at, tall)
        product = None
        for mask, x_ref in zip(masks, x_refs):
            span = block_at(lax.div(partner("row", mask), 2), chunk)
            term = lax.dot_general(d_ref[rows, span], x_ref[...], ROWS_BY_ROWS, preferred_element_type=F32)
            product = term if product is None else product + term
        product = product.T
        if partial:
            product = product + sum_ref[:, rows]
        target[:, rows] = product.astype(target.dtype)
        return carry

    lax.fori_loop(0, d_ref.shape[0] // tall, body, 0)
    if tasks:
        out_ref, flat = refs
        each = out_ref.shape[2]
        for at in range(tasks):
            out_ref[at] = flat[:, at * each : (at + 1) * each]
    elif len(refs) == 2:
        refs[1][...] = gram_pieces(refs[0][...])


def images(held, blocks, masks, partial=None, last=False, tasks=0):
    rows, cols = held.shape
    rank, chunk = blocks[0].shape
    scratch = ()
    if tasks:
        shapes = [shape_of((tasks, rank, rows // tasks), BF16)]
        scratch = [pltpu.VMEM((rank, rows), BF16)]
    elif last:
        shapes = [shape_of((rank, rows), BF16), shape_of((rank, LANES), BF16)]
    else:
        shapes = [shape_of((rank, rows), F32)]
    return call(
        functools.partial(images_kernel, masks, tall_of(rows, 896, 512, 256, 128), partial is not None, tasks),
        "images",
        [*blocks] + ([] if partial is None else [partial]),
        shapes,
        scratch,
        held=held,
        flops=2 * rows * chunk * 384 * len(masks),
    )


def join_kernel(first, *refs):
    in_refs, out_ref = refs[first : first + 2], refs[-1]
    if len(out_ref.shape) == 2:
        out_ref[...] = jnp.concatenate([ref[...] for ref in in_refs], axis=1)
    else:
        for at, ref in enumerate(in_refs):
            out_ref[at * ref.shape[0] : (at + 1) * ref.shape[0]] = ref[...]


def join(one, other, held=None, axis=0, after=()):
    shape = list(one.shape)
    shape[axis] *= 2
    kernel = functools.partial(join_kernel, 0 if held is None else 1)
    return call(kernel, "join", [one, other], [shape_of(tuple(shape), one.dtype)], held=held, idle=after)[0]


def pack_kernel(masks, _, *refs):
    *in_refs, out_ref = refs
    chunk = in_refs[0].shape[1]
    for mask, in_ref in zip(masks, in_refs):
        out_ref[0, :, block_at(lax.div(partner("row", mask), 2), chunk)] = in_ref[...]


def left_kernel(groups, *refs):
    in_refs, (gram_ref, panel_ref, whole) = refs[: len(groups)], refs[-3:]
    tasks, rank, each = in_refs[0].shape[-3:]
    for masks, in_ref in zip(groups, in_refs):
        for place, mask in enumerate(masks):
            down = block_at(partner("task", mask), rank)
            for at in range(tasks):
                whole[down, at * each : (at + 1) * each] = in_ref[place, at]
            panel_ref[down, :] = in_ref[place, partner("task", 0)]
    gram_ref[...] = lax.dot_general(whole[...], whole[...], ROWS_BY_ROWS, preferred_element_type=F32)


def left(blocks, groups, after):
    _, tasks, rank, each = blocks[0].shape
    size = tasks * rank
    return call(
        functools.partial(left_kernel, groups),
        "left",
        blocks,
        [shape_of((size, size), F32), shape_of((size, each), BF16)],
        [pltpu.VMEM((size, tasks * each), BF16)],
        idle=[after],
    )


def add_kernel(one_ref, other_ref, *refs):
    refs[-1][...] = one_ref[...] + other_ref[...]


def add(one, other, *after):
    return call(add_kernel, "add", [one, other], [shape_of(one.shape, F32)], idle=after, flops=10**6)[0]


def root_begin(gram):
    return gram / jnp.sqrt(jnp.sum(gram * gram)), eye_of(gram.shape[0]).astype(F32)


def root_steps(state, count):
    identity = eye_of(state[0].shape[0]).astype(F32)

    def step(_, state):
        upper, lower = state
        middle = 0.5 * (3.0 * identity - square(lower, upper))
        both = square(middle, jnp.concatenate([upper, lower], axis=1))
        return both[:, : identity.shape[0]], both[:, identity.shape[0] :]

    return lax.fori_loop(0, count, step, state)


def root_end(state, gram):
    return state[1] / jnp.sqrt(jnp.sqrt(jnp.sum(gram * gram)))


def right_first_kernel(groups, *refs):
    in_refs, (wide_ref, lower_ref, gram_ref) = refs[: len(groups)], refs[-3:]
    rank = in_refs[0].shape[1]
    for masks, in_ref in zip(groups, in_refs):
        for place, mask in enumerate(masks):
            wide_ref[block_at(partner("task", mask), rank), :] = in_ref[place]
    wide = wide_ref[...]
    raw = lax.dot_general(wide, wide, ROWS_BY_ROWS, preferred_element_type=F32)
    spans = [slice(task * rank, (task + 1) * rank) for task in range(wide.shape[0] // rank)]
    lower_ref[...] = jnp.zeros_like(lower_ref)
    for span, inverse in zip(spans, lower_inverse([raw[span, span] for span in spans])):
        lower_ref[span, span] = inverse
    lower = lower_ref[...]
    gram_ref[...] = square(square(lower, raw), lower.T)


def right_begin_kernel(count, gram_ref, upper_ref, lower_ref):
    upper_ref[...], lower_ref[...] = root_steps(root_begin(gram_ref[...]), count)


def right_steps_kernel(count, upper_in, lower_in, upper_ref, lower_ref):
    upper_ref[...], lower_ref[...] = root_steps((upper_in[...], lower_in[...]), count)


def right_end_kernel(count, gram_ref, upper_ref, lower_ref, change_ref, *refs):
    state = root_steps((upper_ref[...], lower_ref[...]), count)
    refs[-1][...] = square(root_end(state, gram_ref[...]).T, change_ref[...])


def finish_kernel(one_ref, other_ref, panel_ref, wide_ref, lower_ref, right_ref, out_ref, side):
    size = lower_ref.shape[0]

    @pl.when(pl.program_id(0) == 0)
    def _():
        lower = lower_ref[...]
        gram = square(square(lower, one_ref[...] + other_ref[...]), lower.T)
        diagonal = jnp.where(eye_of(size), gram, 0.0)
        down = jnp.sqrt(jnp.sum(diagonal, axis=1, keepdims=True))
        across = jnp.sqrt(jnp.sum(diagonal, axis=0, keepdims=True))
        normed = gram / (down * across)
        mixing = root_end(root_steps(root_begin(normed), ROOT_STEPS), normed) / down * across
        mixed = square(square(lower.T, mixing), right_ref[...])
        panel = panel_ref[...].T
        product = jnp.dot(
            jnp.concatenate([panel, panel], axis=1),
            jnp.concatenate(split_two(mixed), axis=0),
            preferred_element_type=F32,
        )
        side[...] = jnp.concatenate(split_two(product), axis=1)

    wide = wide_ref[...]
    out_ref[...] = jnp.dot(
        side[...], jnp.concatenate([wide, wide], axis=0), preferred_element_type=F32
    ).astype(BF16)


def finish(one, other, panel, wide, lower, right_side):
    size, rows = panel.shape
    cols = wide.shape[1]
    across = 512

    def whole(array):
        return pl.BlockSpec(array.shape, lambda at: (0, 0))

    return pl.pallas_call(
        finish_kernel,
        out_shape=shape_of((rows, cols), BF16),
        grid=(cols // across,),
        in_specs=[
            whole(one),
            whole(other),
            whole(panel),
            pl.BlockSpec((size, across), lambda at: (0, at)),
            whole(lower),
            whole(right_side),
        ],
        out_specs=pl.BlockSpec((rows, across), lambda at: (0, at)),
        scratch_shapes=[pltpu.VMEM((rows, 2 * size), BF16)],
        compiler_params=pltpu.CompilerParams(vmem_limit_bytes=VMEM_BYTES),
        name="finish",
    )(one, other, panel, wide, lower, right_side)


def send(piece, axis, mask, count):
    return lax.ppermute(piece, axis, [(at, at ^ mask) for at in range(count)])


def gather(piece, axis, count, joining):
    masks, groups, blocks, block = [0], [(0,)], [piece], piece
    bit = count // 2
    while bit:
        received = send(block, axis, bit, count)
        groups.append(tuple(mask ^ bit for mask in masks))
        blocks.append(received)
        masks = masks + [mask ^ bit for mask in masks]
        bit //= 2
        if bit:
            block = joining(block, received)
    return groups, blocks


def local(tasks, parts, task_delta, start_block):
    masks = tuple(range(0, parts, 2))
    nearest, farther = masks[1], masks[2:]
    count = len(masks)
    order = (*reversed(masks[1:]), 0)
    held = pltpu.with_memory_space_constraint(task_delta[0], pltpu.VMEM)
    panel, gram = first(held, start_block[0].T)
    for step in range(ITERS):
        last = step == ITERS - 1
        received, after = {}, []
        for mask in order[:-1]:
            piece = backs(held, panel, gram, mask, count, *after)
            received[mask] = send(piece, "row", mask, parts)
            after = [piece]
        keep = backs(held, panel, gram, 0, count, *after, received[order[0]])
        sums = combine(held, [keep, *[received[mask] for mask in masks[1:]]])
        block = settle(held, sums, send(sums, "row", 1, parts))
        blocks = {mask: send(block, "row", mask, parts) for mask in order[:-1]}
        blocks[0] = block
        (partial,) = images(held, [block], (0,))
        (partial,) = images(held, [blocks[nearest]], (nearest,), partial)
        rest = [blocks[mask] for mask in farther]
        if last:
            (own,) = call(
                functools.partial(pack_kernel, masks),
                "pack",
                [blocks[mask] for mask in masks],
                [shape_of((1, block.shape[0], held.shape[1]), BF16)],
                held=held,
            )
            (panel,) = images(held, rest, farther, partial, tasks=tasks)
        else:
            panel, gram = images(held, rest, farther, partial, last=True)
    task_groups, bases = gather(own, "task", tasks, lambda one, other: join(one, other, after=[panel]))
    size = tasks * start_block.shape[2]
    square_shape = shape_of((size, size), F32)
    wide, lower, right_gram = call(
        functools.partial(right_first_kernel, task_groups),
        "right_first",
        bases,
        [shape_of((size, held.shape[1]), BF16), square_shape, square_shape],
    )
    begin, middle = ROOT_STEPS // 2, ROOT_STEPS // 6
    state = call(functools.partial(right_begin_kernel, begin), "right_begin", [right_gram], [square_shape] * 2)
    _, panels = gather(panel[None], "task", tasks, lambda one, other: join(one, other, after=[state[0]]))
    state = call(functools.partial(right_steps_kernel, middle), "right_steps", state, [square_shape] * 2)
    gram, panel = left(panels, task_groups, state[0])
    bit = parts // 2
    other = send(gram, "row", bit, parts)
    (right_side,) = call(
        functools.partial(right_end_kernel, ROOT_STEPS - begin - middle),
        "right_end",
        [right_gram, *state, lower],
        [square_shape],
        idle=[gram],
    )
    after = [right_side]
    while bit > 1:
        gram, after = add(gram, other, *after), []
        bit //= 2
        other = send(gram, "row", bit, parts)
    return finish(gram, other, panel, wide, lower, right_side)


def solution(mesh):
    tasks, parts = mesh.shape["task"], mesh.shape["row"]
    placed = (P("task", "row", None), P("task", None, None))
    return jax.shard_map(
        functools.partial(local, tasks, parts),
        mesh=mesh,
        in_specs=placed,
        out_specs=P(("row", "task"), None),
        check_vma=False,
    )
```

profile of v0, /device:TPU:0, one launch (start us, length us, event | category | flops | bytes accessed | tf_op | source)
XLA Modules:
  0.0 191.8 jit_solution(5541725366767945965)
XLA Ops:
  0.0 9.3 %copy-done = bf16[1,3584,4096]{2,1,0:T(8,128)(2,1)S(1)} copy-done((bf16[1,3584,4096]{2,1,0:T(8,128)(2,1)S(1)}, bf16[1,3584,4096]{2,1,0:T(8,128)(2,1)}, u32[]{:S(2)}) %copy-start) | copy-done | bytes 29360152
  10.4 8.6 %first.1 = (bf16[32,3584]{1,0:T(8,128)(2,1)S(1)}, bf16[32,128]{1,0:T(8,128)(2,1)S(1)}) custom-call(bf16[3584,4096]{1,0:T(8,128)(2,1)S(1)} %bitcast.5, f32[32,4096]{1,0:T(8,128)S(1)} %bitcast.46), custom_call_target="tpu_custom_call" | custom-call | flops 11274289152 | bytes 1000000 | tf_op jit(solution)/shard_map/first/pallas_call | solution.py:31
  19.0 1.4 backs.16.refs_0_
  20.4 5.0 %collective-permute-start = (bf16[32,1152]{1,0:T(8,128)(2,1)S(1)}, bf16[32,1152]{1,0:T(8,128)(2,1)S(1)}, u32[]{:S(2)}, u32[]{:S(2)}) collective-permute-start(bf16[32,1152]{1,0:T(8,128)(2,1)S(1)} %backs.16.refs_0_), channel_id=1, source_target_pairs={{0,6},{1,7},{2,4},{3,5},{4,2},{5,3},{6,0},{7,1},{8,14},{9,15},{10,... | collective-permute-start | bytes 221192 | tf_op jit(solution)/shard_map/ppermute | solution.py:424
  25.4 1.3 backs.17.refs_0_
  26.8 1.4 backs.18.refs_0_
  28.7 1.3 backs.19.refs_0_
  30.1 2.8 %collective-permute-done.1.refs_1_ = bf16[32,1152]{1,0:T(8,128)(2,1)S(1)} collective-permute-done((bf16[32,1152]{1,0:T(8,128)(2,1)S(1)}, bf16[32,1152]{1,0:T(8,128)(2,1)S(1)}, u32[]{:S(2)}, u32[]{:S(2)}) %collective-permute-start.1) | collective-permute-done | bytes 73760 | tf_op jit(solution)/shard_map/ppermute | solution.py:424
  34.1 1.6 collective-permute-start.3
  35.7 2.8 %collective-permute-done.3.other_ref = bf16[32,1152]{1,0:T(8,128)(2,1)S(1)} collective-permute-done((bf16[32,1152]{1,0:T(8,128)(2,1)S(1)}, bf16[32,1152]{1,0:T(8,128)(2,1)S(1)}, u32[]{:S(2)}, u32[]{:S(2)}) %collective-permute-start.3) | collective-permute-done | bytes 73760 | tf_op jit(solution)/shard_map/ppermute | solution.py:424
  39.5 1.5 collective-permute-start.6
  41.7 1.3 collective-permute-start.4
  43.0 2.6 %images.12.refs_1_ = f32[32,3584]{1,0:T(8,128)S(1)} custom-call(bf16[3584,4096]{1,0:T(8,128)(2,1)S(1)} %bitcast.12, bf16[32,1024]{1,0:T(8,128)(2,1)S(1)} %settle.4.refs_0_), custom_call_target="tpu_custom_call" | custom-call | flops 2818572288 | bytes 1000000 | tf_op jit(solution)/shard_map/images/pallas_call | solution.py:31
  45.7 2.6 %images.13.refs_2_ = f32[32,3584]{1,0:T(8,128)S(1)} custom-call(bf16[3584,4096]{1,0:T(8,128)(2,1)S(1)} %bitcast.13, bf16[32,1024]{1,0:T(8,128)(2,1)S(1)} %collective-permute-done.6.refs_0_, f32[32,3584]{1,0:T(8,128)S(1)} %images.12.refs_1_), custom_call_target="tpu_custom_call" | custom-call | flops 2818572288 | bytes 1000000 | tf_op jit(solution)/shard_map/images/pallas_call | solution.py:31
  48.3 4.8 %images.14 = (bf16[32,3584]{1,0:T(8,128)(2,1)S(1)}, bf16[32,128]{1,0:T(8,128)(2,1)S(1)}) custom-call(bf16[3584,4096]{1,0:T(8,128)(2,1)S(1)} %bitcast.14, bf16[32,1024]{1,0:T(8,128)(2,1)S(1)} %collective-permute-done.4.refs_0_, bf16[32,1024]{1,0:T(8,128)(2,1)S(1)} %collective-permute-done.5.refs_1_, f32[32,3584]{1,0:T(8,128)S(1)} %images.13.refs_2_), custom_call_target="tpu_custom_call" | custom-call | flops 5637144576 | bytes 1000000 | tf_op jit(solution)/shard_map/images/pallas_call | solution.py:31
  53.2 1.4 backs.20.refs_0_
  54.5 1.4 backs.21.refs_0_
  55.9 1.9 collective-permute-start.7
  57.8 1.3 backs.22.refs_0_
  59.6 2.0 %collective-permute-start.9 = (bf16[32,1152]{1,0:T(8,128)(2,1)S(1)}, bf16[32,1152]{1,0:T(8,128)(2,1)S(1)}, u32[]{:S(2)}, u32[]{:S(2)}) collective-permute-start(bf16[32,1152]{1,0:T(8,128)(2,1)S(1)} %backs.21.refs_0_), channel_id=1, source_target_pairs={{0,4},{1,5},{2,6},{3,7},{4,0},{5,1},{6,2},{7,3},{8,12},{9,13},{10,... | collective-permute-start | bytes 221192 | tf_op jit(solution)/shard_map/ppermute | solution.py:424
  62.1 1.3 backs.23.refs_0_
  63.5 1.4 collective-permute-done.9.refs_2_
  65.1 1.6 collective-permute-start.10
  66.6 2.8 %collective-permute-done.10.other_ref = bf16[32,1152]{1,0:T(8,128)(2,1)S(1)} collective-permute-done((bf16[32,1152]{1,0:T(8,128)(2,1)S(1)}, bf16[32,1152]{1,0:T(8,128)(2,1)S(1)}, u32[]{:S(2)}, u32[]{:S(2)}) %collective-permute-start.10) | collective-permute-done | bytes 73760 | tf_op jit(solution)/shard_map/ppermute | solution.py:424
  70.4 1.6 collective-permute-start.13
  72.0 2.3 %collective-permute-start.12 = (bf16[32,1024]{1,0:T(8,128)(2,1)S(1)}, bf16[32,1024]{1,0:T(8,128)(2,1)S(1)}, u32[]{:S(2)}, u32[]{:S(2)}) collective-permute-start(bf16[32,1024]{1,0:T(8,128)(2,1)S(1)} %settle.5.refs_0_), channel_id=1, source_target_pairs={{0,6},{1,7},{2,4},{3,5},{4,2},{5,3},{6,0},{7,1},{8,14},{9,15},{10,... | collective-permute-start | bytes 196616 | tf_op jit(solution)/shard_map/ppermute | solution.py:424
  74.8 2.6 %images.15.refs_1_ = f32[32,3584]{1,0:T(8,128)S(1)} custom-call(bf16[3584,4096]{1,0:T(8,128)(2,1)S(1)} %bitcast.21, bf16[32,1024]{1,0:T(8,128)(2,1)S(1)} %settle.5.refs_0_), custom_call_target="tpu_custom_call" | custom-call | flops 2818572288 | bytes 1000000 | tf_op jit(solution)/shard_map/images/pallas_call | solution.py:31
  77.4 2.6 %images.16.refs_2_ = f32[32,3584]{1,0:T(8,128)S(1)} custom-call(bf16[3584,4096]{1,0:T(8,128)(2,1)S(1)} %bitcast.22, bf16[32,1024]{1,0:T(8,128)(2,1)S(1)} %collective-permute-done.13.refs_0_, f32[32,3584]{1,0:T(8,128)S(1)} %images.15.refs_1_), custom_call_target="tpu_custom_call" | custom-call | flops 2818572288 | bytes 1000000 | tf_op jit(solution)/shard_map/images/pallas_call | solution.py:31
  80.1 4.8 %images.17 = (bf16[32,3584]{1,0:T(8,128)(2,1)S(1)}, bf16[32,128]{1,0:T(8,128)(2,1)S(1)}) custom-call(bf16[3584,4096]{1,0:T(8,128)(2,1)S(1)} %bitcast.23, bf16[32,1024]{1,0:T(8,128)(2,1)S(1)} %collective-permute-done.11.refs_0_, bf16[32,1024]{1,0:T(8,128)(2,1)S(1)} %collective-permute-done.12.refs_1_, f32[32,3584]{1,0:T(8,128)S(1)} %images.16.refs_2_), custom_call_target="tpu_custom_call" | custom-call | flops 5637144576 | bytes 1000000 | tf_op jit(solution)/shard_map/images/pallas_call | solution.py:31
  85.0 1.4 backs.24.refs_0_
  86.3 1.4 backs.25.refs_0_
  87.7 2.8 %collective-permute-start.14 = (bf16[32,1152]{1,0:T(8,128)(2,1)S(1)}, bf16[32,1152]{1,0:T(8,128)(2,1)S(1)}, u32[]{:S(2)}, u32[]{:S(2)}) collective-permute-start(bf16[32,1152]{1,0:T(8,128)(2,1)S(1)} %backs.24.refs_0_), channel_id=1, source_target_pairs={{0,6},{1,7},{2,4},{3,5},{4,2},{5,3},{6,0},{7,1},{8,14},{9,15},{10,... | collective-permute-start | bytes 221192 | tf_op jit(solution)/shard_map/ppermute | solution.py:424
  90.5 1.3 backs.26.refs_0_
  92.0 1.5 collective-permute-start.16
  93.9 1.3 backs.27.refs_0_
  97.4 1.6 collective-permute-start.17
  99.0 2.8 %collective-permute-done.17.other_ref = bf16[32,1152]{1,0:T(8,128)(2,1)S(1)} collective-permute-done((bf16[32,1152]{1,0:T(8,128)(2,1)S(1)}, bf16[32,1152]{1,0:T(8,128)(2,1)S(1)}, u32[]{:S(2)}, u32[]{:S(2)}) %collective-permute-start.17) | collective-permute-done | bytes 73760 | tf_op jit(solution)/shard_map/ppermute | solution.py:424
  102.8 2.8 %collective-permute-start.20 = (bf16[32,1024]{1,0:T(8,128)(2,1)S(1)}, bf16[32,1024]{1,0:T(8,128)(2,1)S(1)}, u32[]{:S(2)}, u32[]{:S(2)}) collective-permute-start(bf16[32,1024]{1,0:T(8,128)(2,1)S(1)} %settle.6.refs_0_), channel_id=1, source_target_pairs={{0,2},{1,3},{2,0},{3,1},{4,6},{5,7},{6,4},{7,5},{8,10},{9,11},{10,... | collective-permute-start | bytes 196616 | tf_op jit(solution)/shard_map/ppermute | solution.py:424
  107.1 2.6 %images.18.refs_1_ = f32[32,3584]{1,0:T(8,128)S(1)} custom-call(bf16[3584,4096]{1,0:T(8,128)(2,1)S(1)} %bitcast.30, bf16[32,1024]{1,0:T(8,128)(2,1)S(1)} %settle.6.refs_0_), custom_call_target="tpu_custom_call" | custom-call | flops 2818572288 | bytes 1000000 | tf_op jit(solution)/shard_map/images/pallas_call | solution.py:31
  109.7 2.6 %images.19.refs_2_ = f32[32,3584]{1,0:T(8,128)S(1)} custom-call(bf16[3584,4096]{1,0:T(8,128)(2,1)S(1)} %bitcast.31, bf16[32,1024]{1,0:T(8,128)(2,1)S(1)} %collective-permute-done.20.refs_0_, f32[32,3584]{1,0:T(8,128)S(1)} %images.18.refs_1_), custom_call_target="tpu_custom_call" | custom-call | flops 2818572288 | bytes 1000000 | tf_op jit(solution)/shard_map/images/pallas_call | solution.py:31
  112.4 5.0 %images.20 = (bf16[32,3584]{1,0:T(8,128)(2,1)S(1)}, bf16[32,128]{1,0:T(8,128)(2,1)S(1)}) custom-call(bf16[3584,4096]{1,0:T(8,128)(2,1)S(1)} %bitcast.32, bf16[32,1024]{1,0:T(8,128)(2,1)S(1)} %collective-permute-done.18.refs_0_, bf16[32,1024]{1,0:T(8,128)(2,1)S(1)} %collective-permute-done.19.refs_1_, f32[32,3584]{1,0:T(8,128)S(1)} %images.19.refs_2_), custom_call_target="tpu_custom_call" | custom-call | flops 5637144576 | bytes 1000000 | tf_op jit(solution)/shard_map/images/pallas_call | solution.py:31
  117.4 1.4 backs.28.refs_0_
  118.8 1.4 backs.29.refs_0_
  120.1 2.3 %collective-permute-start.21 = (bf16[32,1152]{1,0:T(8,128)(2,1)S(1)}, bf16[32,1152]{1,0:T(8,128)(2,1)S(1)}, u32[]{:S(2)}, u32[]{:S(2)}) collective-permute-start(bf16[32,1152]{1,0:T(8,128)(2,1)S(1)} %backs.28.refs_0_), channel_id=1, source_target_pairs={{0,6},{1,7},{2,4},{3,5},{4,2},{5,3},{6,0},{7,1},{8,14},{9,15},{10,... | collective-permute-start | bytes 221192 | tf_op jit(solution)/shard_map/ppermute | solution.py:424
  122.4 1.3 backs.30.refs_0_
  124.4 1.5 collective-permute-start.23
  126.4 1.3 backs.31.refs_0_
  129.0 2.7 %collective-permute-done.23.refs_2_ = bf16[32,1152]{1,0:T(8,128)(2,1)S(1)} collective-permute-done((bf16[32,1152]{1,0:T(8,128)(2,1)S(1)}, bf16[32,1152]{1,0:T(8,128)(2,1)S(1)}, u32[]{:S(2)}, u32[]{:S(2)}) %collective-permute-start.23) | collective-permute-done | bytes 73760 | tf_op jit(solution)/shard_map/ppermute | solution.py:424
  131.9 1.5 collective-permute-start.24
  133.4 2.9 %collective-permute-done.24.other_ref = bf16[32,1152]{1,0:T(8,128)(2,1)S(1)} collective-permute-done((bf16[32,1152]{1,0:T(8,128)(2,1)S(1)}, bf16[32,1152]{1,0:T(8,128)(2,1)S(1)}, u32[]{:S(2)}, u32[]{:S(2)}) %collective-permute-start.24) | collective-permute-done | bytes 73760 | tf_op jit(solution)/shard_map/ppermute | solution.py:424
  137.3 2.3 %collective-permute-start.26 = (bf16[32,1024]{1,0:T(8,128)(2,1)S(1)}, bf16[32,1024]{1,0:T(8,128)(2,1)S(1)}, u32[]{:S(2)}, u32[]{:S(2)}) collective-permute-start(bf16[32,1024]{1,0:T(8,128)(2,1)S(1)} %settle.7.refs_0_), channel_id=1, source_target_pairs={{0,6},{1,7},{2,4},{3,5},{4,2},{5,3},{6,0},{7,1},{8,14},{9,15},{10,... | collective-permute-start | bytes 196616 | tf_op jit(solution)/shard_map/ppermute | solution.py:424
  140.8 2.6 %images.21.refs_1_ = f32[32,3584]{1,0:T(8,128)S(1)} custom-call(bf16[3584,4096]{1,0:T(8,128)(2,1)S(1)} %bitcast.39, bf16[32,1024]{1,0:T(8,128)(2,1)S(1)} %settle.7.refs_0_), custom_call_target="tpu_custom_call" | custom-call | flops 2818572288 | bytes 1000000 | tf_op jit(solution)/shard_map/images/pallas_call | solution.py:31
  143.6 1.9 %collective-permute-done.25.refs_0_.refs_2_ = bf16[32,1024]{1,0:T(8,128)(2,1)S(1)} collective-permute-done((bf16[32,1024]{1,0:T(8,128)(2,1)S(1)}, bf16[32,1024]{1,0:T(8,128)(2,1)S(1)}, u32[]{:S(2)}, u32[]{:S(2)}) %collective-permute-start.25) | collective-permute-done | bytes 65568 | tf_op jit(solution)/shard_map/ppermute | solution.py:424
  145.6 1.6 collective-permute-start.29
  147.1 2.6 %images.22.refs_2_ = f32[32,3584]{1,0:T(8,128)S(1)} custom-call(bf16[3584,4096]{1,0:T(8,128)(2,1)S(1)} %bitcast.41, bf16[32,1024]{1,0:T(8,128)(2,1)S(1)} %collective-permute-done.27.refs_0_.refs_1_, f32[32,3584]{1,0:T(8,128)S(1)} %images.21.refs_1_), custom_call_target="tpu_custom_call" | custom-call | flops 2818572288 | bytes 1000000 | tf_op jit(solution)/shard_map/images/pallas_call | solution.py:31
  149.7 4.6 %images.23.refs_2_ = bf16[4,32,896]{2,1,0:T(8,128)(2,1)S(1)} custom-call(bf16[3584,4096]{1,0:T(8,128)(2,1)S(1)} %bitcast.42, bf16[32,1024]{1,0:T(8,128)(2,1)S(1)} %collective-permute-done.25.refs_0_.refs_2_, bf16[32,1024]{1,0:T(8,128)(2,1)S(1)} %collective-permute-done.26.refs_1_.refs_3_, f32[32,3584]{1,0:T(8,128)S(1)} %images.22.refs_2_), custom_call_target="tpu_custom_call" | custom-call | flops 5637144576 | bytes 1000000 | tf_op jit(solution)/shard_map/images/pallas_call | solution.py:31
  156.4 2.8 %right_first.1 = (bf16[128,4096]{1,0:T(8,128)(2,1)S(1)}, f32[128,128]{1,0:T(8,128)S(1)}, f32[128,128]{1,0:T(8,128)S(1)}) custom-call(bf16[1,32,4096]{2,1,0:T(8,128)(2,1)S(1)} %pack.1.refs_0_, bf16[1,32,4096]{2,1,0:T(8,128)(2,1)S(1)} %collective-permute-done.29.refs_1_, bf16[2,32,4096]{2,1,0:T(8,128)(2,1)S(1)} %collective-permute-done.30.refs_2_), custom_call_target="tpu_custom_call" | custom-call | flops 100000000 | bytes 1000000 | tf_op jit(solution)/shard_map/right_first/pallas_call | solution.py:31
  159.2 2.6 %right_begin.1 = (f32[128,128]{1,0:T(8,128)S(1)}, f32[128,128]{1,0:T(8,128)S(1)}) custom-call(f32[128,128]{1,0:T(8,128)S(1)} %get-tuple-element.30.gram_ref), custom_call_target="tpu_custom_call" | custom-call | flops 100000000 | bytes 1000000 | tf_op jit(solution)/shard_map/right_begin/pallas_call | solution.py:31
  165.4 2.1 %right_end.1.refs_0_.right_ref = f32[128,128]{1,0:T(8,128)S(1)} custom-call(f32[128,128]{1,0:T(8,128)S(1)} %get-tuple-element.30.gram_ref, f32[128,128]{1,0:T(8,128)S(1)} %get-tuple-element.33.refs_3_.upper_ref, f32[128,128]{1,0:T(8,128)S(1)} %get-tuple-element.35.lower_ref, f32[128,128]{1,0:T(8,128)S(1)} %get-tuple-element.36.change_ref.lower_ref, ...), custom_call_target="tpu_custom_call" | custom-call | flops 100000000 | bytes 1000000 | tf_op jit(solution)/shard_map/right_end/pallas_call | solution.py:31
  167.5 3.8 %collective-permute-done.32.other_ref = f32[128,128]{1,0:T(8,128)S(1)} collective-permute-done((f32[128,128]{1,0:T(8,128)S(1)}, f32[128,128]{1,0:T(8,128)S(1)}, u32[]{:S(2)}, u32[]{:S(2)}) %collective-permute-start.32) | collective-permute-done | bytes 65568 | tf_op jit(solution)/shard_map/ppermute | solution.py:424
  171.4 4.3 %collective-permute-done.33.other_ref = f32[128,128]{1,0:T(8,128)S(1)} collective-permute-done((f32[128,128]{1,0:T(8,128)S(1)}, f32[128,128]{1,0:T(8,128)S(1)}, u32[]{:S(2)}, u32[]{:S(2)}) %collective-permute-start.33) | collective-permute-done | bytes 65568 | tf_op jit(solution)/shard_map/ppermute | solution.py:424
  175.7 1.6 collective-permute-start.34
  177.3 2.7 %collective-permute-done.34.other_ref = f32[128,128]{1,0:T(8,128)S(1)} collective-permute-done((f32[128,128]{1,0:T(8,128)S(1)}, f32[128,128]{1,0:T(8,128)S(1)}, u32[]{:S(2)}, u32[]{:S(2)}) %collective-permute-start.34) | collective-permute-done | bytes 65568 | tf_op jit(solution)/shard_map/ppermute | solution.py:424
  180.0 11.9 %finish.1 = bf16[896,4096]{1,0:T(8,128)(2,1)} custom-call(f32[128,128]{1,0:T(8,128)S(1)} %add.3.one_ref, f32[128,128]{1,0:T(8,128)S(1)} %collective-permute-done.34.other_ref, bf16[128,896]{1,0:T(8,128)(2,1)S(1)} %get-tuple-element.37.panel_ref, bf16[128,4096]{1,0:T(8,128)(2,1)S(1)} %get-tuple-element.38.wide_ref, ...), custom_call_target="tpu_custom_call" | custom-call | tf_op jit(solution)/shard_map/finish/pallas_call | solution.py:404
  (58 shorter events, 23.1 us)
Async XLA Ops:
  0.0 9.4 %copy-start = (bf16[1,3584,4096]{2,1,0:T(8,128)(2,1)S(1)}, bf16[1,3584,4096]{2,1,0:T(8,128)(2,1)}, u32[]{:S(2)}) copy-start(bf16[1,3584,4096]{2,1,0:T(8,128)(2,1)} %param.2) | copy-start | bytes 88080384
  9.4 1.0 copy-start.1
  20.4 8.3 %collective-permute-start = (bf16[32,1152]{1,0:T(8,128)(2,1)S(1)}, bf16[32,1152]{1,0:T(8,128)(2,1)S(1)}, u32[]{:S(2)}, u32[]{:S(2)}) collective-permute-start(bf16[32,1152]{1,0:T(8,128)(2,1)S(1)} %backs.16.refs_0_), channel_id=1, source_target_pairs={{0,6},{1,7},{2,4},{3,5},{4,2},{5,3},{6,0},{7,1},{8,14},{9,15},{10,... | collective-permute-start | bytes 221192 | tf_op jit(solution)/shard_map/ppermute | solution.py:424
  28.1 4.7 %collective-permute-start.1 = (bf16[32,1152]{1,0:T(8,128)(2,1)S(1)}, bf16[32,1152]{1,0:T(8,128)(2,1)S(1)}, u32[]{:S(2)}, u32[]{:S(2)}) collective-permute-start(bf16[32,1152]{1,0:T(8,128)(2,1)S(1)} %backs.18.refs_0_), channel_id=1, source_target_pairs={{0,2},{1,3},{2,0},{3,1},{4,6},{5,7},{6,4},{7,5},{8,10},{9,11},{10,... | collective-permute-start | bytes 221192 | tf_op jit(solution)/shard_map/ppermute | solution.py:424
  28.1 5.8 %collective-permute-start.2 = (bf16[32,1152]{1,0:T(8,128)(2,1)S(1)}, bf16[32,1152]{1,0:T(8,128)(2,1)S(1)}, u32[]{:S(2)}, u32[]{:S(2)}) collective-permute-start(bf16[32,1152]{1,0:T(8,128)(2,1)S(1)} %backs.17.refs_0_), channel_id=1, source_target_pairs={{0,4},{1,5},{2,6},{3,7},{4,0},{5,1},{6,2},{7,3},{8,12},{9,13},{10,... | collective-permute-start | bytes 221192 | tf_op jit(solution)/shard_map/ppermute | solution.py:424
  34.1 4.4 %collective-permute-start.3 = (bf16[32,1152]{1,0:T(8,128)(2,1)S(1)}, bf16[32,1152]{1,0:T(8,128)(2,1)S(1)}, u32[]{:S(2)}, u32[]{:S(2)}) collective-permute-start(bf16[32,1152]{1,0:T(8,128)(2,1)S(1)} %combine.4.one_ref), channel_id=1, source_target_pairs={{0,1},{1,0},{2,3},{3,2},{4,5},{5,4},{6,7},{7,6},{8,9},{9,8},{10,11... | collective-permute-start | bytes 221192 | tf_op jit(solution)/shard_map/ppermute | solution.py:424
  39.5 6.2 %collective-permute-start.6 = (bf16[32,1024]{1,0:T(8,128)(2,1)S(1)}, bf16[32,1024]{1,0:T(8,128)(2,1)S(1)}, u32[]{:S(2)}, u32[]{:S(2)}) collective-permute-start(bf16[32,1024]{1,0:T(8,128)(2,1)S(1)} %settle.4.refs_0_), channel_id=1, source_target_pairs={{0,2},{1,3},{2,0},{3,1},{4,6},{5,7},{6,4},{7,5},{8,10},{9,11},{10,... | collective-permute-start | bytes 196616 | tf_op jit(solution)/shard_map/ppermute | solution.py:424
  41.0 7.3 %collective-permute-start.5 = (bf16[32,1024]{1,0:T(8,128)(2,1)S(1)}, bf16[32,1024]{1,0:T(8,128)(2,1)S(1)}, u32[]{:S(2)}, u32[]{:S(2)}) collective-permute-start(bf16[32,1024]{1,0:T(8,128)(2,1)S(1)} %settle.4.refs_0_), channel_id=1, source_target_pairs={{0,6},{1,7},{2,4},{3,5},{4,2},{5,3},{6,0},{7,1},{8,14},{9,15},{10,... | collective-permute-start | bytes 196616 | tf_op jit(solution)/shard_map/ppermute | solution.py:424
  41.7 6.6 %collective-permute-start.4 = (bf16[32,1024]{1,0:T(8,128)(2,1)S(1)}, bf16[32,1024]{1,0:T(8,128)(2,1)S(1)}, u32[]{:S(2)}, u32[]{:S(2)}) collective-permute-start(bf16[32,1024]{1,0:T(8,128)(2,1)S(1)} %settle.4.refs_0_), channel_id=1, source_target_pairs={{0,4},{1,5},{2,6},{3,7},{4,0},{5,1},{6,2},{7,3},{8,12},{9,13},{10,... | collective-permute-start | bytes 196616 | tf_op jit(solution)/shard_map/ppermute | solution.py:424
  55.9 6.3 %collective-permute-start.7 = (bf16[32,1152]{1,0:T(8,128)(2,1)S(1)}, bf16[32,1152]{1,0:T(8,128)(2,1)S(1)}, u32[]{:S(2)}, u32[]{:S(2)}) collective-permute-start(bf16[32,1152]{1,0:T(8,128)(2,1)S(1)} %backs.20.refs_0_), channel_id=1, source_target_pairs={{0,6},{1,7},{2,4},{3,5},{4,2},{5,3},{6,0},{7,1},{8,14},{9,15},{10,... | collective-permute-start | bytes 221192 | tf_op jit(solution)/shard_map/ppermute | solution.py:424
  59.1 4.4 %collective-permute-start.8 = (bf16[32,1152]{1,0:T(8,128)(2,1)S(1)}, bf16[32,1152]{1,0:T(8,128)(2,1)S(1)}, u32[]{:S(2)}, u32[]{:S(2)}) collective-permute-start(bf16[32,1152]{1,0:T(8,128)(2,1)S(1)} %backs.22.refs_0_), channel_id=1, source_target_pairs={{0,2},{1,3},{2,0},{3,1},{4,6},{5,7},{6,4},{7,5},{8,10},{9,11},{10,... | collective-permute-start | bytes 221192 | tf_op jit(solution)/shard_map/ppermute | solution.py:424
  59.6 5.3 %collective-permute-start.9 = (bf16[32,1152]{1,0:T(8,128)(2,1)S(1)}, bf16[32,1152]{1,0:T(8,128)(2,1)S(1)}, u32[]{:S(2)}, u32[]{:S(2)}) collective-permute-start(bf16[32,1152]{1,0:T(8,128)(2,1)S(1)} %backs.21.refs_0_), channel_id=1, source_target_pairs={{0,4},{1,5},{2,6},{3,7},{4,0},{5,1},{6,2},{7,3},{8,12},{9,13},{10,... | collective-permute-start | bytes 221192 | tf_op jit(solution)/shard_map/ppermute | solution.py:424
  65.1 4.4 %collective-permute-start.10 = (bf16[32,1152]{1,0:T(8,128)(2,1)S(1)}, bf16[32,1152]{1,0:T(8,128)(2,1)S(1)}, u32[]{:S(2)}, u32[]{:S(2)}) collective-permute-start(bf16[32,1152]{1,0:T(8,128)(2,1)S(1)} %combine.5.one_ref), channel_id=1, source_target_pairs={{0,1},{1,0},{2,3},{3,2},{4,5},{5,4},{6,7},{7,6},{8,9},{9,8},{10,11... | collective-permute-start | bytes 221192 | tf_op jit(solution)/shard_map/ppermute | solution.py:424
  70.4 7.0 %collective-permute-start.13 = (bf16[32,1024]{1,0:T(8,128)(2,1)S(1)}, bf16[32,1024]{1,0:T(8,128)(2,1)S(1)}, u32[]{:S(2)}, u32[]{:S(2)}) collective-permute-start(bf16[32,1024]{1,0:T(8,128)(2,1)S(1)} %settle.5.refs_0_), channel_id=1, source_target_pairs={{0,2},{1,3},{2,0},{3,1},{4,6},{5,7},{6,4},{7,5},{8,10},{9,11},{10,... | collective-permute-start | bytes 196616 | tf_op jit(solution)/shard_map/ppermute | solution.py:424
  72.0 8.0 %collective-permute-start.12 = (bf16[32,1024]{1,0:T(8,128)(2,1)S(1)}, bf16[32,1024]{1,0:T(8,128)(2,1)S(1)}, u32[]{:S(2)}, u32[]{:S(2)}) collective-permute-start(bf16[32,1024]{1,0:T(8,128)(2,1)S(1)} %settle.5.refs_0_), channel_id=1, source_target_pairs={{0,6},{1,7},{2,4},{3,5},{4,2},{5,3},{6,0},{7,1},{8,14},{9,15},{10,... | collective-permute-start | bytes 196616 | tf_op jit(solution)/shard_map/ppermute | solution.py:424
  74.3 5.9 %collective-permute-start.11 = (bf16[32,1024]{1,0:T(8,128)(2,1)S(1)}, bf16[32,1024]{1,0:T(8,128)(2,1)S(1)}, u32[]{:S(2)}, u32[]{:S(2)}) collective-permute-start(bf16[32,1024]{1,0:T(8,128)(2,1)S(1)} %settle.5.refs_0_), channel_id=1, source_target_pairs={{0,4},{1,5},{2,6},{3,7},{4,0},{5,1},{6,2},{7,3},{8,12},{9,13},{10,... | collective-permute-start | bytes 196616 | tf_op jit(solution)/shard_map/ppermute | solution.py:424
  87.7 6.2 %collective-permute-start.14 = (bf16[32,1152]{1,0:T(8,128)(2,1)S(1)}, bf16[32,1152]{1,0:T(8,128)(2,1)S(1)}, u32[]{:S(2)}, u32[]{:S(2)}) collective-permute-start(bf16[32,1152]{1,0:T(8,128)(2,1)S(1)} %backs.24.refs_0_), channel_id=1, source_target_pairs={{0,6},{1,7},{2,4},{3,5},{4,2},{5,3},{6,0},{7,1},{8,14},{9,15},{10,... | collective-permute-start | bytes 221192 | tf_op jit(solution)/shard_map/ppermute | solution.py:424
  91.9 4.4 %collective-permute-start.15 = (bf16[32,1152]{1,0:T(8,128)(2,1)S(1)}, bf16[32,1152]{1,0:T(8,128)(2,1)S(1)}, u32[]{:S(2)}, u32[]{:S(2)}) collective-permute-start(bf16[32,1152]{1,0:T(8,128)(2,1)S(1)} %backs.26.refs_0_), channel_id=1, source_target_pairs={{0,2},{1,3},{2,0},{3,1},{4,6},{5,7},{6,4},{7,5},{8,10},{9,11},{10,... | collective-permute-start | bytes 221192 | tf_op jit(solution)/shard_map/ppermute | solution.py:424
  92.0 5.3 %collective-permute-start.16 = (bf16[32,1152]{1,0:T(8,128)(2,1)S(1)}, bf16[32,1152]{1,0:T(8,128)(2,1)S(1)}, u32[]{:S(2)}, u32[]{:S(2)}) collective-permute-start(bf16[32,1152]{1,0:T(8,128)(2,1)S(1)} %backs.25.refs_0_), channel_id=1, source_target_pairs={{0,4},{1,5},{2,6},{3,7},{4,0},{5,1},{6,2},{7,3},{8,12},{9,13},{10,... | collective-permute-start | bytes 221192 | tf_op jit(solution)/shard_map/ppermute | solution.py:424
  97.4 4.4 %collective-permute-start.17 = (bf16[32,1152]{1,0:T(8,128)(2,1)S(1)}, bf16[32,1152]{1,0:T(8,128)(2,1)S(1)}, u32[]{:S(2)}, u32[]{:S(2)}) collective-permute-start(bf16[32,1152]{1,0:T(8,128)(2,1)S(1)} %combine.6.one_ref), channel_id=1, source_target_pairs={{0,1},{1,0},{2,3},{3,2},{4,5},{5,4},{6,7},{7,6},{8,9},{9,8},{10,11... | collective-permute-start | bytes 221192 | tf_op jit(solution)/shard_map/ppermute | solution.py:424
  102.8 6.9 %collective-permute-start.20 = (bf16[32,1024]{1,0:T(8,128)(2,1)S(1)}, bf16[32,1024]{1,0:T(8,128)(2,1)S(1)}, u32[]{:S(2)}, u32[]{:S(2)}) collective-permute-start(bf16[32,1024]{1,0:T(8,128)(2,1)S(1)} %settle.6.refs_0_), channel_id=1, source_target_pairs={{0,2},{1,3},{2,0},{3,1},{4,6},{5,7},{6,4},{7,5},{8,10},{9,11},{10,... | collective-permute-start | bytes 196616 | tf_op jit(solution)/shard_map/ppermute | solution.py:424
  105.6 6.8 %collective-permute-start.19 = (bf16[32,1024]{1,0:T(8,128)(2,1)S(1)}, bf16[32,1024]{1,0:T(8,128)(2,1)S(1)}, u32[]{:S(2)}, u32[]{:S(2)}) collective-permute-start(bf16[32,1024]{1,0:T(8,128)(2,1)S(1)} %settle.6.refs_0_), channel_id=1, source_target_pairs={{0,6},{1,7},{2,4},{3,5},{4,2},{5,3},{6,0},{7,1},{8,14},{9,15},{10,... | collective-permute-start | bytes 196616 | tf_op jit(solution)/shard_map/ppermute | solution.py:424
  105.8 6.6 %collective-permute-start.18 = (bf16[32,1024]{1,0:T(8,128)(2,1)S(1)}, bf16[32,1024]{1,0:T(8,128)(2,1)S(1)}, u32[]{:S(2)}, u32[]{:S(2)}) collective-permute-start(bf16[32,1024]{1,0:T(8,128)(2,1)S(1)} %settle.6.refs_0_), channel_id=1, source_target_pairs={{0,4},{1,5},{2,6},{3,7},{4,0},{5,1},{6,2},{7,3},{8,12},{9,13},{10,... | collective-permute-start | bytes 196616 | tf_op jit(solution)/shard_map/ppermute | solution.py:424
  120.1 6.2 %collective-permute-start.21 = (bf16[32,1152]{1,0:T(8,128)(2,1)S(1)}, bf16[32,1152]{1,0:T(8,128)(2,1)S(1)}, u32[]{:S(2)}, u32[]{:S(2)}) collective-permute-start(bf16[32,1152]{1,0:T(8,128)(2,1)S(1)} %backs.28.refs_0_), channel_id=1, source_target_pairs={{0,6},{1,7},{2,4},{3,5},{4,2},{5,3},{6,0},{7,1},{8,14},{9,15},{10,... | collective-permute-start | bytes 221192 | tf_op jit(solution)/shard_map/ppermute | solution.py:424
  123.8 5.2 %collective-permute-start.22 = (bf16[32,1152]{1,0:T(8,128)(2,1)S(1)}, bf16[32,1152]{1,0:T(8,128)(2,1)S(1)}, u32[]{:S(2)}, u32[]{:S(2)}) collective-permute-start(bf16[32,1152]{1,0:T(8,128)(2,1)S(1)} %backs.30.refs_0_), channel_id=1, source_target_pairs={{0,2},{1,3},{2,0},{3,1},{4,6},{5,7},{6,4},{7,5},{8,10},{9,11},{10,... | collective-permute-start | bytes 221192 | tf_op jit(solution)/shard_map/ppermute | solution.py:424
  124.4 7.4 %collective-permute-start.23 = (bf16[32,1152]{1,0:T(8,128)(2,1)S(1)}, bf16[32,1152]{1,0:T(8,128)(2,1)S(1)}, u32[]{:S(2)}, u32[]{:S(2)}) collective-permute-start(bf16[32,1152]{1,0:T(8,128)(2,1)S(1)} %backs.29.refs_0_), channel_id=1, source_target_pairs={{0,4},{1,5},{2,6},{3,7},{4,0},{5,1},{6,2},{7,3},{8,12},{9,13},{10,... | collective-permute-start | bytes 221192 | tf_op jit(solution)/shard_map/ppermute | solution.py:424
  131.9 4.4 %collective-permute-start.24 = (bf16[32,1152]{1,0:T(8,128)(2,1)S(1)}, bf16[32,1152]{1,0:T(8,128)(2,1)S(1)}, u32[]{:S(2)}, u32[]{:S(2)}) collective-permute-start(bf16[32,1152]{1,0:T(8,128)(2,1)S(1)} %combine.7.one_ref), channel_id=1, source_target_pairs={{0,1},{1,0},{2,3},{3,2},{4,5},{5,4},{6,7},{7,6},{8,9},{9,8},{10,11... | collective-permute-start | bytes 221192 | tf_op jit(solution)/shard_map/ppermute | solution.py:424
  137.3 6.2 %collective-permute-start.27 = (bf16[32,1024]{1,0:T(8,128)(2,1)S(1)}, bf16[32,1024]{1,0:T(8,128)(2,1)S(1)}, u32[]{:S(2)}, u32[]{:S(2)}) collective-permute-start(bf16[32,1024]{1,0:T(8,128)(2,1)S(1)} %settle.7.refs_0_), channel_id=1, source_target_pairs={{0,2},{1,3},{2,0},{3,1},{4,6},{5,7},{6,4},{7,5},{8,10},{9,11},{10,... | collective-permute-start | bytes 196616 | tf_op jit(solution)/shard_map/ppermute | solution.py:424
  137.3 6.2 %collective-permute-start.26 = (bf16[32,1024]{1,0:T(8,128)(2,1)S(1)}, bf16[32,1024]{1,0:T(8,128)(2,1)S(1)}, u32[]{:S(2)}, u32[]{:S(2)}) collective-permute-start(bf16[32,1024]{1,0:T(8,128)(2,1)S(1)} %settle.7.refs_0_), channel_id=1, source_target_pairs={{0,6},{1,7},{2,4},{3,5},{4,2},{5,3},{6,0},{7,1},{8,14},{9,15},{10,... | collective-permute-start | bytes 196616 | tf_op jit(solution)/shard_map/ppermute | solution.py:424
  139.7 5.9 %collective-permute-start.25 = (bf16[32,1024]{1,0:T(8,128)(2,1)S(1)}, bf16[32,1024]{1,0:T(8,128)(2,1)S(1)}, u32[]{:S(2)}, u32[]{:S(2)}) collective-permute-start(bf16[32,1024]{1,0:T(8,128)(2,1)S(1)} %settle.7.refs_0_), channel_id=1, source_target_pairs={{0,4},{1,5},{2,6},{3,7},{4,0},{5,1},{6,2},{7,3},{8,12},{9,13},{10,... | collective-permute-start | bytes 196616 | tf_op jit(solution)/shard_map/ppermute | solution.py:424
  145.6 8.8 %collective-permute-start.29 = (bf16[1,32,4096]{2,1,0:T(8,128)(2,1)S(1)}, bf16[1,32,4096]{2,1,0:T(8,128)(2,1)S(1)}, u32[]{:S(2)}, u32[]{:S(2)}) collective-permute-start(bf16[1,32,4096]{2,1,0:T(8,128)(2,1)S(1)} %pack.1.refs_0_), channel_id=1, source_target_pairs={{0,16},{8,24},{16,0},{24,8},{1,17},{9,25},{17,1},{25,9},{2,18},{10... | collective-permute-start | bytes 786440 | tf_op jit(solution)/shard_map/ppermute | solution.py:424
  154.4 2.0 %collective-permute-start.30 = (bf16[2,32,4096]{2,1,0:T(8,128)(2,1)S(1)}, bf16[2,32,4096]{2,1,0:T(8,128)(2,1)S(1)}, u32[]{:S(2)}, u32[]{:S(2)}) collective-permute-start(bf16[2,32,4096]{2,1,0:T(8,128)(2,1)S(1)} %join.2), channel_id=1, source_target_pairs={{0,8},{8,0},{16,24},{24,16},{1,9},{9,1},{17,25},{25,17},{2,10},{10... | collective-permute-start | bytes 1572872 | tf_op jit(solution)/shard_map/ppermute | solution.py:424
  154.5 8.0 %collective-permute-start.28 = (bf16[1,4,32,896]{3,2,1,0:T(8,128)(2,1)S(1)}, bf16[1,4,32,896]{3,2,1,0:T(8,128)(2,1)S(1)}, u32[]{:S(2)}, u32[]{:S(2)}) collective-permute-start(bf16[1,4,32,896]{3,2,1,0:T(8,128)(2,1)S(1)} %bitcast.43), channel_id=1, source_target_pairs={{0,16},{8,24},{16,0},{24,8},{1,17},{9,25},{17,1},{25,9},{2,18},{10... | collective-permute-start | bytes 688136 | tf_op jit(solution)/shard_map/ppermute | solution.py:424
  162.5 1.9 collective-permute-start.31
  164.9 6.4 %collective-permute-start.32 = (f32[128,128]{1,0:T(8,128)S(1)}, f32[128,128]{1,0:T(8,128)S(1)}, u32[]{:S(2)}, u32[]{:S(2)}) collective-permute-start(f32[128,128]{1,0:T(8,128)S(1)} %get-tuple-element.34.refs_0_.one_ref), channel_id=1, source_target_pairs={{0,4},{1,5},{2,6},{3,7},{4,0},{5,1},{6,2},{7,3},{8,12},{9,13},{10,... | collective-permute-start | bytes 196616 | tf_op jit(solution)/shard_map/ppermute | solution.py:424
  171.3 4.3 %collective-permute-start.33 = (f32[128,128]{1,0:T(8,128)S(1)}, f32[128,128]{1,0:T(8,128)S(1)}, u32[]{:S(2)}, u32[]{:S(2)}) collective-permute-start(f32[128,128]{1,0:T(8,128)S(1)} %add.2.one_ref), channel_id=1, source_target_pairs={{0,2},{1,3},{2,0},{3,1},{4,6},{5,7},{6,4},{7,5},{8,10},{9,11},{10,... | collective-permute-start | bytes 196616 | tf_op jit(solution)/shard_map/ppermute | solution.py:424
  175.7 4.3 %collective-permute-start.34 = (f32[128,128]{1,0:T(8,128)S(1)}, f32[128,128]{1,0:T(8,128)S(1)}, u32[]{:S(2)}, u32[]{:S(2)}) collective-permute-start(f32[128,128]{1,0:T(8,128)S(1)} %add.3.one_ref), channel_id=1, source_target_pairs={{0,1},{1,0},{2,3},{3,2},{4,5},{5,4},{6,7},{7,6},{8,9},{9,8},{10,11... | collective-permute-start | bytes 196616 | tf_op jit(solution)/shard_map/ppermute | solution.py:424
where the time goes:
time: 192 us
  Pallas kernels  95.8 us (50%)
  starting transfers between devices  45.4 us (24%)
  waiting for transfers between devices  40.1 us (21%)
  local copies, waits for them, and re-layouts  10.4 us (5%)
    pallas_call x47, Pallas kernels, call(): pl.pallas_call(kernel, out_shape=tuple(shapes), in_specs=specs, out_specs...  83.9 us
    ppermute x35, starting transfers between devices, send(): return lax.ppermute(piece, axis, [(at, at ^ mask) for at in range(count)])  45.4 us
    ppermute x35, waiting for transfers between devices, send(): return lax.ppermute(piece, axis, [(at, at ^ mask) for at in range(count)])  40.1 us
    pallas_call x1, Pallas kernels, finish(): pl.pallas_call(finish_kernel, out_shape=shape_of((rows, cols), BF16), gri...  11.9 us
    unnamed x4, local copies, waits for them, and re-layouts  10.4 us
  transfers between devices with their start and end apart: 35, of which 23 were waited for; matrix products, arithmetic and copies ran while one was open for 0% of the time, Pallas kernels for 24%

commit v1 on v0

--- a/solution.py
+++ b/solution.py
@@ -366,55 +366,47 @@
     refs[-1][...] = square(root_end(state, gram_ref[...]).T, change_ref[...])
 
 
-def finish_kernel(one_ref, other_ref, panel_ref, wide_ref, lower_ref, right_ref, out_ref, side):
-    size = lower_ref.shape[0]
-
-    @pl.when(pl.program_id(0) == 0)
-    def _():
-        lower = lower_ref[...]
-        gram = square(square(lower, one_ref[...] + other_ref[...]), lower.T)
-        diagonal = jnp.where(eye_of(size), gram, 0.0)
-        down = jnp.sqrt(jnp.sum(diagonal, axis=1, keepdims=True))
-        across = jnp.sqrt(jnp.sum(diagonal, axis=0, keepdims=True))
-        normed = gram / (down * across)
-        mixing = root_end(root_steps(root_begin(normed), ROOT_STEPS), normed) / down * across
-        mixed = square(square(lower.T, mixing), right_ref[...])
-        panel = panel_ref[...].T
-        product = jnp.dot(
-            jnp.concatenate([panel, panel], axis=1),
-            jnp.concatenate(split_two(mixed), axis=0),
-            preferred_element_type=F32,
-        )
-        side[...] = jnp.concatenate(split_two(product), axis=1)
-
-    wide = wide_ref[...]
-    out_ref[...] = jnp.dot(
-        side[...], jnp.concatenate([wide, wide], axis=0), preferred_element_type=F32
-    ).astype(BF16)
+def finish_kernel(across, one_ref, other_ref, panel_ref, wide_ref, lower_ref, right_ref, out_ref, made, sems):
+    size, cols = wide_ref.shape
+    lower = lower_ref[...]
+    gram = square(square(lower, one_ref[...] + other_ref[...]), lower.T)
+    diagonal = jnp.where(eye_of(size), gram, 0.0)
+    down = jnp.sqrt(jnp.sum(diagonal, axis=1, keepdims=True))
+    over = jnp.sqrt(jnp.sum(diagonal, axis=0, keepdims=True))
+    normed = gram / (down * over)
+    mixing = root_end(root_steps(root_begin(normed), ROOT_STEPS), normed) / down * over
+    mixed = square(square(lower.T, mixing), right_ref[...])
+    panel = panel_ref[...].T
+    product = jnp.dot(
+        jnp.concatenate([panel, panel], axis=1),
+        jnp.concatenate(split_two(mixed), axis=0),
+        preferred_element_type=F32,
+    )
+    side = jnp.concatenate(split_two(product), axis=1)
+    copies = []
+    for at in range(cols // across):
+        span = slice(at * across, (at + 1) * across)
+        wide = wide_ref[:, span]
+        made[at] = jnp.dot(side, jnp.concatenate([wide, wide], axis=0), preferred_element_type=F32).astype(BF16)
+        copies.append(pltpu.make_async_copy(made.at[at], out_ref.at[:, span], sems.at[at]))
+        copies[-1].start()
+    for copy in copies:
+        copy.wait()
 
 
 def finish(one, other, panel, wide, lower, right_side):
     size, rows = panel.shape
     cols = wide.shape[1]
     across = 512
-
-    def whole(array):
-        return pl.BlockSpec(array.shape, lambda at: (0, 0))
-
     return pl.pallas_call(
-        finish_kernel,
+        functools.partial(finish_kernel, across),
         out_shape=shape_of((rows, cols), BF16),
-        grid=(cols // across,),
-        in_specs=[
-            whole(one),
-            whole(other),
-            whole(panel),
-            pl.BlockSpec((size, across), lambda at: (0, at)),
-            whole(lower),
-            whole(right_side),
+        in_specs=[IN_VMEM] * 6,
+        out_specs=ANYWHERE,
+        scratch_shapes=[
+            pltpu.VMEM((cols // across, rows, across), BF16),
+            pltpu.SemaphoreType.DMA((cols // across,)),
         ],
-        out_specs=pl.BlockSpec((rows, across), lambda at: (0, at)),
-        scratch_shapes=[pltpu.VMEM((rows, 2 * size), BF16)],
         compiler_params=pltpu.CompilerParams(vmem_limit_bytes=VMEM_BYTES),
         name="finish",
     )(one, other, panel, wide, lower, right_side)
@@ -457,8 +449,7 @@
         block = settle(held, sums, send(sums, "row", 1, parts))
         blocks = {mask: send(block, "row", mask, parts) for mask in order[:-1]}
         blocks[0] = block
-        (partial,) = images(held, [block], (0,))
-        (partial,) = images(held, [blocks[nearest]], (nearest,), partial)
+        (partial,) = images(held, [block, blocks[nearest]], (0, nearest))
         rest = [blocks[mask] for mask in farther]
         if last:
             (own,) = call(

time: 192 us -> 190 us (0.990)
  Pallas kernels: 95.8 us -> 90.8 us
  waiting for transfers between devices: 40.1 us -> 43.2 us
    ppermute x35, waiting for transfers between devices: 40.1 us -> 43.2 us  [send(): return lax.ppermute(piece, axis, [(at, at ^ mask) for at in range(count)])]
    pallas_call x47 -> x43, Pallas kernels: 83.9 us -> 81.4 us  [call(): pl.pallas_call(kernel, out_shape=tuple(shapes), in_specs=specs, out_specs...]
    pallas_call x1, Pallas kernels: 11.9 us -> 9.4 us  [finish(): pl.pallas_call(functools.partial(finish_kernel, across), out_shape=shape_...]
  transfers between devices with their start and end apart: 35 -> 35, of which waited for: 23 -> 27; matrix products, arithmetic and copies ran while one was open for 0% -> 0% of each run, Pallas kernels for 24% -> 23%
where the time goes in v1:
time: 190 us; the launch traced here: 189 us
  Pallas kernels  90.8 us (48%)
  starting transfers between devices  44.7 us (24%)
  waiting for transfers between devices  43.2 us (23%)
  local copies, waits for them, and re-layouts  10.4 us (5%)
    pallas_call x43, Pallas kernels, call(): pl.pallas_call(kernel, out_shape=tuple(shapes), in_specs=specs, out_specs...  81.4 us
    ppermute x35, starting transfers between devices, send(): return lax.ppermute(piece, axis, [(at, at ^ mask) for at in range(count)])  44.7 us
    ppermute x35, waiting for transfers between devices, send(): return lax.ppermute(piece, axis, [(at, at ^ mask) for at in range(count)])  43.2 us
    unnamed x4, local copies, waits for them, and re-layouts  10.4 us
    pallas_call x1, Pallas kernels, finish(): pl.pallas_call(functools.partial(finish_kernel, across), out_shape=shape_...  9.4 us
  transfers between devices with their start and end apart: 35, of which 27 were waited for; matrix products, arithmetic and copies ran while one was open for 0% of the time, Pallas kernels for 23%

profile of v1, /device:TPU:0, one launch (start us, length us, event | category | flops | bytes accessed | tf_op | source)
XLA Modules:
  0.0 189.5 jit_solution(8117179275975422204)
XLA Ops:
  0.0 9.3 %copy-done = bf16[1,3584,4096]{2,1,0:T(8,128)(2,1)S(1)} copy-done((bf16[1,3584,4096]{2,1,0:T(8,128)(2,1)S(1)}, bf16[1,3584,4096]{2,1,0:T(8,128)(2,1)}, u32[]{:S(2)}) %copy-start) | copy-done | bytes 29360152
  10.4 8.6 %first.1 = (bf16[32,3584]{1,0:T(8,128)(2,1)S(1)}, bf16[32,128]{1,0:T(8,128)(2,1)S(1)}) custom-call(bf16[3584,4096]{1,0:T(8,128)(2,1)S(1)} %bitcast.5, f32[32,4096]{1,0:T(8,128)S(1)} %bitcast.42), custom_call_target="tpu_custom_call" | custom-call | flops 11274289152 | bytes 1000000 | tf_op jit(solution)/shard_map/first/pallas_call | solution.py:31
  19.0 1.4 backs.16.refs_0_
  20.4 5.0 %collective-permute-start = (bf16[32,1152]{1,0:T(8,128)(2,1)S(1)}, bf16[32,1152]{1,0:T(8,128)(2,1)S(1)}, u32[]{:S(2)}, u32[]{:S(2)}) collective-permute-start(bf16[32,1152]{1,0:T(8,128)(2,1)S(1)} %backs.16.refs_0_), channel_id=1, source_target_pairs={{0,6},{1,7},{2,4},{3,5},{4,2},{5,3},{6,0},{7,1},{8,14},{9,15},{10,... | collective-permute-start | bytes 221192 | tf_op jit(solution)/shard_map/ppermute | solution.py:416
  25.4 1.3 backs.17.refs_0_
  26.8 1.4 backs.18.refs_0_
  28.7 1.3 backs.19.refs_0_
  30.1 2.8 %collective-permute-done.1.refs_1_ = bf16[32,1152]{1,0:T(8,128)(2,1)S(1)} collective-permute-done((bf16[32,1152]{1,0:T(8,128)(2,1)S(1)}, bf16[32,1152]{1,0:T(8,128)(2,1)S(1)}, u32[]{:S(2)}, u32[]{:S(2)}) %collective-permute-start.1) | collective-permute-done | bytes 73760 | tf_op jit(solution)/shard_map/ppermute | solution.py:416
  32.9 1.1 collective-permute-done.2.refs_2_
  34.1 1.6 collective-permute-start.3
  35.7 2.8 %collective-permute-done.3.other_ref = bf16[32,1152]{1,0:T(8,128)(2,1)S(1)} collective-permute-done((bf16[32,1152]{1,0:T(8,128)(2,1)S(1)}, bf16[32,1152]{1,0:T(8,128)(2,1)S(1)}, u32[]{:S(2)}, u32[]{:S(2)}) %collective-permute-start.3) | collective-permute-done | bytes 73760 | tf_op jit(solution)/shard_map/ppermute | solution.py:416
  39.5 1.5 collective-permute-start.6
  41.7 1.3 collective-permute-start.4
  43.0 1.4 collective-permute-done.6.refs_1_
  44.4 4.6 %images.8.refs_2_ = f32[32,3584]{1,0:T(8,128)S(1)} custom-call(bf16[3584,4096]{1,0:T(8,128)(2,1)S(1)} %bitcast.12, bf16[32,1024]{1,0:T(8,128)(2,1)S(1)} %settle.4.refs_0_, bf16[32,1024]{1,0:T(8,128)(2,1)S(1)} %collective-permute-done.6.refs_1_), custom_call_target="tpu_custom_call" | custom-call | flops 5637144576 | bytes 1000000 | tf_op jit(solution)/shard_map/images/pallas_call | solution.py:31
  49.0 5.0 %images.9 = (bf16[32,3584]{1,0:T(8,128)(2,1)S(1)}, bf16[32,128]{1,0:T(8,128)(2,1)S(1)}) custom-call(bf16[3584,4096]{1,0:T(8,128)(2,1)S(1)} %bitcast.13, bf16[32,1024]{1,0:T(8,128)(2,1)S(1)} %collective-permute-done.4.refs_0_, bf16[32,1024]{1,0:T(8,128)(2,1)S(1)} %collective-permute-done.5.refs_1_, f32[32,3584]{1,0:T(8,128)S(1)} %images.8.refs_2_), custom_call_target="tpu_custom_call" | custom-call | flops 5637144576 | bytes 1000000 | tf_op jit(solution)/shard_map/images/pallas_call | solution.py:31
  54.0 1.4 backs.20.refs_0_
  55.4 1.4 backs.21.refs_0_
  56.7 1.8 collective-permute-start.7
  58.5 1.3 backs.22.refs_0_
  59.9 2.6 %collective-permute-start.9 = (bf16[32,1152]{1,0:T(8,128)(2,1)S(1)}, bf16[32,1152]{1,0:T(8,128)(2,1)S(1)}, u32[]{:S(2)}, u32[]{:S(2)}) collective-permute-start(bf16[32,1152]{1,0:T(8,128)(2,1)S(1)} %backs.21.refs_0_), channel_id=1, source_target_pairs={{0,4},{1,5},{2,6},{3,7},{4,0},{5,1},{6,2},{7,3},{8,12},{9,13},{10,... | collective-permute-start | bytes 221192 | tf_op jit(solution)/shard_map/ppermute | solution.py:416
  62.9 1.3 backs.23.refs_0_
  65.4 1.6 collective-permute-start.10
  66.9 2.8 %collective-permute-done.10.other_ref = bf16[32,1152]{1,0:T(8,128)(2,1)S(1)} collective-permute-done((bf16[32,1152]{1,0:T(8,128)(2,1)S(1)}, bf16[32,1152]{1,0:T(8,128)(2,1)S(1)}, u32[]{:S(2)}, u32[]{:S(2)}) %collective-permute-start.10) | collective-permute-done | bytes 73760 | tf_op jit(solution)/shard_map/ppermute | solution.py:416
  70.7 2.0 %collective-permute-start.13 = (bf16[32,1024]{1,0:T(8,128)(2,1)S(1)}, bf16[32,1024]{1,0:T(8,128)(2,1)S(1)}, u32[]{:S(2)}, u32[]{:S(2)}) collective-permute-start(bf16[32,1024]{1,0:T(8,128)(2,1)S(1)} %settle.5.refs_0_), channel_id=1, source_target_pairs={{0,2},{1,3},{2,0},{3,1},{4,6},{5,7},{6,4},{7,5},{8,10},{9,11},{10,... | collective-permute-start | bytes 196616 | tf_op jit(solution)/shard_map/ppermute | solution.py:416
  72.8 2.0 %collective-permute-start.12 = (bf16[32,1024]{1,0:T(8,128)(2,1)S(1)}, bf16[32,1024]{1,0:T(8,128)(2,1)S(1)}, u32[]{:S(2)}, u32[]{:S(2)}) collective-permute-start(bf16[32,1024]{1,0:T(8,128)(2,1)S(1)} %settle.5.refs_0_), channel_id=1, source_target_pairs={{0,6},{1,7},{2,4},{3,5},{4,2},{5,3},{6,0},{7,1},{8,14},{9,15},{10,... | collective-permute-start | bytes 196616 | tf_op jit(solution)/shard_map/ppermute | solution.py:416
  75.1 4.6 %images.10.refs_2_ = f32[32,3584]{1,0:T(8,128)S(1)} custom-call(bf16[3584,4096]{1,0:T(8,128)(2,1)S(1)} %bitcast.20, bf16[32,1024]{1,0:T(8,128)(2,1)S(1)} %settle.5.refs_0_, bf16[32,1024]{1,0:T(8,128)(2,1)S(1)} %collective-permute-done.13.refs_1_), custom_call_target="tpu_custom_call" | custom-call | flops 5637144576 | bytes 1000000 | tf_op jit(solution)/shard_map/images/pallas_call | solution.py:31
  80.2 4.8 %images.11 = (bf16[32,3584]{1,0:T(8,128)(2,1)S(1)}, bf16[32,128]{1,0:T(8,128)(2,1)S(1)}) custom-call(bf16[3584,4096]{1,0:T(8,128)(2,1)S(1)} %bitcast.21, bf16[32,1024]{1,0:T(8,128)(2,1)S(1)} %collective-permute-done.11.refs_0_, bf16[32,1024]{1,0:T(8,128)(2,1)S(1)} %collective-permute-done.12.refs_1_, f32[32,3584]{1,0:T(8,128)S(1)} %images.10.refs_2_), custom_call_target="tpu_custom_call" | custom-call | flops 5637144576 | bytes 1000000 | tf_op jit(solution)/shard_map/images/pallas_call | solution.py:31
  85.1 1.4 backs.24.refs_0_
  86.4 1.4 backs.25.refs_0_
  87.8 2.0 %collective-permute-start.14 = (bf16[32,1152]{1,0:T(8,128)(2,1)S(1)}, bf16[32,1152]{1,0:T(8,128)(2,1)S(1)}, u32[]{:S(2)}, u32[]{:S(2)}) collective-permute-start(bf16[32,1152]{1,0:T(8,128)(2,1)S(1)} %backs.24.refs_0_), channel_id=1, source_target_pairs={{0,6},{1,7},{2,4},{3,5},{4,2},{5,3},{6,0},{7,1},{8,14},{9,15},{10,... | collective-permute-start | bytes 221192 | tf_op jit(solution)/shard_map/ppermute | solution.py:416
  89.8 1.3 backs.26.refs_0_
  91.8 1.7 collective-permute-start.16
  94.0 1.3 backs.27.refs_0_
  95.7 2.6 %collective-permute-done.16.refs_2_ = bf16[32,1152]{1,0:T(8,128)(2,1)S(1)} collective-permute-done((bf16[32,1152]{1,0:T(8,128)(2,1)S(1)}, bf16[32,1152]{1,0:T(8,128)(2,1)S(1)}, u32[]{:S(2)}, u32[]{:S(2)}) %collective-permute-start.16) | collective-permute-done | bytes 73760 | tf_op jit(solution)/shard_map/ppermute | solution.py:416
  98.4 1.5 collective-permute-start.17
  100.0 2.9 %collective-permute-done.17.other_ref = bf16[32,1152]{1,0:T(8,128)(2,1)S(1)} collective-permute-done((bf16[32,1152]{1,0:T(8,128)(2,1)S(1)}, bf16[32,1152]{1,0:T(8,128)(2,1)S(1)}, u32[]{:S(2)}, u32[]{:S(2)}) %collective-permute-start.17) | collective-permute-done | bytes 73760 | tf_op jit(solution)/shard_map/ppermute | solution.py:416
  104.2 2.4 %collective-permute-start.19 = (bf16[32,1024]{1,0:T(8,128)(2,1)S(1)}, bf16[32,1024]{1,0:T(8,128)(2,1)S(1)}, u32[]{:S(2)}, u32[]{:S(2)}) collective-permute-start(bf16[32,1024]{1,0:T(8,128)(2,1)S(1)} %settle.6.refs_0_), channel_id=1, source_target_pairs={{0,6},{1,7},{2,4},{3,5},{4,2},{5,3},{6,0},{7,1},{8,14},{9,15},{10,... | collective-permute-start | bytes 196616 | tf_op jit(solution)/shard_map/ppermute | solution.py:416
  108.1 4.6 %images.12.refs_2_ = f32[32,3584]{1,0:T(8,128)S(1)} custom-call(bf16[3584,4096]{1,0:T(8,128)(2,1)S(1)} %bitcast.28, bf16[32,1024]{1,0:T(8,128)(2,1)S(1)} %settle.6.refs_0_, bf16[32,1024]{1,0:T(8,128)(2,1)S(1)} %collective-permute-done.20.refs_1_), custom_call_target="tpu_custom_call" | custom-call | flops 5637144576 | bytes 1000000 | tf_op jit(solution)/shard_map/images/pallas_call | solution.py:31
  112.7 5.1 %images.13 = (bf16[32,3584]{1,0:T(8,128)(2,1)S(1)}, bf16[32,128]{1,0:T(8,128)(2,1)S(1)}) custom-call(bf16[3584,4096]{1,0:T(8,128)(2,1)S(1)} %bitcast.29, bf16[32,1024]{1,0:T(8,128)(2,1)S(1)} %collective-permute-done.18.refs_0_, bf16[32,1024]{1,0:T(8,128)(2,1)S(1)} %collective-permute-done.19.refs_1_, f32[32,3584]{1,0:T(8,128)S(1)} %images.12.refs_2_), custom_call_target="tpu_custom_call" | custom-call | flops 5637144576 | bytes 1000000 | tf_op jit(solution)/shard_map/images/pallas_call | solution.py:31
  117.8 1.4 backs.28.refs_0_
  119.1 1.4 backs.29.refs_0_
  120.5 1.3 collective-permute-start.21
  121.7 1.3 backs.30.refs_0_
  123.8 2.4 %collective-permute-start.23 = (bf16[32,1152]{1,0:T(8,128)(2,1)S(1)}, bf16[32,1152]{1,0:T(8,128)(2,1)S(1)}, u32[]{:S(2)}, u32[]{:S(2)}) collective-permute-start(bf16[32,1152]{1,0:T(8,128)(2,1)S(1)} %backs.29.refs_0_), channel_id=1, source_target_pairs={{0,4},{1,5},{2,6},{3,7},{4,0},{5,1},{6,2},{7,3},{8,12},{9,13},{10,... | collective-permute-start | bytes 221192 | tf_op jit(solution)/shard_map/ppermute | solution.py:416
  127.2 1.3 backs.31.refs_0_
  129.1 1.3 collective-permute-done.23.refs_2_
  130.6 1.5 collective-permute-start.24
  132.1 2.8 %collective-permute-done.24.other_ref = bf16[32,1152]{1,0:T(8,128)(2,1)S(1)} collective-permute-done((bf16[32,1152]{1,0:T(8,128)(2,1)S(1)}, bf16[32,1152]{1,0:T(8,128)(2,1)S(1)}, u32[]{:S(2)}, u32[]{:S(2)}) %collective-permute-start.24) | collective-permute-done | bytes 73760 | tf_op jit(solution)/shard_map/ppermute | solution.py:416
  136.0 2.6 %collective-permute-start.26 = (bf16[32,1024]{1,0:T(8,128)(2,1)S(1)}, bf16[32,1024]{1,0:T(8,128)(2,1)S(1)}, u32[]{:S(2)}, u32[]{:S(2)}) collective-permute-start(bf16[32,1024]{1,0:T(8,128)(2,1)S(1)} %settle.7.refs_0_), channel_id=1, source_target_pairs={{0,6},{1,7},{2,4},{3,5},{4,2},{5,3},{6,0},{7,1},{8,14},{9,15},{10,... | collective-permute-start | bytes 196616 | tf_op jit(solution)/shard_map/ppermute | solution.py:416
  140.3 2.0 %collective-permute-done.26.refs_1_.refs_3_ = bf16[32,1024]{1,0:T(8,128)(2,1)S(1)} collective-permute-done((bf16[32,1024]{1,0:T(8,128)(2,1)S(1)}, bf16[32,1024]{1,0:T(8,128)(2,1)S(1)}, u32[]{:S(2)}, u32[]{:S(2)}) %collective-permute-start.26) | collective-permute-done | bytes 65568 | tf_op jit(solution)/shard_map/ppermute | solution.py:416
  142.2 1.6 collective-permute-done.25.refs_0_.refs_2_
  143.9 1.5 collective-permute-start.29
  145.4 4.6 %images.14.refs_2_ = f32[32,3584]{1,0:T(8,128)S(1)} custom-call(bf16[3584,4096]{1,0:T(8,128)(2,1)S(1)} %bitcast.37, bf16[32,1024]{1,0:T(8,128)(2,1)S(1)} %settle.7.refs_0_, bf16[32,1024]{1,0:T(8,128)(2,1)S(1)} %collective-permute-done.27.refs_1_), custom_call_target="tpu_custom_call" | custom-call | flops 5637144576 | bytes 1000000 | tf_op jit(solution)/shard_map/images/pallas_call | solution.py:31
  150.0 4.6 %images.15.refs_2_ = bf16[4,32,896]{2,1,0:T(8,128)(2,1)S(1)} custom-call(bf16[3584,4096]{1,0:T(8,128)(2,1)S(1)} %bitcast.38, bf16[32,1024]{1,0:T(8,128)(2,1)S(1)} %collective-permute-done.25.refs_0_.refs_2_, bf16[32,1024]{1,0:T(8,128)(2,1)S(1)} %collective-permute-done.26.refs_1_.refs_3_, f32[32,3584]{1,0:T(8,128)S(1)} %images.14.refs_2_), custom_call_target="tpu_custom_call" | custom-call | flops 5637144576 | bytes 1000000 | tf_op jit(solution)/shard_map/images/pallas_call | solution.py:31
  155.3 1.3 collective-permute-done.30.refs_2_
  156.6 2.8 %right_first.1 = (bf16[128,4096]{1,0:T(8,128)(2,1)S(1)}, f32[128,128]{1,0:T(8,128)S(1)}, f32[128,128]{1,0:T(8,128)S(1)}) custom-call(bf16[1,32,4096]{2,1,0:T(8,128)(2,1)S(1)} %pack.1.refs_0_, bf16[1,32,4096]{2,1,0:T(8,128)(2,1)S(1)} %collective-permute-done.29.refs_1_, bf16[2,32,4096]{2,1,0:T(8,128)(2,1)S(1)} %collective-permute-done.30.refs_2_), custom_call_target="tpu_custom_call" | custom-call | flops 100000000 | bytes 1000000 | tf_op jit(solution)/shard_map/right_first/pallas_call | solution.py:31
  159.5 2.6 %right_begin.1 = (f32[128,128]{1,0:T(8,128)S(1)}, f32[128,128]{1,0:T(8,128)S(1)}) custom-call(f32[128,128]{1,0:T(8,128)S(1)} %get-tuple-element.30.gram_ref), custom_call_target="tpu_custom_call" | custom-call | flops 100000000 | bytes 1000000 | tf_op jit(solution)/shard_map/right_begin/pallas_call | solution.py:31
  166.1 2.1 %right_end.1.refs_0_.right_ref = f32[128,128]{1,0:T(8,128)S(1)} custom-call(f32[128,128]{1,0:T(8,128)S(1)} %get-tuple-element.30.gram_ref, f32[128,128]{1,0:T(8,128)S(1)} %get-tuple-element.33.refs_3_.upper_ref, f32[128,128]{1,0:T(8,128)S(1)} %get-tuple-element.35.lower_ref, f32[128,128]{1,0:T(8,128)S(1)} %get-tuple-element.36.change_ref.lower_ref, ...), custom_call_target="tpu_custom_call" | custom-call | flops 100000000 | bytes 1000000 | tf_op jit(solution)/shard_map/right_end/pallas_call | solution.py:31
  168.1 3.1 %collective-permute-done.32.other_ref = f32[128,128]{1,0:T(8,128)S(1)} collective-permute-done((f32[128,128]{1,0:T(8,128)S(1)}, f32[128,128]{1,0:T(8,128)S(1)}, u32[]{:S(2)}, u32[]{:S(2)}) %collective-permute-start.32) | collective-permute-done | bytes 65568 | tf_op jit(solution)/shard_map/ppermute | solution.py:416
  171.3 4.3 %collective-permute-done.33.other_ref = f32[128,128]{1,0:T(8,128)S(1)} collective-permute-done((f32[128,128]{1,0:T(8,128)S(1)}, f32[128,128]{1,0:T(8,128)S(1)}, u32[]{:S(2)}, u32[]{:S(2)}) %collective-permute-start.33) | collective-permute-done | bytes 65568 | tf_op jit(solution)/shard_map/ppermute | solution.py:416
  175.6 1.7 collective-permute-start.34
  177.2 2.7 %collective-permute-done.34.other_ref = f32[128,128]{1,0:T(8,128)S(1)} collective-permute-done((f32[128,128]{1,0:T(8,128)S(1)}, f32[128,128]{1,0:T(8,128)S(1)}, u32[]{:S(2)}, u32[]{:S(2)}) %collective-permute-start.34) | collective-permute-done | bytes 65568 | tf_op jit(solution)/shard_map/ppermute | solution.py:416
  179.9 9.4 %finish.1 = bf16[896,4096]{1,0:T(8,128)(2,1)} custom-call(f32[128,128]{1,0:T(8,128)S(1)} %add.3.one_ref, f32[128,128]{1,0:T(8,128)S(1)} %collective-permute-done.34.other_ref, bf16[128,896]{1,0:T(8,128)(2,1)S(1)} %get-tuple-element.37.panel_ref, bf16[128,4096]{1,0:T(8,128)(2,1)S(1)} %get-tuple-element.38.wide_ref, ...), custom_call_target="tpu_custom_call" | custom-call | tf_op jit(solution)/shard_map/finish/pallas_call | solution.py:401
  (54 shorter events, 21.3 us)
Async XLA Ops:
  0.0 9.4 %copy-start = (bf16[1,3584,4096]{2,1,0:T(8,128)(2,1)S(1)}, bf16[1,3584,4096]{2,1,0:T(8,128)(2,1)}, u32[]{:S(2)}) copy-start(bf16[1,3584,4096]{2,1,0:T(8,128)(2,1)} %param.2) | copy-start | bytes 88080384
  9.4 1.0 copy-start.1
  20.4 8.3 %collective-permute-start = (bf16[32,1152]{1,0:T(8,128)(2,1)S(1)}, bf16[32,1152]{1,0:T(8,128)(2,1)S(1)}, u32[]{:S(2)}, u32[]{:S(2)}) collective-permute-start(bf16[32,1152]{1,0:T(8,128)(2,1)S(1)} %backs.16.refs_0_), channel_id=1, source_target_pairs={{0,6},{1,7},{2,4},{3,5},{4,2},{5,3},{6,0},{7,1},{8,14},{9,15},{10,... | collective-permute-start | bytes 221192 | tf_op jit(solution)/shard_map/ppermute | solution.py:416
  28.1 4.7 %collective-permute-start.1 = (bf16[32,1152]{1,0:T(8,128)(2,1)S(1)}, bf16[32,1152]{1,0:T(8,128)(2,1)S(1)}, u32[]{:S(2)}, u32[]{:S(2)}) collective-permute-start(bf16[32,1152]{1,0:T(8,128)(2,1)S(1)} %backs.18.refs_0_), channel_id=1, source_target_pairs={{0,2},{1,3},{2,0},{3,1},{4,6},{5,7},{6,4},{7,5},{8,10},{9,11},{10,... | collective-permute-start | bytes 221192 | tf_op jit(solution)/shard_map/ppermute | solution.py:416
  28.1 5.8 %collective-permute-start.2 = (bf16[32,1152]{1,0:T(8,128)(2,1)S(1)}, bf16[32,1152]{1,0:T(8,128)(2,1)S(1)}, u32[]{:S(2)}, u32[]{:S(2)}) collective-permute-start(bf16[32,1152]{1,0:T(8,128)(2,1)S(1)} %backs.17.refs_0_), channel_id=1, source_target_pairs={{0,4},{1,5},{2,6},{3,7},{4,0},{5,1},{6,2},{7,3},{8,12},{9,13},{10,... | collective-permute-start | bytes 221192 | tf_op jit(solution)/shard_map/ppermute | solution.py:416
  34.1 4.4 %collective-permute-start.3 = (bf16[32,1152]{1,0:T(8,128)(2,1)S(1)}, bf16[32,1152]{1,0:T(8,128)(2,1)S(1)}, u32[]{:S(2)}, u32[]{:S(2)}) collective-permute-start(bf16[32,1152]{1,0:T(8,128)(2,1)S(1)} %combine.4.one_ref), channel_id=1, source_target_pairs={{0,1},{1,0},{2,3},{3,2},{4,5},{5,4},{6,7},{7,6},{8,9},{9,8},{10,11... | collective-permute-start | bytes 221192 | tf_op jit(solution)/shard_map/ppermute | solution.py:416
  39.5 4.9 %collective-permute-start.6 = (bf16[32,1024]{1,0:T(8,128)(2,1)S(1)}, bf16[32,1024]{1,0:T(8,128)(2,1)S(1)}, u32[]{:S(2)}, u32[]{:S(2)}) collective-permute-start(bf16[32,1024]{1,0:T(8,128)(2,1)S(1)} %settle.4.refs_0_), channel_id=1, source_target_pairs={{0,2},{1,3},{2,0},{3,1},{4,6},{5,7},{6,4},{7,5},{8,10},{9,11},{10,... | collective-permute-start | bytes 196616 | tf_op jit(solution)/shard_map/ppermute | solution.py:416
  41.0 8.0 %collective-permute-start.5 = (bf16[32,1024]{1,0:T(8,128)(2,1)S(1)}, bf16[32,1024]{1,0:T(8,128)(2,1)S(1)}, u32[]{:S(2)}, u32[]{:S(2)}) collective-permute-start(bf16[32,1024]{1,0:T(8,128)(2,1)S(1)} %settle.4.refs_0_), channel_id=1, source_target_pairs={{0,6},{1,7},{2,4},{3,5},{4,2},{5,3},{6,0},{7,1},{8,14},{9,15},{10,... | collective-permute-start | bytes 196616 | tf_op jit(solution)/shard_map/ppermute | solution.py:416
  41.7 7.3 %collective-permute-start.4 = (bf16[32,1024]{1,0:T(8,128)(2,1)S(1)}, bf16[32,1024]{1,0:T(8,128)(2,1)S(1)}, u32[]{:S(2)}, u32[]{:S(2)}) collective-permute-start(bf16[32,1024]{1,0:T(8,128)(2,1)S(1)} %settle.4.refs_0_), channel_id=1, source_target_pairs={{0,4},{1,5},{2,6},{3,7},{4,0},{5,1},{6,2},{7,3},{8,12},{9,13},{10,... | collective-permute-start | bytes 196616 | tf_op jit(solution)/shard_map/ppermute | solution.py:416
  56.7 6.2 %collective-permute-start.7 = (bf16[32,1152]{1,0:T(8,128)(2,1)S(1)}, bf16[32,1152]{1,0:T(8,128)(2,1)S(1)}, u32[]{:S(2)}, u32[]{:S(2)}) collective-permute-start(bf16[32,1152]{1,0:T(8,128)(2,1)S(1)} %backs.20.refs_0_), channel_id=1, source_target_pairs={{0,6},{1,7},{2,4},{3,5},{4,2},{5,3},{6,0},{7,1},{8,14},{9,15},{10,... | collective-permute-start | bytes 221192 | tf_op jit(solution)/shard_map/ppermute | solution.py:416
  59.9 4.4 %collective-permute-start.8 = (bf16[32,1152]{1,0:T(8,128)(2,1)S(1)}, bf16[32,1152]{1,0:T(8,128)(2,1)S(1)}, u32[]{:S(2)}, u32[]{:S(2)}) collective-permute-start(bf16[32,1152]{1,0:T(8,128)(2,1)S(1)} %backs.22.refs_0_), channel_id=1, source_target_pairs={{0,2},{1,3},{2,0},{3,1},{4,6},{5,7},{6,4},{7,5},{8,10},{9,11},{10,... | collective-permute-start | bytes 221192 | tf_op jit(solution)/shard_map/ppermute | solution.py:416
  59.9 5.3 %collective-permute-start.9 = (bf16[32,1152]{1,0:T(8,128)(2,1)S(1)}, bf16[32,1152]{1,0:T(8,128)(2,1)S(1)}, u32[]{:S(2)}, u32[]{:S(2)}) collective-permute-start(bf16[32,1152]{1,0:T(8,128)(2,1)S(1)} %backs.21.refs_0_), channel_id=1, source_target_pairs={{0,4},{1,5},{2,6},{3,7},{4,0},{5,1},{6,2},{7,3},{8,12},{9,13},{10,... | collective-permute-start | bytes 221192 | tf_op jit(solution)/shard_map/ppermute | solution.py:416
  65.4 4.4 %collective-permute-start.10 = (bf16[32,1152]{1,0:T(8,128)(2,1)S(1)}, bf16[32,1152]{1,0:T(8,128)(2,1)S(1)}, u32[]{:S(2)}, u32[]{:S(2)}) collective-permute-start(bf16[32,1152]{1,0:T(8,128)(2,1)S(1)} %combine.5.one_ref), channel_id=1, source_target_pairs={{0,1},{1,0},{2,3},{3,2},{4,5},{5,4},{6,7},{7,6},{8,9},{9,8},{10,11... | collective-permute-start | bytes 221192 | tf_op jit(solution)/shard_map/ppermute | solution.py:416
  70.7 4.3 %collective-permute-start.13 = (bf16[32,1024]{1,0:T(8,128)(2,1)S(1)}, bf16[32,1024]{1,0:T(8,128)(2,1)S(1)}, u32[]{:S(2)}, u32[]{:S(2)}) collective-permute-start(bf16[32,1024]{1,0:T(8,128)(2,1)S(1)} %settle.5.refs_0_), channel_id=1, source_target_pairs={{0,2},{1,3},{2,0},{3,1},{4,6},{5,7},{6,4},{7,5},{8,10},{9,11},{10,... | collective-permute-start | bytes 196616 | tf_op jit(solution)/shard_map/ppermute | solution.py:416
  72.8 6.9 %collective-permute-start.12 = (bf16[32,1024]{1,0:T(8,128)(2,1)S(1)}, bf16[32,1024]{1,0:T(8,128)(2,1)S(1)}, u32[]{:S(2)}, u32[]{:S(2)}) collective-permute-start(bf16[32,1024]{1,0:T(8,128)(2,1)S(1)} %settle.5.refs_0_), channel_id=1, source_target_pairs={{0,6},{1,7},{2,4},{3,5},{4,2},{5,3},{6,0},{7,1},{8,14},{9,15},{10,... | collective-permute-start | bytes 196616 | tf_op jit(solution)/shard_map/ppermute | solution.py:416
  74.8 5.4 %collective-permute-start.11 = (bf16[32,1024]{1,0:T(8,128)(2,1)S(1)}, bf16[32,1024]{1,0:T(8,128)(2,1)S(1)}, u32[]{:S(2)}, u32[]{:S(2)}) collective-permute-start(bf16[32,1024]{1,0:T(8,128)(2,1)S(1)} %settle.5.refs_0_), channel_id=1, source_target_pairs={{0,4},{1,5},{2,6},{3,7},{4,0},{5,1},{6,2},{7,3},{8,12},{9,13},{10,... | collective-permute-start | bytes 196616 | tf_op jit(solution)/shard_map/ppermute | solution.py:416
  87.8 6.2 %collective-permute-start.14 = (bf16[32,1152]{1,0:T(8,128)(2,1)S(1)}, bf16[32,1152]{1,0:T(8,128)(2,1)S(1)}, u32[]{:S(2)}, u32[]{:S(2)}) collective-permute-start(bf16[32,1152]{1,0:T(8,128)(2,1)S(1)} %backs.24.refs_0_), channel_id=1, source_target_pairs={{0,6},{1,7},{2,4},{3,5},{4,2},{5,3},{6,0},{7,1},{8,14},{9,15},{10,... | collective-permute-start | bytes 221192 | tf_op jit(solution)/shard_map/ppermute | solution.py:416
  91.2 4.5 %collective-permute-start.15 = (bf16[32,1152]{1,0:T(8,128)(2,1)S(1)}, bf16[32,1152]{1,0:T(8,128)(2,1)S(1)}, u32[]{:S(2)}, u32[]{:S(2)}) collective-permute-start(bf16[32,1152]{1,0:T(8,128)(2,1)S(1)} %backs.26.refs_0_), channel_id=1, source_target_pairs={{0,2},{1,3},{2,0},{3,1},{4,6},{5,7},{6,4},{7,5},{8,10},{9,11},{10,... | collective-permute-start | bytes 221192 | tf_op jit(solution)/shard_map/ppermute | solution.py:416
  91.8 6.4 %collective-permute-start.16 = (bf16[32,1152]{1,0:T(8,128)(2,1)S(1)}, bf16[32,1152]{1,0:T(8,128)(2,1)S(1)}, u32[]{:S(2)}, u32[]{:S(2)}) collective-permute-start(bf16[32,1152]{1,0:T(8,128)(2,1)S(1)} %backs.25.refs_0_), channel_id=1, source_target_pairs={{0,4},{1,5},{2,6},{3,7},{4,0},{5,1},{6,2},{7,3},{8,12},{9,13},{10,... | collective-permute-start | bytes 221192 | tf_op jit(solution)/shard_map/ppermute | solution.py:416
  98.4 4.4 %collective-permute-start.17 = (bf16[32,1152]{1,0:T(8,128)(2,1)S(1)}, bf16[32,1152]{1,0:T(8,128)(2,1)S(1)}, u32[]{:S(2)}, u32[]{:S(2)}) collective-permute-start(bf16[32,1152]{1,0:T(8,128)(2,1)S(1)} %combine.6.one_ref), channel_id=1, source_target_pairs={{0,1},{1,0},{2,3},{3,2},{4,5},{5,4},{6,7},{7,6},{8,9},{9,8},{10,11... | collective-permute-start | bytes 221192 | tf_op jit(solution)/shard_map/ppermute | solution.py:416
  103.8 4.3 %collective-permute-start.20 = (bf16[32,1024]{1,0:T(8,128)(2,1)S(1)}, bf16[32,1024]{1,0:T(8,128)(2,1)S(1)}, u32[]{:S(2)}, u32[]{:S(2)}) collective-permute-start(bf16[32,1024]{1,0:T(8,128)(2,1)S(1)} %settle.6.refs_0_), channel_id=1, source_target_pairs={{0,2},{1,3},{2,0},{3,1},{4,6},{5,7},{6,4},{7,5},{8,10},{9,11},{10,... | collective-permute-start | bytes 196616 | tf_op jit(solution)/shard_map/ppermute | solution.py:416
  104.2 8.5 %collective-permute-start.19 = (bf16[32,1024]{1,0:T(8,128)(2,1)S(1)}, bf16[32,1024]{1,0:T(8,128)(2,1)S(1)}, u32[]{:S(2)}, u32[]{:S(2)}) collective-permute-start(bf16[32,1024]{1,0:T(8,128)(2,1)S(1)} %settle.6.refs_0_), channel_id=1, source_target_pairs={{0,6},{1,7},{2,4},{3,5},{4,2},{5,3},{6,0},{7,1},{8,14},{9,15},{10,... | collective-permute-start | bytes 196616 | tf_op jit(solution)/shard_map/ppermute | solution.py:416
  106.6 6.1 %collective-permute-start.18 = (bf16[32,1024]{1,0:T(8,128)(2,1)S(1)}, bf16[32,1024]{1,0:T(8,128)(2,1)S(1)}, u32[]{:S(2)}, u32[]{:S(2)}) collective-permute-start(bf16[32,1024]{1,0:T(8,128)(2,1)S(1)} %settle.6.refs_0_), channel_id=1, source_target_pairs={{0,4},{1,5},{2,6},{3,7},{4,0},{5,1},{6,2},{7,3},{8,12},{9,13},{10,... | collective-permute-start | bytes 196616 | tf_op jit(solution)/shard_map/ppermute | solution.py:416
  120.5 6.8 %collective-permute-start.21 = (bf16[32,1152]{1,0:T(8,128)(2,1)S(1)}, bf16[32,1152]{1,0:T(8,128)(2,1)S(1)}, u32[]{:S(2)}, u32[]{:S(2)}) collective-permute-start(bf16[32,1152]{1,0:T(8,128)(2,1)S(1)} %backs.28.refs_0_), channel_id=1, source_target_pairs={{0,6},{1,7},{2,4},{3,5},{4,2},{5,3},{6,0},{7,1},{8,14},{9,15},{10,... | collective-permute-start | bytes 221192 | tf_op jit(solution)/shard_map/ppermute | solution.py:416
  123.1 6.0 %collective-permute-start.22 = (bf16[32,1152]{1,0:T(8,128)(2,1)S(1)}, bf16[32,1152]{1,0:T(8,128)(2,1)S(1)}, u32[]{:S(2)}, u32[]{:S(2)}) collective-permute-start(bf16[32,1152]{1,0:T(8,128)(2,1)S(1)} %backs.30.refs_0_), channel_id=1, source_target_pairs={{0,2},{1,3},{2,0},{3,1},{4,6},{5,7},{6,4},{7,5},{8,10},{9,11},{10,... | collective-permute-start | bytes 221192 | tf_op jit(solution)/shard_map/ppermute | solution.py:416
  123.8 6.6 %collective-permute-start.23 = (bf16[32,1152]{1,0:T(8,128)(2,1)S(1)}, bf16[32,1152]{1,0:T(8,128)(2,1)S(1)}, u32[]{:S(2)}, u32[]{:S(2)}) collective-permute-start(bf16[32,1152]{1,0:T(8,128)(2,1)S(1)} %backs.29.refs_0_), channel_id=1, source_target_pairs={{0,4},{1,5},{2,6},{3,7},{4,0},{5,1},{6,2},{7,3},{8,12},{9,13},{10,... | collective-permute-start | bytes 221192 | tf_op jit(solution)/shard_map/ppermute | solution.py:416
  130.6 4.4 %collective-permute-start.24 = (bf16[32,1152]{1,0:T(8,128)(2,1)S(1)}, bf16[32,1152]{1,0:T(8,128)(2,1)S(1)}, u32[]{:S(2)}, u32[]{:S(2)}) collective-permute-start(bf16[32,1152]{1,0:T(8,128)(2,1)S(1)} %combine.7.one_ref), channel_id=1, source_target_pairs={{0,1},{1,0},{2,3},{3,2},{4,5},{5,4},{6,7},{7,6},{8,9},{9,8},{10,11... | collective-permute-start | bytes 221192 | tf_op jit(solution)/shard_map/ppermute | solution.py:416
  135.9 4.3 %collective-permute-start.27 = (bf16[32,1024]{1,0:T(8,128)(2,1)S(1)}, bf16[32,1024]{1,0:T(8,128)(2,1)S(1)}, u32[]{:S(2)}, u32[]{:S(2)}) collective-permute-start(bf16[32,1024]{1,0:T(8,128)(2,1)S(1)} %settle.7.refs_0_), channel_id=1, source_target_pairs={{0,2},{1,3},{2,0},{3,1},{4,6},{5,7},{6,4},{7,5},{8,10},{9,11},{10,... | collective-permute-start | bytes 196616 | tf_op jit(solution)/shard_map/ppermute | solution.py:416
  136.0 6.2 %collective-permute-start.26 = (bf16[32,1024]{1,0:T(8,128)(2,1)S(1)}, bf16[32,1024]{1,0:T(8,128)(2,1)S(1)}, u32[]{:S(2)}, u32[]{:S(2)}) collective-permute-start(bf16[32,1024]{1,0:T(8,128)(2,1)S(1)} %settle.7.refs_0_), channel_id=1, source_target_pairs={{0,6},{1,7},{2,4},{3,5},{4,2},{5,3},{6,0},{7,1},{8,14},{9,15},{10,... | collective-permute-start | bytes 196616 | tf_op jit(solution)/shard_map/ppermute | solution.py:416
  138.6 5.3 %collective-permute-start.25 = (bf16[32,1024]{1,0:T(8,128)(2,1)S(1)}, bf16[32,1024]{1,0:T(8,128)(2,1)S(1)}, u32[]{:S(2)}, u32[]{:S(2)}) collective-permute-start(bf16[32,1024]{1,0:T(8,128)(2,1)S(1)} %settle.7.refs_0_), channel_id=1, source_target_pairs={{0,4},{1,5},{2,6},{3,7},{4,0},{5,1},{6,2},{7,3},{8,12},{9,13},{10,... | collective-permute-start | bytes 196616 | tf_op jit(solution)/shard_map/ppermute | solution.py:416
  143.9 10.7 %collective-permute-start.29 = (bf16[1,32,4096]{2,1,0:T(8,128)(2,1)S(1)}, bf16[1,32,4096]{2,1,0:T(8,128)(2,1)S(1)}, u32[]{:S(2)}, u32[]{:S(2)}) collective-permute-start(bf16[1,32,4096]{2,1,0:T(8,128)(2,1)S(1)} %pack.1.refs_0_), channel_id=1, source_target_pairs={{0,16},{8,24},{16,0},{24,8},{1,17},{9,25},{17,1},{25,9},{2,18},{10... | collective-permute-start | bytes 786440 | tf_op jit(solution)/shard_map/ppermute | solution.py:416
  154.6 2.0 %collective-permute-start.30 = (bf16[2,32,4096]{2,1,0:T(8,128)(2,1)S(1)}, bf16[2,32,4096]{2,1,0:T(8,128)(2,1)S(1)}, u32[]{:S(2)}, u32[]{:S(2)}) collective-permute-start(bf16[2,32,4096]{2,1,0:T(8,128)(2,1)S(1)} %join.2), channel_id=1, source_target_pairs={{0,8},{8,0},{16,24},{24,16},{1,9},{9,1},{17,25},{25,17},{2,10},{10... | collective-permute-start | bytes 1572872 | tf_op jit(solution)/shard_map/ppermute | solution.py:416
  154.7 8.0 %collective-permute-start.28 = (bf16[1,4,32,896]{3,2,1,0:T(8,128)(2,1)S(1)}, bf16[1,4,32,896]{3,2,1,0:T(8,128)(2,1)S(1)}, u32[]{:S(2)}, u32[]{:S(2)}) collective-permute-start(bf16[1,4,32,896]{3,2,1,0:T(8,128)(2,1)S(1)} %bitcast.39), channel_id=1, source_target_pairs={{0,16},{8,24},{16,0},{24,8},{1,17},{9,25},{17,1},{25,9},{2,18},{10... | collective-permute-start | bytes 688136 | tf_op jit(solution)/shard_map/ppermute | solution.py:416
  162.8 1.9 collective-permute-start.31
  165.2 6.0 %collective-permute-start.32 = (f32[128,128]{1,0:T(8,128)S(1)}, f32[128,128]{1,0:T(8,128)S(1)}, u32[]{:S(2)}, u32[]{:S(2)}) collective-permute-start(f32[128,128]{1,0:T(8,128)S(1)} %get-tuple-element.34.refs_0_.one_ref), channel_id=1, source_target_pairs={{0,4},{1,5},{2,6},{3,7},{4,0},{5,1},{6,2},{7,3},{8,12},{9,13},{10,... | collective-permute-start | bytes 196616 | tf_op jit(solution)/shard_map/ppermute | solution.py:416
  171.2 4.3 %collective-permute-start.33 = (f32[128,128]{1,0:T(8,128)S(1)}, f32[128,128]{1,0:T(8,128)S(1)}, u32[]{:S(2)}, u32[]{:S(2)}) collective-permute-start(f32[128,128]{1,0:T(8,128)S(1)} %add.2.one_ref), channel_id=1, source_target_pairs={{0,2},{1,3},{2,0},{3,1},{4,6},{5,7},{6,4},{7,5},{8,10},{9,11},{10,... | collective-permute-start | bytes 196616 | tf_op jit(solution)/shard_map/ppermute | solution.py:416
  175.6 4.3 %collective-permute-start.34 = (f32[128,128]{1,0:T(8,128)S(1)}, f32[128,128]{1,0:T(8,128)S(1)}, u32[]{:S(2)}, u32[]{:S(2)}) collective-permute-start(f32[128,128]{1,0:T(8,128)S(1)} %add.3.one_ref), channel_id=1, source_target_pairs={{0,1},{1,0},{2,3},{3,2},{4,5},{5,4},{6,7},{7,6},{8,9},{9,8},{10,11... | collective-permute-start | bytes 196616 | tf_op jit(solution)/shard_map/ppermute | solution.py:416

commit v2 on v1

--- a/solution.py
+++ b/solution.py
@@ -139,7 +139,7 @@
     rows, cols = held.shape
     rank = start.shape[0]
     return call(
-        functools.partial(first_kernel, tall_of(rows, 896, 512, 256, 128)),
+        functools.partial(first_kernel, tall_of(rows, 1792, 896, 512, 256, 128)),
         "first",
         [start],
         [shape_of((rank, rows), BF16), shape_of((rank, LANES), BF16)],
@@ -278,7 +278,7 @@
 
 
 def pack_kernel(masks, _, *refs):
-    *in_refs, out_ref = refs
+    in_refs, out_ref = refs[: len(masks)], refs[-1]
     chunk = in_refs[0].shape[1]
     for mask, in_ref in zip(masks, in_refs):
         out_ref[0, :, block_at(lax.div(partner("row", mask), 2), chunk)] = in_ref[...]
@@ -309,12 +309,13 @@
     )
 
 
-def add_kernel(one_ref, other_ref, *refs):
-    refs[-1][...] = one_ref[...] + other_ref[...]
-
-
-def add(one, other, *after):
-    return call(add_kernel, "add", [one, other], [shape_of(one.shape, F32)], idle=after, flops=10**6)[0]
+def add_kernel(count, *refs):
+    refs[-1][...] = tree_sum([ref[...] for ref in refs[:count]])
+
+
+def add(terms, *after):
+    kernel = functools.partial(add_kernel, len(terms))
+    return call(kernel, "add", terms, [shape_of(terms[0].shape, F32)], idle=after, flops=10**6)[0]
 
 
 def root_begin(gram):
@@ -458,6 +459,7 @@
                 [blocks[mask] for mask in masks],
                 [shape_of((1, block.shape[0], held.shape[1]), BF16)],
                 held=held,
+                idle=[partial],
             )
             (panel,) = images(held, rest, farther, partial, tasks=tasks)
         else:
@@ -476,8 +478,7 @@
     _, panels = gather(panel[None], "task", tasks, lambda one, other: join(one, other, after=[state[0]]))
     state = call(functools.partial(right_steps_kernel, middle), "right_steps", state, [square_shape] * 2)
     gram, panel = left(panels, task_groups, state[0])
-    bit = parts // 2
-    other = send(gram, "row", bit, parts)
+    received = {mask: send(gram, "row", mask, parts) for mask in order[:-1]}
     (right_side,) = call(
         functools.partial(right_end_kernel, ROOT_STEPS - begin - middle),
         "right_end",
@@ -485,11 +486,8 @@
         [square_shape],
         idle=[gram],
     )
-    after = [right_side]
-    while bit > 1:
-        gram, after = add(gram, other, *after), []
-        bit //= 2
-        other = send(gram, "row", bit, parts)
+    gram = add([gram, *[received[mask] for mask in masks[1:]]], right_side)
+    other = send(gram, "row", 1, parts)
     return finish(gram, other, panel, wide, lower, right_side)
 
 

time: 190 us -> 185 us (0.974)
  waiting for transfers between devices: 43.2 us -> 34 us
  starting transfers between devices: 44.7 us -> 49.1 us
    ppermute x35 -> x36, waiting for transfers between devices: 43.2 us -> 34 us  [send(): return lax.ppermute(piece, axis, [(at, at ^ mask) for at in range(count)])]
    ppermute x35 -> x36, starting transfers between devices: 44.7 us -> 49.1 us  [send(): return lax.ppermute(piece, axis, [(at, at ^ mask) for at in range(count)])]
    pallas_call x43 -> x42, Pallas kernels: 81.4 us -> 81.1 us  [call(): pl.pallas_call(kernel, out_shape=tuple(shapes), in_specs=specs, out_specs...]
  transfers between devices with their start and end apart: 35 -> 36, of which waited for: 27 -> 26; matrix products, arithmetic and copies ran while one was open for 0% -> 0% of each run, Pallas kernels for 23% -> 23%
where the time goes in v2:
time: 185 us; the launch traced here: 184 us
  Pallas kernels  90.5 us (49%)
  starting transfers between devices  49.1 us (27%)
  waiting for transfers between devices  34 us (18%)
  local copies, waits for them, and re-layouts  10.4 us (6%)
    pallas_call x42, Pallas kernels, call(): pl.pallas_call(kernel, out_shape=tuple(shapes), in_specs=specs, out_specs...  81.1 us
    ppermute x36, starting transfers between devices, send(): return lax.ppermute(piece, axis, [(at, at ^ mask) for at in range(count)])  49.1 us
    ppermute x36, waiting for transfers between devices, send(): return lax.ppermute(piece, axis, [(at, at ^ mask) for at in range(count)])  34 us
    unnamed x4, local copies, waits for them, and re-layouts  10.4 us
    pallas_call x1, Pallas kernels, finish(): pl.pallas_call(functools.partial(finish_kernel, across), out_shape=shape_...  9.4 us
  transfers between devices with their start and end apart: 36, of which 26 were waited for; matrix products, arithmetic and copies ran while one was open for 0% of the time, Pallas kernels for 23%

profile of v2, /device:TPU:0, one launch (start us, length us, event | category | flops | bytes accessed | tf_op | source)
XLA Modules:
  0.0 184.3 jit_solution(4000498271252584158)
XLA Ops:
  0.0 9.3 %copy-done = bf16[1,3584,4096]{2,1,0:T(8,128)(2,1)S(1)} copy-done((bf16[1,3584,4096]{2,1,0:T(8,128)(2,1)S(1)}, bf16[1,3584,4096]{2,1,0:T(8,128)(2,1)}, u32[]{:S(2)}) %copy-start) | copy-done | bytes 29360152
  9.4 1.0 copy-done.1
  10.4 8.3 %first.1 = (bf16[32,3584]{1,0:T(8,128)(2,1)S(1)}, bf16[32,128]{1,0:T(8,128)(2,1)S(1)}) custom-call(bf16[3584,4096]{1,0:T(8,128)(2,1)S(1)} %bitcast.5, f32[32,4096]{1,0:T(8,128)S(1)} %bitcast.42), custom_call_target="tpu_custom_call" | custom-call | flops 11274289152 | bytes 1000000 | tf_op jit(solution)/shard_map/first/pallas_call | solution.py:31
  18.7 1.4 backs.16.refs_0_
  20.1 5.1 %collective-permute-start = (bf16[32,1152]{1,0:T(8,128)(2,1)S(1)}, bf16[32,1152]{1,0:T(8,128)(2,1)S(1)}, u32[]{:S(2)}, u32[]{:S(2)}) collective-permute-start(bf16[32,1152]{1,0:T(8,128)(2,1)S(1)} %backs.16.refs_0_), channel_id=1, source_target_pairs={{0,6},{1,7},{2,4},{3,5},{4,2},{5,3},{6,0},{7,1},{8,14},{9,15},{10,... | collective-permute-start | bytes 221192 | tf_op jit(solution)/shard_map/ppermute | solution.py:417
  25.1 1.3 backs.17.refs_0_
  26.5 1.4 backs.18.refs_0_
  28.4 1.3 backs.19.refs_0_
  29.8 2.8 %collective-permute-done.1.refs_1_ = bf16[32,1152]{1,0:T(8,128)(2,1)S(1)} collective-permute-done((bf16[32,1152]{1,0:T(8,128)(2,1)S(1)}, bf16[32,1152]{1,0:T(8,128)(2,1)S(1)}, u32[]{:S(2)}, u32[]{:S(2)}) %collective-permute-start.1) | collective-permute-done | bytes 73760 | tf_op jit(solution)/shard_map/ppermute | solution.py:417
  32.6 1.1 collective-permute-done.2.refs_2_
  33.8 1.6 collective-permute-start.3
  35.4 2.8 %collective-permute-done.3.other_ref = bf16[32,1152]{1,0:T(8,128)(2,1)S(1)} collective-permute-done((bf16[32,1152]{1,0:T(8,128)(2,1)S(1)}, bf16[32,1152]{1,0:T(8,128)(2,1)S(1)}, u32[]{:S(2)}, u32[]{:S(2)}) %collective-permute-start.3) | collective-permute-done | bytes 73760 | tf_op jit(solution)/shard_map/ppermute | solution.py:417
  39.2 1.5 collective-permute-start.6
  41.4 1.3 collective-permute-start.4
  42.7 1.4 collective-permute-done.6.refs_1_
  44.1 4.6 %images.8.refs_2_ = f32[32,3584]{1,0:T(8,128)S(1)} custom-call(bf16[3584,4096]{1,0:T(8,128)(2,1)S(1)} %bitcast.12, bf16[32,1024]{1,0:T(8,128)(2,1)S(1)} %settle.4.refs_0_, bf16[32,1024]{1,0:T(8,128)(2,1)S(1)} %collective-permute-done.6.refs_1_), custom_call_target="tpu_custom_call" | custom-call | flops 5637144576 | bytes 1000000 | tf_op jit(solution)/shard_map/images/pallas_call | solution.py:31
  48.7 5.0 %images.9 = (bf16[32,3584]{1,0:T(8,128)(2,1)S(1)}, bf16[32,128]{1,0:T(8,128)(2,1)S(1)}) custom-call(bf16[3584,4096]{1,0:T(8,128)(2,1)S(1)} %bitcast.13, bf16[32,1024]{1,0:T(8,128)(2,1)S(1)} %collective-permute-done.4.refs_0_, bf16[32,1024]{1,0:T(8,128)(2,1)S(1)} %collective-permute-done.5.refs_1_, f32[32,3584]{1,0:T(8,128)S(1)} %images.8.refs_2_), custom_call_target="tpu_custom_call" | custom-call | flops 5637144576 | bytes 1000000 | tf_op jit(solution)/shard_map/images/pallas_call | solution.py:31
  53.7 1.4 backs.20.refs_0_
  55.0 1.4 backs.21.refs_0_
  56.4 1.8 collective-permute-start.7
  58.2 1.3 backs.22.refs_0_
  59.6 2.6 %collective-permute-start.9 = (bf16[32,1152]{1,0:T(8,128)(2,1)S(1)}, bf16[32,1152]{1,0:T(8,128)(2,1)S(1)}, u32[]{:S(2)}, u32[]{:S(2)}) collective-permute-start(bf16[32,1152]{1,0:T(8,128)(2,1)S(1)} %backs.21.refs_0_), channel_id=1, source_target_pairs={{0,4},{1,5},{2,6},{3,7},{4,0},{5,1},{6,2},{7,3},{8,12},{9,13},{10,... | collective-permute-start | bytes 221192 | tf_op jit(solution)/shard_map/ppermute | solution.py:417
  62.6 1.3 backs.23.refs_0_
  65.1 1.6 collective-permute-start.10
  66.6 2.8 %collective-permute-done.10.other_ref = bf16[32,1152]{1,0:T(8,128)(2,1)S(1)} collective-permute-done((bf16[32,1152]{1,0:T(8,128)(2,1)S(1)}, bf16[32,1152]{1,0:T(8,128)(2,1)S(1)}, u32[]{:S(2)}, u32[]{:S(2)}) %collective-permute-start.10) | collective-permute-done | bytes 73760 | tf_op jit(solution)/shard_map/ppermute | solution.py:417
  70.4 2.0 %collective-permute-start.13 = (bf16[32,1024]{1,0:T(8,128)(2,1)S(1)}, bf16[32,1024]{1,0:T(8,128)(2,1)S(1)}, u32[]{:S(2)}, u32[]{:S(2)}) collective-permute-start(bf16[32,1024]{1,0:T(8,128)(2,1)S(1)} %settle.5.refs_0_), channel_id=1, source_target_pairs={{0,2},{1,3},{2,0},{3,1},{4,6},{5,7},{6,4},{7,5},{8,10},{9,11},{10,... | collective-permute-start | bytes 196616 | tf_op jit(solution)/shard_map/ppermute | solution.py:417
  72.5 2.0 %collective-permute-start.12 = (bf16[32,1024]{1,0:T(8,128)(2,1)S(1)}, bf16[32,1024]{1,0:T(8,128)(2,1)S(1)}, u32[]{:S(2)}, u32[]{:S(2)}) collective-permute-start(bf16[32,1024]{1,0:T(8,128)(2,1)S(1)} %settle.5.refs_0_), channel_id=1, source_target_pairs={{0,6},{1,7},{2,4},{3,5},{4,2},{5,3},{6,0},{7,1},{8,14},{9,15},{10,... | collective-permute-start | bytes 196616 | tf_op jit(solution)/shard_map/ppermute | solution.py:417
  74.8 4.6 %images.10.refs_2_ = f32[32,3584]{1,0:T(8,128)S(1)} custom-call(bf16[3584,4096]{1,0:T(8,128)(2,1)S(1)} %bitcast.20, bf16[32,1024]{1,0:T(8,128)(2,1)S(1)} %settle.5.refs_0_, bf16[32,1024]{1,0:T(8,128)(2,1)S(1)} %collective-permute-done.13.refs_1_), custom_call_target="tpu_custom_call" | custom-call | flops 5637144576 | bytes 1000000 | tf_op jit(solution)/shard_map/images/pallas_call | solution.py:31
  79.9 4.8 %images.11 = (bf16[32,3584]{1,0:T(8,128)(2,1)S(1)}, bf16[32,128]{1,0:T(8,128)(2,1)S(1)}) custom-call(bf16[3584,4096]{1,0:T(8,128)(2,1)S(1)} %bitcast.21, bf16[32,1024]{1,0:T(8,128)(2,1)S(1)} %collective-permute-done.11.refs_0_, bf16[32,1024]{1,0:T(8,128)(2,1)S(1)} %collective-permute-done.12.refs_1_, f32[32,3584]{1,0:T(8,128)S(1)} %images.10.refs_2_), custom_call_target="tpu_custom_call" | custom-call | flops 5637144576 | bytes 1000000 | tf_op jit(solution)/shard_map/images/pallas_call | solution.py:31
  84.8 1.4 backs.24.refs_0_
  86.1 1.4 backs.25.refs_0_
  87.5 2.0 %collective-permute-start.14 = (bf16[32,1152]{1,0:T(8,128)(2,1)S(1)}, bf16[32,1152]{1,0:T(8,128)(2,1)S(1)}, u32[]{:S(2)}, u32[]{:S(2)}) collective-permute-start(bf16[32,1152]{1,0:T(8,128)(2,1)S(1)} %backs.24.refs_0_), channel_id=1, source_target_pairs={{0,6},{1,7},{2,4},{3,5},{4,2},{5,3},{6,0},{7,1},{8,14},{9,15},{10,... | collective-permute-start | bytes 221192 | tf_op jit(solution)/shard_map/ppermute | solution.py:417
  89.5 1.3 backs.26.refs_0_
  91.5 1.7 collective-permute-start.16
  93.7 1.3 backs.27.refs_0_
  95.4 2.6 %collective-permute-done.16.refs_2_ = bf16[32,1152]{1,0:T(8,128)(2,1)S(1)} collective-permute-done((bf16[32,1152]{1,0:T(8,128)(2,1)S(1)}, bf16[32,1152]{1,0:T(8,128)(2,1)S(1)}, u32[]{:S(2)}, u32[]{:S(2)}) %collective-permute-start.16) | collective-permute-done | bytes 73760 | tf_op jit(solution)/shard_map/ppermute | solution.py:417
  98.1 1.5 collective-permute-start.17
  99.7 2.9 %collective-permute-done.17.other_ref = bf16[32,1152]{1,0:T(8,128)(2,1)S(1)} collective-permute-done((bf16[32,1152]{1,0:T(8,128)(2,1)S(1)}, bf16[32,1152]{1,0:T(8,128)(2,1)S(1)}, u32[]{:S(2)}, u32[]{:S(2)}) %collective-permute-start.17) | collective-permute-done | bytes 73760 | tf_op jit(solution)/shard_map/ppermute | solution.py:417
  103.9 2.4 %collective-permute-start.19 = (bf16[32,1024]{1,0:T(8,128)(2,1)S(1)}, bf16[32,1024]{1,0:T(8,128)(2,1)S(1)}, u32[]{:S(2)}, u32[]{:S(2)}) collective-permute-start(bf16[32,1024]{1,0:T(8,128)(2,1)S(1)} %settle.6.refs_0_), channel_id=1, source_target_pairs={{0,6},{1,7},{2,4},{3,5},{4,2},{5,3},{6,0},{7,1},{8,14},{9,15},{10,... | collective-permute-start | bytes 196616 | tf_op jit(solution)/shard_map/ppermute | solution.py:417
  107.8 4.6 %images.12.refs_2_ = f32[32,3584]{1,0:T(8,128)S(1)} custom-call(bf16[3584,4096]{1,0:T(8,128)(2,1)S(1)} %bitcast.28, bf16[32,1024]{1,0:T(8,128)(2,1)S(1)} %settle.6.refs_0_, bf16[32,1024]{1,0:T(8,128)(2,1)S(1)} %collective-permute-done.20.refs_1_), custom_call_target="tpu_custom_call" | custom-call | flops 5637144576 | bytes 1000000 | tf_op jit(solution)/shard_map/images/pallas_call | solution.py:31
  112.4 5.1 %images.13 = (bf16[32,3584]{1,0:T(8,128)(2,1)S(1)}, bf16[32,128]{1,0:T(8,128)(2,1)S(1)}) custom-call(bf16[3584,4096]{1,0:T(8,128)(2,1)S(1)} %bitcast.29, bf16[32,1024]{1,0:T(8,128)(2,1)S(1)} %collective-permute-done.18.refs_0_, bf16[32,1024]{1,0:T(8,128)(2,1)S(1)} %collective-permute-done.19.refs_1_, f32[32,3584]{1,0:T(8,128)S(1)} %images.12.refs_2_), custom_call_target="tpu_custom_call" | custom-call | flops 5637144576 | bytes 1000000 | tf_op jit(solution)/shard_map/images/pallas_call | solution.py:31
  117.5 1.4 backs.28.refs_0_
  118.8 1.4 backs.29.refs_0_
  120.2 1.3 collective-permute-start.21
  121.4 1.3 backs.30.refs_0_
  123.5 2.4 %collective-permute-start.23 = (bf16[32,1152]{1,0:T(8,128)(2,1)S(1)}, bf16[32,1152]{1,0:T(8,128)(2,1)S(1)}, u32[]{:S(2)}, u32[]{:S(2)}) collective-permute-start(bf16[32,1152]{1,0:T(8,128)(2,1)S(1)} %backs.29.refs_0_), channel_id=1, source_target_pairs={{0,4},{1,5},{2,6},{3,7},{4,0},{5,1},{6,2},{7,3},{8,12},{9,13},{10,... | collective-permute-start | bytes 221192 | tf_op jit(solution)/shard_map/ppermute | solution.py:417
  126.9 1.3 backs.31.refs_0_
  128.8 1.3 collective-permute-done.23.refs_2_
  130.3 1.5 collective-permute-start.24
  131.8 2.8 %collective-permute-done.24.other_ref = bf16[32,1152]{1,0:T(8,128)(2,1)S(1)} collective-permute-done((bf16[32,1152]{1,0:T(8,128)(2,1)S(1)}, bf16[32,1152]{1,0:T(8,128)(2,1)S(1)}, u32[]{:S(2)}, u32[]{:S(2)}) %collective-permute-start.24) | collective-permute-done | bytes 73760 | tf_op jit(solution)/shard_map/ppermute | solution.py:417
  135.7 2.6 %collective-permute-start.26 = (bf16[32,1024]{1,0:T(8,128)(2,1)S(1)}, bf16[32,1024]{1,0:T(8,128)(2,1)S(1)}, u32[]{:S(2)}, u32[]{:S(2)}) collective-permute-start(bf16[32,1024]{1,0:T(8,128)(2,1)S(1)} %settle.7.refs_0_), channel_id=1, source_target_pairs={{0,6},{1,7},{2,4},{3,5},{4,2},{5,3},{6,0},{7,1},{8,14},{9,15},{10,... | collective-permute-start | bytes 196616 | tf_op jit(solution)/shard_map/ppermute | solution.py:417
  140.0 4.6 %images.14.refs_2_.refs_4_ = f32[32,3584]{1,0:T(8,128)S(1)} custom-call(bf16[3584,4096]{1,0:T(8,128)(2,1)S(1)} %bitcast.36, bf16[32,1024]{1,0:T(8,128)(2,1)S(1)} %settle.7.refs_0_, bf16[32,1024]{1,0:T(8,128)(2,1)S(1)} %collective-permute-done.27.refs_1_), custom_call_target="tpu_custom_call" | custom-call | flops 5637144576 | bytes 1000000 | tf_op jit(solution)/shard_map/images/pallas_call | solution.py:31
  144.6 1.5 collective-permute-start.29
  146.1 4.6 %images.15.refs_2_ = bf16[4,32,896]{2,1,0:T(8,128)(2,1)S(1)} custom-call(bf16[3584,4096]{1,0:T(8,128)(2,1)S(1)} %bitcast.38, bf16[32,1024]{1,0:T(8,128)(2,1)S(1)} %collective-permute-done.25.refs_0_.refs_2_, bf16[32,1024]{1,0:T(8,128)(2,1)S(1)} %collective-permute-done.26.refs_1_.refs_3_, f32[32,3584]{1,0:T(8,128)S(1)} %images.14.refs_2_.refs_4_), custom_call_target="tpu_custom_call" | custom-call | flops 5637144576 | bytes 1000000 | tf_op jit(solution)/shard_map/images/pallas_call | solution.py:31
  151.1 1.5 collective-permute-start.28
  153.0 2.8 %right_first.1 = (bf16[128,4096]{1,0:T(8,128)(2,1)S(1)}, f32[128,128]{1,0:T(8,128)S(1)}, f32[128,128]{1,0:T(8,128)S(1)}) custom-call(bf16[1,32,4096]{2,1,0:T(8,128)(2,1)S(1)} %pack.1.refs_0_, bf16[1,32,4096]{2,1,0:T(8,128)(2,1)S(1)} %collective-permute-done.29.refs_1_, bf16[2,32,4096]{2,1,0:T(8,128)(2,1)S(1)} %collective-permute-done.30.refs_2_), custom_call_target="tpu_custom_call" | custom-call | flops 100000000 | bytes 1000000 | tf_op jit(solution)/shard_map/right_first/pallas_call | solution.py:31
  155.9 2.6 %right_begin.1 = (f32[128,128]{1,0:T(8,128)S(1)}, f32[128,128]{1,0:T(8,128)S(1)}) custom-call(f32[128,128]{1,0:T(8,128)S(1)} %get-tuple-element.30.gram_ref), custom_call_target="tpu_custom_call" | custom-call | flops 100000000 | bytes 1000000 | tf_op jit(solution)/shard_map/right_begin/pallas_call | solution.py:31
  161.6 1.3 collective-permute-start.34
  163.3 2.7 %collective-permute-start.32 = (f32[128,128]{1,0:T(8,128)S(1)}, f32[128,128]{1,0:T(8,128)S(1)}, u32[]{:S(2)}, u32[]{:S(2)}) collective-permute-start(f32[128,128]{1,0:T(8,128)S(1)} %get-tuple-element.34.refs_0_), channel_id=1, source_target_pairs={{0,2},{1,3},{2,0},{3,1},{4,6},{5,7},{6,4},{7,5},{8,10},{9,11},{10,... | collective-permute-start | bytes 196616 | tf_op jit(solution)/shard_map/ppermute | solution.py:417
  166.0 2.1 %right_end.1.refs_4_.right_ref = f32[128,128]{1,0:T(8,128)S(1)} custom-call(f32[128,128]{1,0:T(8,128)S(1)} %get-tuple-element.30.gram_ref, f32[128,128]{1,0:T(8,128)S(1)} %get-tuple-element.33.refs_3_.upper_ref, f32[128,128]{1,0:T(8,128)S(1)} %get-tuple-element.35.lower_ref, f32[128,128]{1,0:T(8,128)S(1)} %get-tuple-element.36.change_ref.lower_ref, ...), custom_call_target="tpu_custom_call" | custom-call | flops 100000000 | bytes 1000000 | tf_op jit(solution)/shard_map/right_end/pallas_call | solution.py:31
  168.4 1.9 %collective-permute-done.33.refs_2_ = f32[128,128]{1,0:T(8,128)S(1)} collective-permute-done((f32[128,128]{1,0:T(8,128)S(1)}, f32[128,128]{1,0:T(8,128)S(1)}, u32[]{:S(2)}, u32[]{:S(2)}) %collective-permute-start.33) | collective-permute-done | bytes 65568 | tf_op jit(solution)/shard_map/ppermute | solution.py:417
  170.4 1.6 collective-permute-start.35
  172.0 2.8 %collective-permute-done.35.other_ref = f32[128,128]{1,0:T(8,128)S(1)} collective-permute-done((f32[128,128]{1,0:T(8,128)S(1)}, f32[128,128]{1,0:T(8,128)S(1)}, u32[]{:S(2)}, u32[]{:S(2)}) %collective-permute-start.35) | collective-permute-done | bytes 65568 | tf_op jit(solution)/shard_map/ppermute | solution.py:417
  174.7 9.4 %finish.1 = bf16[896,4096]{1,0:T(8,128)(2,1)} custom-call(f32[128,128]{1,0:T(8,128)S(1)} %add.1.one_ref, f32[128,128]{1,0:T(8,128)S(1)} %collective-permute-done.35.other_ref, bf16[128,896]{1,0:T(8,128)(2,1)S(1)} %get-tuple-element.37.panel_ref, bf16[128,4096]{1,0:T(8,128)(2,1)S(1)} %get-tuple-element.38.wide_ref, ...), custom_call_target="tpu_custom_call" | custom-call | tf_op jit(solution)/shard_map/finish/pallas_call | solution.py:402
  (55 shorter events, 20.1 us)
Async XLA Ops:
  0.0 9.4 %copy-start = (bf16[1,3584,4096]{2,1,0:T(8,128)(2,1)S(1)}, bf16[1,3584,4096]{2,1,0:T(8,128)(2,1)}, u32[]{:S(2)}) copy-start(bf16[1,3584,4096]{2,1,0:T(8,128)(2,1)} %param.2) | copy-start | bytes 88080384
  9.4 1.0 copy-start.1
  20.1 8.4 %collective-permute-start = (bf16[32,1152]{1,0:T(8,128)(2,1)S(1)}, bf16[32,1152]{1,0:T(8,128)(2,1)S(1)}, u32[]{:S(2)}, u32[]{:S(2)}) collective-permute-start(bf16[32,1152]{1,0:T(8,128)(2,1)S(1)} %backs.16.refs_0_), channel_id=1, source_target_pairs={{0,6},{1,7},{2,4},{3,5},{4,2},{5,3},{6,0},{7,1},{8,14},{9,15},{10,... | collective-permute-start | bytes 221192 | tf_op jit(solution)/shard_map/ppermute | solution.py:417
  27.8 4.7 %collective-permute-start.1 = (bf16[32,1152]{1,0:T(8,128)(2,1)S(1)}, bf16[32,1152]{1,0:T(8,128)(2,1)S(1)}, u32[]{:S(2)}, u32[]{:S(2)}) collective-permute-start(bf16[32,1152]{1,0:T(8,128)(2,1)S(1)} %backs.18.refs_0_), channel_id=1, source_target_pairs={{0,2},{1,3},{2,0},{3,1},{4,6},{5,7},{6,4},{7,5},{8,10},{9,11},{10,... | collective-permute-start | bytes 221192 | tf_op jit(solution)/shard_map/ppermute | solution.py:417
  27.8 5.8 %collective-permute-start.2 = (bf16[32,1152]{1,0:T(8,128)(2,1)S(1)}, bf16[32,1152]{1,0:T(8,128)(2,1)S(1)}, u32[]{:S(2)}, u32[]{:S(2)}) collective-permute-start(bf16[32,1152]{1,0:T(8,128)(2,1)S(1)} %backs.17.refs_0_), channel_id=1, source_target_pairs={{0,4},{1,5},{2,6},{3,7},{4,0},{5,1},{6,2},{7,3},{8,12},{9,13},{10,... | collective-permute-start | bytes 221192 | tf_op jit(solution)/shard_map/ppermute | solution.py:417
  33.8 4.4 %collective-permute-start.3 = (bf16[32,1152]{1,0:T(8,128)(2,1)S(1)}, bf16[32,1152]{1,0:T(8,128)(2,1)S(1)}, u32[]{:S(2)}, u32[]{:S(2)}) collective-permute-start(bf16[32,1152]{1,0:T(8,128)(2,1)S(1)} %combine.4.one_ref), channel_id=1, source_target_pairs={{0,1},{1,0},{2,3},{3,2},{4,5},{5,4},{6,7},{7,6},{8,9},{9,8},{10,11... | collective-permute-start | bytes 221192 | tf_op jit(solution)/shard_map/ppermute | solution.py:417
  39.2 4.9 %collective-permute-start.6 = (bf16[32,1024]{1,0:T(8,128)(2,1)S(1)}, bf16[32,1024]{1,0:T(8,128)(2,1)S(1)}, u32[]{:S(2)}, u32[]{:S(2)}) collective-permute-start(bf16[32,1024]{1,0:T(8,128)(2,1)S(1)} %settle.4.refs_0_), channel_id=1, source_target_pairs={{0,2},{1,3},{2,0},{3,1},{4,6},{5,7},{6,4},{7,5},{8,10},{9,11},{10,... | collective-permute-start | bytes 196616 | tf_op jit(solution)/shard_map/ppermute | solution.py:417
  40.7 8.0 %collective-permute-start.5 = (bf16[32,1024]{1,0:T(8,128)(2,1)S(1)}, bf16[32,1024]{1,0:T(8,128)(2,1)S(1)}, u32[]{:S(2)}, u32[]{:S(2)}) collective-permute-start(bf16[32,1024]{1,0:T(8,128)(2,1)S(1)} %settle.4.refs_0_), channel_id=1, source_target_pairs={{0,6},{1,7},{2,4},{3,5},{4,2},{5,3},{6,0},{7,1},{8,14},{9,15},{10,... | collective-permute-start | bytes 196616 | tf_op jit(solution)/shard_map/ppermute | solution.py:417
  41.4 7.3 %collective-permute-start.4 = (bf16[32,1024]{1,0:T(8,128)(2,1)S(1)}, bf16[32,1024]{1,0:T(8,128)(2,1)S(1)}, u32[]{:S(2)}, u32[]{:S(2)}) collective-permute-start(bf16[32,1024]{1,0:T(8,128)(2,1)S(1)} %settle.4.refs_0_), channel_id=1, source_target_pairs={{0,4},{1,5},{2,6},{3,7},{4,0},{5,1},{6,2},{7,3},{8,12},{9,13},{10,... | collective-permute-start | bytes 196616 | tf_op jit(solution)/shard_map/ppermute | solution.py:417
  56.4 6.2 %collective-permute-start.7 = (bf16[32,1152]{1,0:T(8,128)(2,1)S(1)}, bf16[32,1152]{1,0:T(8,128)(2,1)S(1)}, u32[]{:S(2)}, u32[]{:S(2)}) collective-permute-start(bf16[32,1152]{1,0:T(8,128)(2,1)S(1)} %backs.20.refs_0_), channel_id=1, source_target_pairs={{0,6},{1,7},{2,4},{3,5},{4,2},{5,3},{6,0},{7,1},{8,14},{9,15},{10,... | collective-permute-start | bytes 221192 | tf_op jit(solution)/shard_map/ppermute | solution.py:417
  59.6 4.4 %collective-permute-start.8 = (bf16[32,1152]{1,0:T(8,128)(2,1)S(1)}, bf16[32,1152]{1,0:T(8,128)(2,1)S(1)}, u32[]{:S(2)}, u32[]{:S(2)}) collective-permute-start(bf16[32,1152]{1,0:T(8,128)(2,1)S(1)} %backs.22.refs_0_), channel_id=1, source_target_pairs={{0,2},{1,3},{2,0},{3,1},{4,6},{5,7},{6,4},{7,5},{8,10},{9,11},{10,... | collective-permute-start | bytes 221192 | tf_op jit(solution)/shard_map/ppermute | solution.py:417
  59.6 5.3 %collective-permute-start.9 = (bf16[32,1152]{1,0:T(8,128)(2,1)S(1)}, bf16[32,1152]{1,0:T(8,128)(2,1)S(1)}, u32[]{:S(2)}, u32[]{:S(2)}) collective-permute-start(bf16[32,1152]{1,0:T(8,128)(2,1)S(1)} %backs.21.refs_0_), channel_id=1, source_target_pairs={{0,4},{1,5},{2,6},{3,7},{4,0},{5,1},{6,2},{7,3},{8,12},{9,13},{10,... | collective-permute-start | bytes 221192 | tf_op jit(solution)/shard_map/ppermute | solution.py:417
  65.1 4.4 %collective-permute-start.10 = (bf16[32,1152]{1,0:T(8,128)(2,1)S(1)}, bf16[32,1152]{1,0:T(8,128)(2,1)S(1)}, u32[]{:S(2)}, u32[]{:S(2)}) collective-permute-start(bf16[32,1152]{1,0:T(8,128)(2,1)S(1)} %combine.5.one_ref), channel_id=1, source_target_pairs={{0,1},{1,0},{2,3},{3,2},{4,5},{5,4},{6,7},{7,6},{8,9},{9,8},{10,11... | collective-permute-start | bytes 221192 | tf_op jit(solution)/shard_map/ppermute | solution.py:417
  70.4 4.3 %collective-permute-start.13 = (bf16[32,1024]{1,0:T(8,128)(2,1)S(1)}, bf16[32,1024]{1,0:T(8,128)(2,1)S(1)}, u32[]{:S(2)}, u32[]{:S(2)}) collective-permute-start(bf16[32,1024]{1,0:T(8,128)(2,1)S(1)} %settle.5.refs_0_), channel_id=1, source_target_pairs={{0,2},{1,3},{2,0},{3,1},{4,6},{5,7},{6,4},{7,5},{8,10},{9,11},{10,... | collective-permute-start | bytes 196616 | tf_op jit(solution)/shard_map/ppermute | solution.py:417
  72.5 6.9 %collective-permute-start.12 = (bf16[32,1024]{1,0:T(8,128)(2,1)S(1)}, bf16[32,1024]{1,0:T(8,128)(2,1)S(1)}, u32[]{:S(2)}, u32[]{:S(2)}) collective-permute-start(bf16[32,1024]{1,0:T(8,128)(2,1)S(1)} %settle.5.refs_0_), channel_id=1, source_target_pairs={{0,6},{1,7},{2,4},{3,5},{4,2},{5,3},{6,0},{7,1},{8,14},{9,15},{10,... | collective-permute-start | bytes 196616 | tf_op jit(solution)/shard_map/ppermute | solution.py:417
  74.5 5.4 %collective-permute-start.11 = (bf16[32,1024]{1,0:T(8,128)(2,1)S(1)}, bf16[32,1024]{1,0:T(8,128)(2,1)S(1)}, u32[]{:S(2)}, u32[]{:S(2)}) collective-permute-start(bf16[32,1024]{1,0:T(8,128)(2,1)S(1)} %settle.5.refs_0_), channel_id=1, source_target_pairs={{0,4},{1,5},{2,6},{3,7},{4,0},{5,1},{6,2},{7,3},{8,12},{9,13},{10,... | collective-permute-start | bytes 196616 | tf_op jit(solution)/shard_map/ppermute | solution.py:417
  87.5 6.2 %collective-permute-start.14 = (bf16[32,1152]{1,0:T(8,128)(2,1)S(1)}, bf16[32,1152]{1,0:T(8,128)(2,1)S(1)}, u32[]{:S(2)}, u32[]{:S(2)}) collective-permute-start(bf16[32,1152]{1,0:T(8,128)(2,1)S(1)} %backs.24.refs_0_), channel_id=1, source_target_pairs={{0,6},{1,7},{2,4},{3,5},{4,2},{5,3},{6,0},{7,1},{8,14},{9,15},{10,... | collective-permute-start | bytes 221192 | tf_op jit(solution)/shard_map/ppermute | solution.py:417
  90.9 4.5 %collective-permute-start.15 = (bf16[32,1152]{1,0:T(8,128)(2,1)S(1)}, bf16[32,1152]{1,0:T(8,128)(2,1)S(1)}, u32[]{:S(2)}, u32[]{:S(2)}) collective-permute-start(bf16[32,1152]{1,0:T(8,128)(2,1)S(1)} %backs.26.refs_0_), channel_id=1, source_target_pairs={{0,2},{1,3},{2,0},{3,1},{4,6},{5,7},{6,4},{7,5},{8,10},{9,11},{10,... | collective-permute-start | bytes 221192 | tf_op jit(solution)/shard_map/ppermute | solution.py:417
  91.5 6.4 %collective-permute-start.16 = (bf16[32,1152]{1,0:T(8,128)(2,1)S(1)}, bf16[32,1152]{1,0:T(8,128)(2,1)S(1)}, u32[]{:S(2)}, u32[]{:S(2)}) collective-permute-start(bf16[32,1152]{1,0:T(8,128)(2,1)S(1)} %backs.25.refs_0_), channel_id=1, source_target_pairs={{0,4},{1,5},{2,6},{3,7},{4,0},{5,1},{6,2},{7,3},{8,12},{9,13},{10,... | collective-permute-start | bytes 221192 | tf_op jit(solution)/shard_map/ppermute | solution.py:417
  98.1 4.4 %collective-permute-start.17 = (bf16[32,1152]{1,0:T(8,128)(2,1)S(1)}, bf16[32,1152]{1,0:T(8,128)(2,1)S(1)}, u32[]{:S(2)}, u32[]{:S(2)}) collective-permute-start(bf16[32,1152]{1,0:T(8,128)(2,1)S(1)} %combine.6.one_ref), channel_id=1, source_target_pairs={{0,1},{1,0},{2,3},{3,2},{4,5},{5,4},{6,7},{7,6},{8,9},{9,8},{10,11... | collective-permute-start | bytes 221192 | tf_op jit(solution)/shard_map/ppermute | solution.py:417
  103.5 4.3 %collective-permute-start.20 = (bf16[32,1024]{1,0:T(8,128)(2,1)S(1)}, bf16[32,1024]{1,0:T(8,128)(2,1)S(1)}, u32[]{:S(2)}, u32[]{:S(2)}) collective-permute-start(bf16[32,1024]{1,0:T(8,128)(2,1)S(1)} %settle.6.refs_0_), channel_id=1, source_target_pairs={{0,2},{1,3},{2,0},{3,1},{4,6},{5,7},{6,4},{7,5},{8,10},{9,11},{10,... | collective-permute-start | bytes 196616 | tf_op jit(solution)/shard_map/ppermute | solution.py:417
  103.9 8.5 %collective-permute-start.19 = (bf16[32,1024]{1,0:T(8,128)(2,1)S(1)}, bf16[32,1024]{1,0:T(8,128)(2,1)S(1)}, u32[]{:S(2)}, u32[]{:S(2)}) collective-permute-start(bf16[32,1024]{1,0:T(8,128)(2,1)S(1)} %settle.6.refs_0_), channel_id=1, source_target_pairs={{0,6},{1,7},{2,4},{3,5},{4,2},{5,3},{6,0},{7,1},{8,14},{9,15},{10,... | collective-permute-start | bytes 196616 | tf_op jit(solution)/shard_map/ppermute | solution.py:417
  106.3 6.1 %collective-permute-start.18 = (bf16[32,1024]{1,0:T(8,128)(2,1)S(1)}, bf16[32,1024]{1,0:T(8,128)(2,1)S(1)}, u32[]{:S(2)}, u32[]{:S(2)}) collective-permute-start(bf16[32,1024]{1,0:T(8,128)(2,1)S(1)} %settle.6.refs_0_), channel_id=1, source_target_pairs={{0,4},{1,5},{2,6},{3,7},{4,0},{5,1},{6,2},{7,3},{8,12},{9,13},{10,... | collective-permute-start | bytes 196616 | tf_op jit(solution)/shard_map/ppermute | solution.py:417
  120.2 6.8 %collective-permute-start.21 = (bf16[32,1152]{1,0:T(8,128)(2,1)S(1)}, bf16[32,1152]{1,0:T(8,128)(2,1)S(1)}, u32[]{:S(2)}, u32[]{:S(2)}) collective-permute-start(bf16[32,1152]{1,0:T(8,128)(2,1)S(1)} %backs.28.refs_0_), channel_id=1, source_target_pairs={{0,6},{1,7},{2,4},{3,5},{4,2},{5,3},{6,0},{7,1},{8,14},{9,15},{10,... | collective-permute-start | bytes 221192 | tf_op jit(solution)/shard_map/ppermute | solution.py:417
  122.8 6.0 %collective-permute-start.22 = (bf16[32,1152]{1,0:T(8,128)(2,1)S(1)}, bf16[32,1152]{1,0:T(8,128)(2,1)S(1)}, u32[]{:S(2)}, u32[]{:S(2)}) collective-permute-start(bf16[32,1152]{1,0:T(8,128)(2,1)S(1)} %backs.30.refs_0_), channel_id=1, source_target_pairs={{0,2},{1,3},{2,0},{3,1},{4,6},{5,7},{6,4},{7,5},{8,10},{9,11},{10,... | collective-permute-start | bytes 221192 | tf_op jit(solution)/shard_map/ppermute | solution.py:417
  123.5 6.6 %collective-permute-start.23 = (bf16[32,1152]{1,0:T(8,128)(2,1)S(1)}, bf16[32,1152]{1,0:T(8,128)(2,1)S(1)}, u32[]{:S(2)}, u32[]{:S(2)}) collective-permute-start(bf16[32,1152]{1,0:T(8,128)(2,1)S(1)} %backs.29.refs_0_), channel_id=1, source_target_pairs={{0,4},{1,5},{2,6},{3,7},{4,0},{5,1},{6,2},{7,3},{8,12},{9,13},{10,... | collective-permute-start | bytes 221192 | tf_op jit(solution)/shard_map/ppermute | solution.py:417
  130.3 4.4 %collective-permute-start.24 = (bf16[32,1152]{1,0:T(8,128)(2,1)S(1)}, bf16[32,1152]{1,0:T(8,128)(2,1)S(1)}, u32[]{:S(2)}, u32[]{:S(2)}) collective-permute-start(bf16[32,1152]{1,0:T(8,128)(2,1)S(1)} %combine.7.one_ref), channel_id=1, source_target_pairs={{0,1},{1,0},{2,3},{3,2},{4,5},{5,4},{6,7},{7,6},{8,9},{9,8},{10,11... | collective-permute-start | bytes 221192 | tf_op jit(solution)/shard_map/ppermute | solution.py:417
  135.6 4.3 %collective-permute-start.27 = (bf16[32,1024]{1,0:T(8,128)(2,1)S(1)}, bf16[32,1024]{1,0:T(8,128)(2,1)S(1)}, u32[]{:S(2)}, u32[]{:S(2)}) collective-permute-start(bf16[32,1024]{1,0:T(8,128)(2,1)S(1)} %settle.7.refs_0_), channel_id=1, source_target_pairs={{0,2},{1,3},{2,0},{3,1},{4,6},{5,7},{6,4},{7,5},{8,10},{9,11},{10,... | collective-permute-start | bytes 196616 | tf_op jit(solution)/shard_map/ppermute | solution.py:417
  135.7 8.8 %collective-permute-start.26 = (bf16[32,1024]{1,0:T(8,128)(2,1)S(1)}, bf16[32,1024]{1,0:T(8,128)(2,1)S(1)}, u32[]{:S(2)}, u32[]{:S(2)}) collective-permute-start(bf16[32,1024]{1,0:T(8,128)(2,1)S(1)} %settle.7.refs_0_), channel_id=1, source_target_pairs={{0,6},{1,7},{2,4},{3,5},{4,2},{5,3},{6,0},{7,1},{8,14},{9,15},{10,... | collective-permute-start | bytes 196616 | tf_op jit(solution)/shard_map/ppermute | solution.py:417
  138.3 6.3 %collective-permute-start.25 = (bf16[32,1024]{1,0:T(8,128)(2,1)S(1)}, bf16[32,1024]{1,0:T(8,128)(2,1)S(1)}, u32[]{:S(2)}, u32[]{:S(2)}) collective-permute-start(bf16[32,1024]{1,0:T(8,128)(2,1)S(1)} %settle.7.refs_0_), channel_id=1, source_target_pairs={{0,4},{1,5},{2,6},{3,7},{4,0},{5,1},{6,2},{7,3},{8,12},{9,13},{10,... | collective-permute-start | bytes 196616 | tf_op jit(solution)/shard_map/ppermute | solution.py:417
  144.6 6.4 %collective-permute-start.29 = (bf16[1,32,4096]{2,1,0:T(8,128)(2,1)S(1)}, bf16[1,32,4096]{2,1,0:T(8,128)(2,1)S(1)}, u32[]{:S(2)}, u32[]{:S(2)}) collective-permute-start(bf16[1,32,4096]{2,1,0:T(8,128)(2,1)S(1)} %pack.1.refs_0_), channel_id=1, source_target_pairs={{0,16},{8,24},{16,0},{24,8},{1,17},{9,25},{17,1},{25,9},{2,18},{10... | collective-permute-start | bytes 786440 | tf_op jit(solution)/shard_map/ppermute | solution.py:417
  151.1 2.0 %collective-permute-start.30 = (bf16[2,32,4096]{2,1,0:T(8,128)(2,1)S(1)}, bf16[2,32,4096]{2,1,0:T(8,128)(2,1)S(1)}, u32[]{:S(2)}, u32[]{:S(2)}) collective-permute-start(bf16[2,32,4096]{2,1,0:T(8,128)(2,1)S(1)} %join.2), channel_id=1, source_target_pairs={{0,8},{8,0},{16,24},{24,16},{1,9},{9,1},{17,25},{25,17},{2,10},{10... | collective-permute-start | bytes 1572872 | tf_op jit(solution)/shard_map/ppermute | solution.py:417
  151.1 8.0 %collective-permute-start.28 = (bf16[1,4,32,896]{3,2,1,0:T(8,128)(2,1)S(1)}, bf16[1,4,32,896]{3,2,1,0:T(8,128)(2,1)S(1)}, u32[]{:S(2)}, u32[]{:S(2)}) collective-permute-start(bf16[1,4,32,896]{3,2,1,0:T(8,128)(2,1)S(1)} %bitcast.39), channel_id=1, source_target_pairs={{0,16},{8,24},{16,0},{24,8},{1,17},{9,25},{17,1},{25,9},{2,18},{10... | collective-permute-start | bytes 688136 | tf_op jit(solution)/shard_map/ppermute | solution.py:417
  159.2 1.9 %collective-permute-start.31 = (bf16[2,4,32,896]{3,2,1,0:T(8,128)(2,1)S(1)}, bf16[2,4,32,896]{3,2,1,0:T(8,128)(2,1)S(1)}, u32[]{:S(2)}, u32[]{:S(2)}) collective-permute-start(bf16[2,4,32,896]{3,2,1,0:T(8,128)(2,1)S(1)} %join.3), channel_id=1, source_target_pairs={{0,8},{8,0},{16,24},{24,16},{1,9},{9,1},{17,25},{25,17},{2,10},{10... | collective-permute-start | bytes 1376264 | tf_op jit(solution)/shard_map/ppermute | solution.py:417
  161.6 6.9 %collective-permute-start.34 = (f32[128,128]{1,0:T(8,128)S(1)}, f32[128,128]{1,0:T(8,128)S(1)}, u32[]{:S(2)}, u32[]{:S(2)}) collective-permute-start(f32[128,128]{1,0:T(8,128)S(1)} %get-tuple-element.34.refs_0_), channel_id=1, source_target_pairs={{0,6},{1,7},{2,4},{3,5},{4,2},{5,3},{6,0},{7,1},{8,14},{9,15},{10,... | collective-permute-start | bytes 196616 | tf_op jit(solution)/shard_map/ppermute | solution.py:417
  162.9 7.5 %collective-permute-start.33 = (f32[128,128]{1,0:T(8,128)S(1)}, f32[128,128]{1,0:T(8,128)S(1)}, u32[]{:S(2)}, u32[]{:S(2)}) collective-permute-start(f32[128,128]{1,0:T(8,128)S(1)} %get-tuple-element.34.refs_0_), channel_id=1, source_target_pairs={{0,4},{1,5},{2,6},{3,7},{4,0},{5,1},{6,2},{7,3},{8,12},{9,13},{10,... | collective-permute-start | bytes 196616 | tf_op jit(solution)/shard_map/ppermute | solution.py:417
  163.3 7.1 %collective-permute-start.32 = (f32[128,128]{1,0:T(8,128)S(1)}, f32[128,128]{1,0:T(8,128)S(1)}, u32[]{:S(2)}, u32[]{:S(2)}) collective-permute-start(f32[128,128]{1,0:T(8,128)S(1)} %get-tuple-element.34.refs_0_), channel_id=1, source_target_pairs={{0,2},{1,3},{2,0},{3,1},{4,6},{5,7},{6,4},{7,5},{8,10},{9,11},{10,... | collective-permute-start | bytes 196616 | tf_op jit(solution)/shard_map/ppermute | solution.py:417
  170.4 4.3 %collective-permute-start.35 = (f32[128,128]{1,0:T(8,128)S(1)}, f32[128,128]{1,0:T(8,128)S(1)}, u32[]{:S(2)}, u32[]{:S(2)}) collective-permute-start(f32[128,128]{1,0:T(8,128)S(1)} %add.1.one_ref), channel_id=1, source_target_pairs={{0,1},{1,0},{2,3},{3,2},{4,5},{5,4},{6,7},{7,6},{8,9},{9,8},{10,11... | collective-permute-start | bytes 196616 | tf_op jit(solution)/shard_map/ppermute | solution.py:417

commit v3 on v2

--- a/solution.py
+++ b/solution.py
@@ -186,11 +186,20 @@
     )[0]
 
 
+def far_kernel(_, *refs):
+    *in_refs, out_ref = refs
+    rank = out_ref.shape[0]
+    out_ref[:, :rank] = tree_sum([from_pieces(ref[:, :LANES]) for ref in in_refs])
+    out_ref[:, LANES:] = tree_sum([ref[:, LANES:].astype(F32) for ref in in_refs])
+
+
 def combine_kernel(_, *refs):
-    *in_refs, out_ref = refs
-    gram = tree_sum([from_pieces(ref[:, :LANES]) for ref in in_refs])
+    *in_refs, far_ref, out_ref = refs
+    rank = out_ref.shape[0]
+    gram = tree_sum([from_pieces(ref[:, :LANES]) for ref in in_refs]) + far_ref[:, :rank]
+    total = tree_sum([ref[:, LANES:].astype(F32) for ref in in_refs]) + far_ref[:, LANES:]
     out_ref[:, :LANES] = with_pieces(gram)
-    out_ref[:, LANES:] = tree_sum([ref[:, LANES:].astype(F32) for ref in in_refs]).astype(BF16)
+    out_ref[:, LANES:] = total.astype(BF16)
 
 
 def settle_kernel(_, one_ref, other_ref, out_ref):
@@ -201,7 +210,9 @@
 
 
 def combine(held, pieces):
-    return call(combine_kernel, "combine", pieces, [shape_of(pieces[0].shape, BF16)], held=held)[0]
+    near, far = pieces[: len(pieces) // 2], pieces[len(pieces) // 2 :]
+    (far,) = call(far_kernel, "far", far, [shape_of(far[0].shape, F32)], held=held)
+    return call(combine_kernel, "combine", [*near, far], [shape_of(near[0].shape, BF16)], held=held)[0]
 
 
 def settle(held, one, other):
@@ -319,17 +330,20 @@
 
 
 def root_begin(gram):
-    return gram / jnp.sqrt(jnp.sum(gram * gram)), eye_of(gram.shape[0]).astype(F32)
+    upper = gram / jnp.sqrt(jnp.sum(gram * gram))
+    middle = 0.5 * (3.0 * eye_of(gram.shape[0]).astype(F32) - upper)
+    return square(upper, middle), middle
 
 
 def root_steps(state, count):
-    identity = eye_of(state[0].shape[0]).astype(F32)
+    size = state[0].shape[0]
+    identity = eye_of(size).astype(F32)
 
     def step(_, state):
         upper, lower = state
         middle = 0.5 * (3.0 * identity - square(lower, upper))
         both = square(middle, jnp.concatenate([upper, lower], axis=1))
-        return both[:, : identity.shape[0]], both[:, identity.shape[0] :]
+        return both[:, :size], both[:, size:]
 
     return lax.fori_loop(0, count, step, state)
 
@@ -339,7 +353,7 @@
 
 
 def right_first_kernel(groups, *refs):
-    in_refs, (wide_ref, lower_ref, gram_ref) = refs[: len(groups)], refs[-3:]
+    in_refs, (wide_ref, lower_ref, gram_ref, blocks) = refs[: len(groups)], refs[-4:]
     rank = in_refs[0].shape[1]
     for masks, in_ref in zip(groups, in_refs):
         for place, mask in enumerate(masks):
@@ -347,15 +361,24 @@
     wide = wide_ref[...]
     raw = lax.dot_general(wide, wide, ROWS_BY_ROWS, preferred_element_type=F32)
     spans = [slice(task * rank, (task + 1) * rank) for task in range(wide.shape[0] // rank)]
+    for task, span in enumerate(spans):
+        blocks[task] = raw[span, span]
+
+    def two(at, carry):
+        for task, inverse in enumerate(lower_inverse([blocks[2 * at], blocks[2 * at + 1]])):
+            blocks[2 * at + task] = inverse
+        return carry
+
+    lax.fori_loop(0, len(spans) // 2, two, 0)
     lower_ref[...] = jnp.zeros_like(lower_ref)
-    for span, inverse in zip(spans, lower_inverse([raw[span, span] for span in spans])):
-        lower_ref[span, span] = inverse
+    for task, span in enumerate(spans):
+        lower_ref[span, span] = blocks[task]
     lower = lower_ref[...]
     gram_ref[...] = square(square(lower, raw), lower.T)
 
 
 def right_begin_kernel(count, gram_ref, upper_ref, lower_ref):
-    upper_ref[...], lower_ref[...] = root_steps(root_begin(gram_ref[...]), count)
+    upper_ref[...], lower_ref[...] = root_steps(root_begin(gram_ref[...]), count - 1)
 
 
 def right_steps_kernel(count, upper_in, lower_in, upper_ref, lower_ref):
@@ -375,7 +398,7 @@
     down = jnp.sqrt(jnp.sum(diagonal, axis=1, keepdims=True))
     over = jnp.sqrt(jnp.sum(diagonal, axis=0, keepdims=True))
     normed = gram / (down * over)
-    mixing = root_end(root_steps(root_begin(normed), ROOT_STEPS), normed) / down * over
+    mixing = root_end(root_steps(root_begin(normed), ROOT_STEPS - 1), normed) / down * over
     mixed = square(square(lower.T, mixing), right_ref[...])
     panel = panel_ref[...].T
     product = jnp.dot(
@@ -472,6 +495,7 @@
         "right_first",
         bases,
         [shape_of((size, held.shape[1]), BF16), square_shape, square_shape],
+        [pltpu.VMEM((tasks, size // tasks, size // tasks), F32)],
     )
     begin, middle = ROOT_STEPS // 2, ROOT_STEPS // 6
     state = call(functools.partial(right_begin_kernel, begin), "right_begin", [right_gram], [square_shape] * 2)

time: 185 us -> 182 us (0.984)
  waiting for transfers between devices: 34 us -> 31.6 us
    ppermute x36, waiting for transfers between devices: 34 us -> 31.6 us  [send(): return lax.ppermute(piece, axis, [(at, at ^ mask) for at in range(count)])]
    pallas_call x42 -> x46, Pallas kernels: 81.1 us -> 81.2 us  [call(): pl.pallas_call(kernel, out_shape=tuple(shapes), in_specs=specs, out_specs...]
  transfers between devices with their start and end apart: 36 -> 36, of which waited for: 26 -> 24; matrix products, arithmetic and copies ran while one was open for 0% -> 0% of each run, Pallas kernels for 23% -> 26%
where the time goes in v3:
time: 182 us
  Pallas kernels  90.4 us (50%)
  starting transfers between devices  49.2 us (27%)
  waiting for transfers between devices  31.6 us (17%)
  local copies, waits for them, and re-layouts  10.4 us (6%)
    pallas_call x46, Pallas kernels, call(): pl.pallas_call(kernel, out_shape=tuple(shapes), in_specs=specs, out_specs...  81.2 us
    ppermute x36, starting transfers between devices, send(): return lax.ppermute(piece, axis, [(at, at ^ mask) for at in range(count)])  49.2 us
    ppermute x36, waiting for transfers between devices, send(): return lax.ppermute(piece, axis, [(at, at ^ mask) for at in range(count)])  31.6 us
    unnamed x4, local copies, waits for them, and re-layouts  10.4 us
    pallas_call x1, Pallas kernels, finish(): pl.pallas_call(functools.partial(finish_kernel, across), out_shape=shape_...  9.2 us
  transfers between devices with their start and end apart: 36, of which 24 were waited for; matrix products, arithmetic and copies ran while one was open for 0% of the time, Pallas kernels for 26%

profile of v3, /device:TPU:0, one launch (start us, length us, event | category | flops | bytes accessed | tf_op | source)
XLA Modules:
  0.0 182.1 jit_solution(2225645718186576459)
XLA Ops:
  0.0 9.3 %copy-done = bf16[1,3584,4096]{2,1,0:T(8,128)(2,1)S(1)} copy-done((bf16[1,3584,4096]{2,1,0:T(8,128)(2,1)S(1)}, bf16[1,3584,4096]{2,1,0:T(8,128)(2,1)}, u32[]{:S(2)}) %copy-start) | copy-done | bytes 29360152
  10.4 8.3 %first.1 = (bf16[32,3584]{1,0:T(8,128)(2,1)S(1)}, bf16[32,128]{1,0:T(8,128)(2,1)S(1)}) custom-call(bf16[3584,4096]{1,0:T(8,128)(2,1)S(1)} %bitcast.5, f32[32,4096]{1,0:T(8,128)S(1)} %bitcast.46), custom_call_target="tpu_custom_call" | custom-call | flops 11274289152 | bytes 1000000 | tf_op jit(solution)/shard_map/first/pallas_call | solution.py:31
  18.7 1.4 backs.16.refs_0_
  20.1 5.1 %collective-permute-start = (bf16[32,1152]{1,0:T(8,128)(2,1)S(1)}, bf16[32,1152]{1,0:T(8,128)(2,1)S(1)}, u32[]{:S(2)}, u32[]{:S(2)}) collective-permute-start(bf16[32,1152]{1,0:T(8,128)(2,1)S(1)} %backs.16.refs_0_), channel_id=1, source_target_pairs={{0,6},{1,7},{2,4},{3,5},{4,2},{5,3},{6,0},{7,1},{8,14},{9,15},{10,... | collective-permute-start | bytes 221192 | tf_op jit(solution)/shard_map/ppermute | solution.py:440
  25.1 1.3 backs.17.refs_0_
  26.5 1.4 backs.18.refs_0_
  28.4 1.3 backs.19.refs_0_
  29.8 2.2 %collective-permute-done.2.refs_0_ = bf16[32,1152]{1,0:T(8,128)(2,1)S(1)} collective-permute-done((bf16[32,1152]{1,0:T(8,128)(2,1)S(1)}, bf16[32,1152]{1,0:T(8,128)(2,1)S(1)}, u32[]{:S(2)}, u32[]{:S(2)}) %collective-permute-start.2) | collective-permute-done | bytes 73760 | tf_op jit(solution)/shard_map/ppermute | solution.py:440
  32.9 1.5 collective-permute-start.3
  34.4 2.8 %collective-permute-done.3.other_ref = bf16[32,1152]{1,0:T(8,128)(2,1)S(1)} collective-permute-done((bf16[32,1152]{1,0:T(8,128)(2,1)S(1)}, bf16[32,1152]{1,0:T(8,128)(2,1)S(1)}, u32[]{:S(2)}, u32[]{:S(2)}) %collective-permute-start.3) | collective-permute-done | bytes 73760 | tf_op jit(solution)/shard_map/ppermute | solution.py:440
  38.3 3.8 %collective-permute-start.5 = (bf16[32,1024]{1,0:T(8,128)(2,1)S(1)}, bf16[32,1024]{1,0:T(8,128)(2,1)S(1)}, u32[]{:S(2)}, u32[]{:S(2)}) collective-permute-start(bf16[32,1024]{1,0:T(8,128)(2,1)S(1)} %settle.4.refs_0_), channel_id=1, source_target_pairs={{0,6},{1,7},{2,4},{3,5},{4,2},{5,3},{6,0},{7,1},{8,14},{9,15},{10,... | collective-permute-start | bytes 196616 | tf_op jit(solution)/shard_map/ppermute | solution.py:440
  42.8 4.6 %images.8.refs_2_ = f32[32,3584]{1,0:T(8,128)S(1)} custom-call(bf16[3584,4096]{1,0:T(8,128)(2,1)S(1)} %bitcast.13, bf16[32,1024]{1,0:T(8,128)(2,1)S(1)} %settle.4.refs_0_, bf16[32,1024]{1,0:T(8,128)(2,1)S(1)} %collective-permute-done.6.refs_1_), custom_call_target="tpu_custom_call" | custom-call | flops 5637144576 | bytes 1000000 | tf_op jit(solution)/shard_map/images/pallas_call | solution.py:31
  47.4 5.0 %images.9 = (bf16[32,3584]{1,0:T(8,128)(2,1)S(1)}, bf16[32,128]{1,0:T(8,128)(2,1)S(1)}) custom-call(bf16[3584,4096]{1,0:T(8,128)(2,1)S(1)} %bitcast.14, bf16[32,1024]{1,0:T(8,128)(2,1)S(1)} %collective-permute-done.4.refs_0_, bf16[32,1024]{1,0:T(8,128)(2,1)S(1)} %collective-permute-done.5.refs_1_, f32[32,3584]{1,0:T(8,128)S(1)} %images.8.refs_2_), custom_call_target="tpu_custom_call" | custom-call | flops 5637144576 | bytes 1000000 | tf_op jit(solution)/shard_map/images/pallas_call | solution.py:31
  52.4 1.4 backs.20.refs_0_
  53.8 2.8 %collective-permute-start.7 = (bf16[32,1152]{1,0:T(8,128)(2,1)S(1)}, bf16[32,1152]{1,0:T(8,128)(2,1)S(1)}, u32[]{:S(2)}, u32[]{:S(2)}) collective-permute-start(bf16[32,1152]{1,0:T(8,128)(2,1)S(1)} %backs.20.refs_0_), channel_id=1, source_target_pairs={{0,6},{1,7},{2,4},{3,5},{4,2},{5,3},{6,0},{7,1},{8,14},{9,15},{10,... | collective-permute-start | bytes 221192 | tf_op jit(solution)/shard_map/ppermute | solution.py:440
  56.6 1.3 backs.21.refs_0_
  58.0 1.4 backs.22.refs_0_
  59.3 1.6 collective-permute-start.8
  60.9 1.3 backs.23.refs_0_
  62.3 1.2 collective-permute-done.9.refs_0_
  64.4 1.5 collective-permute-start.10
  65.9 2.8 %collective-permute-done.10.other_ref = bf16[32,1152]{1,0:T(8,128)(2,1)S(1)} collective-permute-done((bf16[32,1152]{1,0:T(8,128)(2,1)S(1)}, bf16[32,1152]{1,0:T(8,128)(2,1)S(1)}, u32[]{:S(2)}, u32[]{:S(2)}) %collective-permute-start.10) | collective-permute-done | bytes 73760 | tf_op jit(solution)/shard_map/ppermute | solution.py:440
  69.7 1.1 collective-permute-start.13
  70.8 2.8 %collective-permute-start.12 = (bf16[32,1024]{1,0:T(8,128)(2,1)S(1)}, bf16[32,1024]{1,0:T(8,128)(2,1)S(1)}, u32[]{:S(2)}, u32[]{:S(2)}) collective-permute-start(bf16[32,1024]{1,0:T(8,128)(2,1)S(1)} %settle.5.refs_0_), channel_id=1, source_target_pairs={{0,6},{1,7},{2,4},{3,5},{4,2},{5,3},{6,0},{7,1},{8,14},{9,15},{10,... | collective-permute-start | bytes 196616 | tf_op jit(solution)/shard_map/ppermute | solution.py:440
  74.1 4.6 %images.10.refs_2_ = f32[32,3584]{1,0:T(8,128)S(1)} custom-call(bf16[3584,4096]{1,0:T(8,128)(2,1)S(1)} %bitcast.22, bf16[32,1024]{1,0:T(8,128)(2,1)S(1)} %settle.5.refs_0_, bf16[32,1024]{1,0:T(8,128)(2,1)S(1)} %collective-permute-done.13.refs_1_), custom_call_target="tpu_custom_call" | custom-call | flops 5637144576 | bytes 1000000 | tf_op jit(solution)/shard_map/images/pallas_call | solution.py:31
  78.8 4.8 %images.11 = (bf16[32,3584]{1,0:T(8,128)(2,1)S(1)}, bf16[32,128]{1,0:T(8,128)(2,1)S(1)}) custom-call(bf16[3584,4096]{1,0:T(8,128)(2,1)S(1)} %bitcast.23, bf16[32,1024]{1,0:T(8,128)(2,1)S(1)} %collective-permute-done.11.refs_0_, bf16[32,1024]{1,0:T(8,128)(2,1)S(1)} %collective-permute-done.12.refs_1_, f32[32,3584]{1,0:T(8,128)S(1)} %images.10.refs_2_), custom_call_target="tpu_custom_call" | custom-call | flops 5637144576 | bytes 1000000 | tf_op jit(solution)/shard_map/images/pallas_call | solution.py:31
  83.7 1.4 backs.24.refs_0_
  85.0 2.3 %collective-permute-start.14 = (bf16[32,1152]{1,0:T(8,128)(2,1)S(1)}, bf16[32,1152]{1,0:T(8,128)(2,1)S(1)}, u32[]{:S(2)}, u32[]{:S(2)}) collective-permute-start(bf16[32,1152]{1,0:T(8,128)(2,1)S(1)} %backs.24.refs_0_), channel_id=1, source_target_pairs={{0,6},{1,7},{2,4},{3,5},{4,2},{5,3},{6,0},{7,1},{8,14},{9,15},{10,... | collective-permute-start | bytes 221192 | tf_op jit(solution)/shard_map/ppermute | solution.py:440
  87.3 1.3 backs.25.refs_0_
  88.9 1.3 backs.26.refs_0_
  90.2 2.0 %collective-permute-start.15 = (bf16[32,1152]{1,0:T(8,128)(2,1)S(1)}, bf16[32,1152]{1,0:T(8,128)(2,1)S(1)}, u32[]{:S(2)}, u32[]{:S(2)}) collective-permute-start(bf16[32,1152]{1,0:T(8,128)(2,1)S(1)} %backs.26.refs_0_), channel_id=1, source_target_pairs={{0,2},{1,3},{2,0},{3,1},{4,6},{5,7},{6,4},{7,5},{8,10},{9,11},{10,... | collective-permute-start | bytes 221192 | tf_op jit(solution)/shard_map/ppermute | solution.py:440
  92.2 1.3 backs.27.refs_0_
  93.5 1.4 collective-permute-done.16.refs_0_
  95.8 1.6 collective-permute-start.17
  97.3 2.8 %collective-permute-done.17.other_ref = bf16[32,1152]{1,0:T(8,128)(2,1)S(1)} collective-permute-done((bf16[32,1152]{1,0:T(8,128)(2,1)S(1)}, bf16[32,1152]{1,0:T(8,128)(2,1)S(1)}, u32[]{:S(2)}, u32[]{:S(2)}) %collective-permute-start.17) | collective-permute-done | bytes 73760 | tf_op jit(solution)/shard_map/ppermute | solution.py:440
  101.1 1.5 collective-permute-start.20
  102.7 1.7 collective-permute-start.19
  105.5 4.6 %images.12.refs_2_ = f32[32,3584]{1,0:T(8,128)S(1)} custom-call(bf16[3584,4096]{1,0:T(8,128)(2,1)S(1)} %bitcast.31, bf16[32,1024]{1,0:T(8,128)(2,1)S(1)} %settle.6.refs_0_, bf16[32,1024]{1,0:T(8,128)(2,1)S(1)} %collective-permute-done.20.refs_1_), custom_call_target="tpu_custom_call" | custom-call | flops 5637144576 | bytes 1000000 | tf_op jit(solution)/shard_map/images/pallas_call | solution.py:31
  110.1 5.0 %images.13 = (bf16[32,3584]{1,0:T(8,128)(2,1)S(1)}, bf16[32,128]{1,0:T(8,128)(2,1)S(1)}) custom-call(bf16[3584,4096]{1,0:T(8,128)(2,1)S(1)} %bitcast.32, bf16[32,1024]{1,0:T(8,128)(2,1)S(1)} %collective-permute-done.18.refs_0_, bf16[32,1024]{1,0:T(8,128)(2,1)S(1)} %collective-permute-done.19.refs_1_, f32[32,3584]{1,0:T(8,128)S(1)} %images.12.refs_2_), custom_call_target="tpu_custom_call" | custom-call | flops 5637144576 | bytes 1000000 | tf_op jit(solution)/shard_map/images/pallas_call | solution.py:31
  115.1 1.4 backs.28.refs_0_
  116.5 2.0 %collective-permute-start.21 = (bf16[32,1152]{1,0:T(8,128)(2,1)S(1)}, bf16[32,1152]{1,0:T(8,128)(2,1)S(1)}, u32[]{:S(2)}, u32[]{:S(2)}) collective-permute-start(bf16[32,1152]{1,0:T(8,128)(2,1)S(1)} %backs.28.refs_0_), channel_id=1, source_target_pairs={{0,6},{1,7},{2,4},{3,5},{4,2},{5,3},{6,0},{7,1},{8,14},{9,15},{10,... | collective-permute-start | bytes 221192 | tf_op jit(solution)/shard_map/ppermute | solution.py:440
  118.5 1.3 backs.29.refs_0_
  119.8 1.1 collective-permute-start.23
  120.9 1.3 backs.30.refs_0_
  122.2 1.4 collective-permute-start.22
  123.6 1.3 backs.31.refs_0_
  124.9 3.0 %collective-permute-done.23.refs_0_ = bf16[32,1152]{1,0:T(8,128)(2,1)S(1)} collective-permute-done((bf16[32,1152]{1,0:T(8,128)(2,1)S(1)}, bf16[32,1152]{1,0:T(8,128)(2,1)S(1)}, u32[]{:S(2)}, u32[]{:S(2)}) %collective-permute-start.23) | collective-permute-done | bytes 73760 | tf_op jit(solution)/shard_map/ppermute | solution.py:440
  128.2 1.5 collective-permute-start.24
  129.7 2.9 %collective-permute-done.24.other_ref = bf16[32,1152]{1,0:T(8,128)(2,1)S(1)} collective-permute-done((bf16[32,1152]{1,0:T(8,128)(2,1)S(1)}, bf16[32,1152]{1,0:T(8,128)(2,1)S(1)}, u32[]{:S(2)}, u32[]{:S(2)}) %collective-permute-start.24) | collective-permute-done | bytes 73760 | tf_op jit(solution)/shard_map/ppermute | solution.py:440
  133.6 1.9 %collective-permute-start.26 = (bf16[32,1024]{1,0:T(8,128)(2,1)S(1)}, bf16[32,1024]{1,0:T(8,128)(2,1)S(1)}, u32[]{:S(2)}, u32[]{:S(2)}) collective-permute-start(bf16[32,1024]{1,0:T(8,128)(2,1)S(1)} %settle.7.refs_0_), channel_id=1, source_target_pairs={{0,6},{1,7},{2,4},{3,5},{4,2},{5,3},{6,0},{7,1},{8,14},{9,15},{10,... | collective-permute-start | bytes 196616 | tf_op jit(solution)/shard_map/ppermute | solution.py:440
  135.5 1.6 collective-permute-start.25
  137.9 4.6 %images.14.refs_2_.refs_4_ = f32[32,3584]{1,0:T(8,128)S(1)} custom-call(bf16[3584,4096]{1,0:T(8,128)(2,1)S(1)} %bitcast.40, bf16[32,1024]{1,0:T(8,128)(2,1)S(1)} %settle.7.refs_0_, bf16[32,1024]{1,0:T(8,128)(2,1)S(1)} %collective-permute-done.27.refs_1_), custom_call_target="tpu_custom_call" | custom-call | flops 5637144576 | bytes 1000000 | tf_op jit(solution)/shard_map/images/pallas_call | solution.py:31
  142.5 1.5 collective-permute-start.29
  144.0 4.6 %images.15.refs_2_ = bf16[4,32,896]{2,1,0:T(8,128)(2,1)S(1)} custom-call(bf16[3584,4096]{1,0:T(8,128)(2,1)S(1)} %bitcast.42, bf16[32,1024]{1,0:T(8,128)(2,1)S(1)} %collective-permute-done.25.refs_0_.refs_2_, bf16[32,1024]{1,0:T(8,128)(2,1)S(1)} %collective-permute-done.26.refs_1_.refs_3_, f32[32,3584]{1,0:T(8,128)S(1)} %images.14.refs_2_.refs_4_), custom_call_target="tpu_custom_call" | custom-call | flops 5637144576 | bytes 1000000 | tf_op jit(solution)/shard_map/images/pallas_call | solution.py:31
  149.1 1.5 collective-permute-start.28
  151.0 2.9 %right_first.1 = (bf16[128,4096]{1,0:T(8,128)(2,1)S(1)}, f32[128,128]{1,0:T(8,128)S(1)}, f32[128,128]{1,0:T(8,128)S(1)}) custom-call(bf16[1,32,4096]{2,1,0:T(8,128)(2,1)S(1)} %pack.1.refs_0_, bf16[1,32,4096]{2,1,0:T(8,128)(2,1)S(1)} %collective-permute-done.29.refs_1_, bf16[2,32,4096]{2,1,0:T(8,128)(2,1)S(1)} %collective-permute-done.30.refs_2_), custom_call_target="tpu_custom_call" | custom-call | flops 100000000 | bytes 1000000 | tf_op jit(solution)/shard_map/right_first/pallas_call | solution.py:31
  153.9 2.4 %right_begin.1 = (f32[128,128]{1,0:T(8,128)S(1)}, f32[128,128]{1,0:T(8,128)S(1)}) custom-call(f32[128,128]{1,0:T(8,128)S(1)} %get-tuple-element.30.gram_ref), custom_call_target="tpu_custom_call" | custom-call | flops 100000000 | bytes 1000000 | tf_op jit(solution)/shard_map/right_begin/pallas_call | solution.py:31
  159.5 1.8 %collective-permute-start.34 = (f32[128,128]{1,0:T(8,128)S(1)}, f32[128,128]{1,0:T(8,128)S(1)}, u32[]{:S(2)}, u32[]{:S(2)}) collective-permute-start(f32[128,128]{1,0:T(8,128)S(1)} %get-tuple-element.34.refs_0_), channel_id=1, source_target_pairs={{0,6},{1,7},{2,4},{3,5},{4,2},{5,3},{6,0},{7,1},{8,14},{9,15},{10,... | collective-permute-start | bytes 196616 | tf_op jit(solution)/shard_map/ppermute | solution.py:440
  161.3 2.6 %collective-permute-start.32 = (f32[128,128]{1,0:T(8,128)S(1)}, f32[128,128]{1,0:T(8,128)S(1)}, u32[]{:S(2)}, u32[]{:S(2)}) collective-permute-start(f32[128,128]{1,0:T(8,128)S(1)} %get-tuple-element.34.refs_0_), channel_id=1, source_target_pairs={{0,2},{1,3},{2,0},{3,1},{4,6},{5,7},{6,4},{7,5},{8,10},{9,11},{10,... | collective-permute-start | bytes 196616 | tf_op jit(solution)/shard_map/ppermute | solution.py:440
  164.0 2.1 %right_end.1.refs_4_.right_ref = f32[128,128]{1,0:T(8,128)S(1)} custom-call(f32[128,128]{1,0:T(8,128)S(1)} %get-tuple-element.30.gram_ref, f32[128,128]{1,0:T(8,128)S(1)} %get-tuple-element.33.refs_3_.upper_ref, f32[128,128]{1,0:T(8,128)S(1)} %get-tuple-element.35.lower_ref, f32[128,128]{1,0:T(8,128)S(1)} %get-tuple-element.36.change_ref.lower_ref, ...), custom_call_target="tpu_custom_call" | custom-call | flops 100000000 | bytes 1000000 | tf_op jit(solution)/shard_map/right_end/pallas_call | solution.py:31
  166.3 2.0 %collective-permute-done.33.refs_2_ = f32[128,128]{1,0:T(8,128)S(1)} collective-permute-done((f32[128,128]{1,0:T(8,128)S(1)}, f32[128,128]{1,0:T(8,128)S(1)}, u32[]{:S(2)}, u32[]{:S(2)}) %collective-permute-start.33) | collective-permute-done | bytes 65568 | tf_op jit(solution)/shard_map/ppermute | solution.py:440
  168.3 1.6 collective-permute-start.35
  169.9 2.8 %collective-permute-done.35.other_ref = f32[128,128]{1,0:T(8,128)S(1)} collective-permute-done((f32[128,128]{1,0:T(8,128)S(1)}, f32[128,128]{1,0:T(8,128)S(1)}, u32[]{:S(2)}, u32[]{:S(2)}) %collective-permute-start.35) | collective-permute-done | bytes 65568 | tf_op jit(solution)/shard_map/ppermute | solution.py:440
  172.7 9.2 %finish.1 = bf16[896,4096]{1,0:T(8,128)(2,1)} custom-call(f32[128,128]{1,0:T(8,128)S(1)} %add.1.one_ref, f32[128,128]{1,0:T(8,128)S(1)} %collective-permute-done.35.other_ref, bf16[128,896]{1,0:T(8,128)(2,1)S(1)} %get-tuple-element.37.panel_ref, bf16[128,4096]{1,0:T(8,128)(2,1)S(1)} %get-tuple-element.38.wide_ref, ...), custom_call_target="tpu_custom_call" | custom-call | tf_op jit(solution)/shard_map/finish/pallas_call | solution.py:425
  (59 shorter events, 16.4 us)
Async XLA Ops:
  0.0 9.4 %copy-start = (bf16[1,3584,4096]{2,1,0:T(8,128)(2,1)S(1)}, bf16[1,3584,4096]{2,1,0:T(8,128)(2,1)}, u32[]{:S(2)}) copy-start(bf16[1,3584,4096]{2,1,0:T(8,128)(2,1)} %param.2) | copy-start | bytes 88080384
  9.4 1.0 copy-start.1
  20.1 8.4 %collective-permute-start = (bf16[32,1152]{1,0:T(8,128)(2,1)S(1)}, bf16[32,1152]{1,0:T(8,128)(2,1)S(1)}, u32[]{:S(2)}, u32[]{:S(2)}) collective-permute-start(bf16[32,1152]{1,0:T(8,128)(2,1)S(1)} %backs.16.refs_0_), channel_id=1, source_target_pairs={{0,6},{1,7},{2,4},{3,5},{4,2},{5,3},{6,0},{7,1},{8,14},{9,15},{10,... | collective-permute-start | bytes 221192 | tf_op jit(solution)/shard_map/ppermute | solution.py:440
  26.5 5.5 %collective-permute-start.2 = (bf16[32,1152]{1,0:T(8,128)(2,1)S(1)}, bf16[32,1152]{1,0:T(8,128)(2,1)S(1)}, u32[]{:S(2)}, u32[]{:S(2)}) collective-permute-start(bf16[32,1152]{1,0:T(8,128)(2,1)S(1)} %backs.17.refs_0_), channel_id=1, source_target_pairs={{0,4},{1,5},{2,6},{3,7},{4,0},{5,1},{6,2},{7,3},{8,12},{9,13},{10,... | collective-permute-start | bytes 221192 | tf_op jit(solution)/shard_map/ppermute | solution.py:440
  27.8 4.9 %collective-permute-start.1 = (bf16[32,1152]{1,0:T(8,128)(2,1)S(1)}, bf16[32,1152]{1,0:T(8,128)(2,1)S(1)}, u32[]{:S(2)}, u32[]{:S(2)}) collective-permute-start(bf16[32,1152]{1,0:T(8,128)(2,1)S(1)} %backs.18.refs_0_), channel_id=1, source_target_pairs={{0,2},{1,3},{2,0},{3,1},{4,6},{5,7},{6,4},{7,5},{8,10},{9,11},{10,... | collective-permute-start | bytes 221192 | tf_op jit(solution)/shard_map/ppermute | solution.py:440
  32.9 4.4 %collective-permute-start.3 = (bf16[32,1152]{1,0:T(8,128)(2,1)S(1)}, bf16[32,1152]{1,0:T(8,128)(2,1)S(1)}, u32[]{:S(2)}, u32[]{:S(2)}) collective-permute-start(bf16[32,1152]{1,0:T(8,128)(2,1)S(1)} %combine.4.one_ref), channel_id=1, source_target_pairs={{0,1},{1,0},{2,3},{3,2},{4,5},{5,4},{6,7},{7,6},{8,9},{9,8},{10,11... | collective-permute-start | bytes 221192 | tf_op jit(solution)/shard_map/ppermute | solution.py:440
  38.2 4.6 %collective-permute-start.6 = (bf16[32,1024]{1,0:T(8,128)(2,1)S(1)}, bf16[32,1024]{1,0:T(8,128)(2,1)S(1)}, u32[]{:S(2)}, u32[]{:S(2)}) collective-permute-start(bf16[32,1024]{1,0:T(8,128)(2,1)S(1)} %settle.4.refs_0_), channel_id=1, source_target_pairs={{0,2},{1,3},{2,0},{3,1},{4,6},{5,7},{6,4},{7,5},{8,10},{9,11},{10,... | collective-permute-start | bytes 196616 | tf_op jit(solution)/shard_map/ppermute | solution.py:440
  38.3 9.1 %collective-permute-start.5 = (bf16[32,1024]{1,0:T(8,128)(2,1)S(1)}, bf16[32,1024]{1,0:T(8,128)(2,1)S(1)}, u32[]{:S(2)}, u32[]{:S(2)}) collective-permute-start(bf16[32,1024]{1,0:T(8,128)(2,1)S(1)} %settle.4.refs_0_), channel_id=1, source_target_pairs={{0,6},{1,7},{2,4},{3,5},{4,2},{5,3},{6,0},{7,1},{8,14},{9,15},{10,... | collective-permute-start | bytes 196616 | tf_op jit(solution)/shard_map/ppermute | solution.py:440
  42.2 5.3 %collective-permute-start.4 = (bf16[32,1024]{1,0:T(8,128)(2,1)S(1)}, bf16[32,1024]{1,0:T(8,128)(2,1)S(1)}, u32[]{:S(2)}, u32[]{:S(2)}) collective-permute-start(bf16[32,1024]{1,0:T(8,128)(2,1)S(1)} %settle.4.refs_0_), channel_id=1, source_target_pairs={{0,4},{1,5},{2,6},{3,7},{4,0},{5,1},{6,2},{7,3},{8,12},{9,13},{10,... | collective-permute-start | bytes 196616 | tf_op jit(solution)/shard_map/ppermute | solution.py:440
  53.8 7.1 %collective-permute-start.7 = (bf16[32,1152]{1,0:T(8,128)(2,1)S(1)}, bf16[32,1152]{1,0:T(8,128)(2,1)S(1)}, u32[]{:S(2)}, u32[]{:S(2)}) collective-permute-start(bf16[32,1152]{1,0:T(8,128)(2,1)S(1)} %backs.20.refs_0_), channel_id=1, source_target_pairs={{0,6},{1,7},{2,4},{3,5},{4,2},{5,3},{6,0},{7,1},{8,14},{9,15},{10,... | collective-permute-start | bytes 221192 | tf_op jit(solution)/shard_map/ppermute | solution.py:440
  58.0 5.5 %collective-permute-start.9 = (bf16[32,1152]{1,0:T(8,128)(2,1)S(1)}, bf16[32,1152]{1,0:T(8,128)(2,1)S(1)}, u32[]{:S(2)}, u32[]{:S(2)}) collective-permute-start(bf16[32,1152]{1,0:T(8,128)(2,1)S(1)} %backs.21.refs_0_), channel_id=1, source_target_pairs={{0,4},{1,5},{2,6},{3,7},{4,0},{5,1},{6,2},{7,3},{8,12},{9,13},{10,... | collective-permute-start | bytes 221192 | tf_op jit(solution)/shard_map/ppermute | solution.py:440
  59.3 4.9 %collective-permute-start.8 = (bf16[32,1152]{1,0:T(8,128)(2,1)S(1)}, bf16[32,1152]{1,0:T(8,128)(2,1)S(1)}, u32[]{:S(2)}, u32[]{:S(2)}) collective-permute-start(bf16[32,1152]{1,0:T(8,128)(2,1)S(1)} %backs.22.refs_0_), channel_id=1, source_target_pairs={{0,2},{1,3},{2,0},{3,1},{4,6},{5,7},{6,4},{7,5},{8,10},{9,11},{10,... | collective-permute-start | bytes 221192 | tf_op jit(solution)/shard_map/ppermute | solution.py:440
  64.4 4.4 %collective-permute-start.10 = (bf16[32,1152]{1,0:T(8,128)(2,1)S(1)}, bf16[32,1152]{1,0:T(8,128)(2,1)S(1)}, u32[]{:S(2)}, u32[]{:S(2)}) collective-permute-start(bf16[32,1152]{1,0:T(8,128)(2,1)S(1)} %combine.5.one_ref), channel_id=1, source_target_pairs={{0,1},{1,0},{2,3},{3,2},{4,5},{5,4},{6,7},{7,6},{8,9},{9,8},{10,11... | collective-permute-start | bytes 221192 | tf_op jit(solution)/shard_map/ppermute | solution.py:440
  69.7 4.3 %collective-permute-start.13 = (bf16[32,1024]{1,0:T(8,128)(2,1)S(1)}, bf16[32,1024]{1,0:T(8,128)(2,1)S(1)}, u32[]{:S(2)}, u32[]{:S(2)}) collective-permute-start(bf16[32,1024]{1,0:T(8,128)(2,1)S(1)} %settle.5.refs_0_), channel_id=1, source_target_pairs={{0,2},{1,3},{2,0},{3,1},{4,6},{5,7},{6,4},{7,5},{8,10},{9,11},{10,... | collective-permute-start | bytes 196616 | tf_op jit(solution)/shard_map/ppermute | solution.py:440
  70.8 7.8 %collective-permute-start.12 = (bf16[32,1024]{1,0:T(8,128)(2,1)S(1)}, bf16[32,1024]{1,0:T(8,128)(2,1)S(1)}, u32[]{:S(2)}, u32[]{:S(2)}) collective-permute-start(bf16[32,1024]{1,0:T(8,128)(2,1)S(1)} %settle.5.refs_0_), channel_id=1, source_target_pairs={{0,6},{1,7},{2,4},{3,5},{4,2},{5,3},{6,0},{7,1},{8,14},{9,15},{10,... | collective-permute-start | bytes 196616 | tf_op jit(solution)/shard_map/ppermute | solution.py:440
  73.7 5.2 %collective-permute-start.11 = (bf16[32,1024]{1,0:T(8,128)(2,1)S(1)}, bf16[32,1024]{1,0:T(8,128)(2,1)S(1)}, u32[]{:S(2)}, u32[]{:S(2)}) collective-permute-start(bf16[32,1024]{1,0:T(8,128)(2,1)S(1)} %settle.5.refs_0_), channel_id=1, source_target_pairs={{0,4},{1,5},{2,6},{3,7},{4,0},{5,1},{6,2},{7,3},{8,12},{9,13},{10,... | collective-permute-start | bytes 196616 | tf_op jit(solution)/shard_map/ppermute | solution.py:440
  85.0 7.1 %collective-permute-start.14 = (bf16[32,1152]{1,0:T(8,128)(2,1)S(1)}, bf16[32,1152]{1,0:T(8,128)(2,1)S(1)}, u32[]{:S(2)}, u32[]{:S(2)}) collective-permute-start(bf16[32,1152]{1,0:T(8,128)(2,1)S(1)} %backs.24.refs_0_), channel_id=1, source_target_pairs={{0,6},{1,7},{2,4},{3,5},{4,2},{5,3},{6,0},{7,1},{8,14},{9,15},{10,... | collective-permute-start | bytes 221192 | tf_op jit(solution)/shard_map/ppermute | solution.py:440
  88.7 6.2 %collective-permute-start.16 = (bf16[32,1152]{1,0:T(8,128)(2,1)S(1)}, bf16[32,1152]{1,0:T(8,128)(2,1)S(1)}, u32[]{:S(2)}, u32[]{:S(2)}) collective-permute-start(bf16[32,1152]{1,0:T(8,128)(2,1)S(1)} %backs.25.refs_0_), channel_id=1, source_target_pairs={{0,4},{1,5},{2,6},{3,7},{4,0},{5,1},{6,2},{7,3},{8,12},{9,13},{10,... | collective-permute-start | bytes 221192 | tf_op jit(solution)/shard_map/ppermute | solution.py:440
  90.2 5.4 %collective-permute-start.15 = (bf16[32,1152]{1,0:T(8,128)(2,1)S(1)}, bf16[32,1152]{1,0:T(8,128)(2,1)S(1)}, u32[]{:S(2)}, u32[]{:S(2)}) collective-permute-start(bf16[32,1152]{1,0:T(8,128)(2,1)S(1)} %backs.26.refs_0_), channel_id=1, source_target_pairs={{0,2},{1,3},{2,0},{3,1},{4,6},{5,7},{6,4},{7,5},{8,10},{9,11},{10,... | collective-permute-start | bytes 221192 | tf_op jit(solution)/shard_map/ppermute | solution.py:440
  95.8 4.4 %collective-permute-start.17 = (bf16[32,1152]{1,0:T(8,128)(2,1)S(1)}, bf16[32,1152]{1,0:T(8,128)(2,1)S(1)}, u32[]{:S(2)}, u32[]{:S(2)}) collective-permute-start(bf16[32,1152]{1,0:T(8,128)(2,1)S(1)} %combine.6.one_ref), channel_id=1, source_target_pairs={{0,1},{1,0},{2,3},{3,2},{4,5},{5,4},{6,7},{7,6},{8,9},{9,8},{10,11... | collective-permute-start | bytes 221192 | tf_op jit(solution)/shard_map/ppermute | solution.py:440
  101.1 4.3 %collective-permute-start.20 = (bf16[32,1024]{1,0:T(8,128)(2,1)S(1)}, bf16[32,1024]{1,0:T(8,128)(2,1)S(1)}, u32[]{:S(2)}, u32[]{:S(2)}) collective-permute-start(bf16[32,1024]{1,0:T(8,128)(2,1)S(1)} %settle.6.refs_0_), channel_id=1, source_target_pairs={{0,2},{1,3},{2,0},{3,1},{4,6},{5,7},{6,4},{7,5},{8,10},{9,11},{10,... | collective-permute-start | bytes 196616 | tf_op jit(solution)/shard_map/ppermute | solution.py:440
  102.7 7.4 %collective-permute-start.19 = (bf16[32,1024]{1,0:T(8,128)(2,1)S(1)}, bf16[32,1024]{1,0:T(8,128)(2,1)S(1)}, u32[]{:S(2)}, u32[]{:S(2)}) collective-permute-start(bf16[32,1024]{1,0:T(8,128)(2,1)S(1)} %settle.6.refs_0_), channel_id=1, source_target_pairs={{0,6},{1,7},{2,4},{3,5},{4,2},{5,3},{6,0},{7,1},{8,14},{9,15},{10,... | collective-permute-start | bytes 196616 | tf_op jit(solution)/shard_map/ppermute | solution.py:440
  104.4 5.7 %collective-permute-start.18 = (bf16[32,1024]{1,0:T(8,128)(2,1)S(1)}, bf16[32,1024]{1,0:T(8,128)(2,1)S(1)}, u32[]{:S(2)}, u32[]{:S(2)}) collective-permute-start(bf16[32,1024]{1,0:T(8,128)(2,1)S(1)} %settle.6.refs_0_), channel_id=1, source_target_pairs={{0,4},{1,5},{2,6},{3,7},{4,0},{5,1},{6,2},{7,3},{8,12},{9,13},{10,... | collective-permute-start | bytes 196616 | tf_op jit(solution)/shard_map/ppermute | solution.py:440
  116.5 7.1 %collective-permute-start.21 = (bf16[32,1152]{1,0:T(8,128)(2,1)S(1)}, bf16[32,1152]{1,0:T(8,128)(2,1)S(1)}, u32[]{:S(2)}, u32[]{:S(2)}) collective-permute-start(bf16[32,1152]{1,0:T(8,128)(2,1)S(1)} %backs.28.refs_0_), channel_id=1, source_target_pairs={{0,6},{1,7},{2,4},{3,5},{4,2},{5,3},{6,0},{7,1},{8,14},{9,15},{10,... | collective-permute-start | bytes 221192 | tf_op jit(solution)/shard_map/ppermute | solution.py:440
  119.8 8.2 %collective-permute-start.23 = (bf16[32,1152]{1,0:T(8,128)(2,1)S(1)}, bf16[32,1152]{1,0:T(8,128)(2,1)S(1)}, u32[]{:S(2)}, u32[]{:S(2)}) collective-permute-start(bf16[32,1152]{1,0:T(8,128)(2,1)S(1)} %backs.29.refs_0_), channel_id=1, source_target_pairs={{0,4},{1,5},{2,6},{3,7},{4,0},{5,1},{6,2},{7,3},{8,12},{9,13},{10,... | collective-permute-start | bytes 221192 | tf_op jit(solution)/shard_map/ppermute | solution.py:440
  122.2 5.8 %collective-permute-start.22 = (bf16[32,1152]{1,0:T(8,128)(2,1)S(1)}, bf16[32,1152]{1,0:T(8,128)(2,1)S(1)}, u32[]{:S(2)}, u32[]{:S(2)}) collective-permute-start(bf16[32,1152]{1,0:T(8,128)(2,1)S(1)} %backs.30.refs_0_), channel_id=1, source_target_pairs={{0,2},{1,3},{2,0},{3,1},{4,6},{5,7},{6,4},{7,5},{8,10},{9,11},{10,... | collective-permute-start | bytes 221192 | tf_op jit(solution)/shard_map/ppermute | solution.py:440
  128.2 4.4 %collective-permute-start.24 = (bf16[32,1152]{1,0:T(8,128)(2,1)S(1)}, bf16[32,1152]{1,0:T(8,128)(2,1)S(1)}, u32[]{:S(2)}, u32[]{:S(2)}) collective-permute-start(bf16[32,1152]{1,0:T(8,128)(2,1)S(1)} %combine.7.one_ref), channel_id=1, source_target_pairs={{0,1},{1,0},{2,3},{3,2},{4,5},{5,4},{6,7},{7,6},{8,9},{9,8},{10,11... | collective-permute-start | bytes 221192 | tf_op jit(solution)/shard_map/ppermute | solution.py:440
  133.6 4.3 %collective-permute-start.27 = (bf16[32,1024]{1,0:T(8,128)(2,1)S(1)}, bf16[32,1024]{1,0:T(8,128)(2,1)S(1)}, u32[]{:S(2)}, u32[]{:S(2)}) collective-permute-start(bf16[32,1024]{1,0:T(8,128)(2,1)S(1)} %settle.7.refs_0_), channel_id=1, source_target_pairs={{0,2},{1,3},{2,0},{3,1},{4,6},{5,7},{6,4},{7,5},{8,10},{9,11},{10,... | collective-permute-start | bytes 196616 | tf_op jit(solution)/shard_map/ppermute | solution.py:440
  133.6 8.8 %collective-permute-start.26 = (bf16[32,1024]{1,0:T(8,128)(2,1)S(1)}, bf16[32,1024]{1,0:T(8,128)(2,1)S(1)}, u32[]{:S(2)}, u32[]{:S(2)}) collective-permute-start(bf16[32,1024]{1,0:T(8,128)(2,1)S(1)} %settle.7.refs_0_), channel_id=1, source_target_pairs={{0,6},{1,7},{2,4},{3,5},{4,2},{5,3},{6,0},{7,1},{8,14},{9,15},{10,... | collective-permute-start | bytes 196616 | tf_op jit(solution)/shard_map/ppermute | solution.py:440
  135.5 7.0 %collective-permute-start.25 = (bf16[32,1024]{1,0:T(8,128)(2,1)S(1)}, bf16[32,1024]{1,0:T(8,128)(2,1)S(1)}, u32[]{:S(2)}, u32[]{:S(2)}) collective-permute-start(bf16[32,1024]{1,0:T(8,128)(2,1)S(1)} %settle.7.refs_0_), channel_id=1, source_target_pairs={{0,4},{1,5},{2,6},{3,7},{4,0},{5,1},{6,2},{7,3},{8,12},{9,13},{10,... | collective-permute-start | bytes 196616 | tf_op jit(solution)/shard_map/ppermute | solution.py:440
  142.5 6.4 %collective-permute-start.29 = (bf16[1,32,4096]{2,1,0:T(8,128)(2,1)S(1)}, bf16[1,32,4096]{2,1,0:T(8,128)(2,1)S(1)}, u32[]{:S(2)}, u32[]{:S(2)}) collective-permute-start(bf16[1,32,4096]{2,1,0:T(8,128)(2,1)S(1)} %pack.1.refs_0_), channel_id=1, source_target_pairs={{0,16},{8,24},{16,0},{24,8},{1,17},{9,25},{17,1},{25,9},{2,18},{10... | collective-permute-start | bytes 786440 | tf_op jit(solution)/shard_map/ppermute | solution.py:440
  149.0 2.0 %collective-permute-start.30 = (bf16[2,32,4096]{2,1,0:T(8,128)(2,1)S(1)}, bf16[2,32,4096]{2,1,0:T(8,128)(2,1)S(1)}, u32[]{:S(2)}, u32[]{:S(2)}) collective-permute-start(bf16[2,32,4096]{2,1,0:T(8,128)(2,1)S(1)} %join.2), channel_id=1, source_target_pairs={{0,8},{8,0},{16,24},{24,16},{1,9},{9,1},{17,25},{25,17},{2,10},{10... | collective-permute-start | bytes 1572872 | tf_op jit(solution)/shard_map/ppermute | solution.py:440
  149.1 8.0 %collective-permute-start.28 = (bf16[1,4,32,896]{3,2,1,0:T(8,128)(2,1)S(1)}, bf16[1,4,32,896]{3,2,1,0:T(8,128)(2,1)S(1)}, u32[]{:S(2)}, u32[]{:S(2)}) collective-permute-start(bf16[1,4,32,896]{3,2,1,0:T(8,128)(2,1)S(1)} %bitcast.43), channel_id=1, source_target_pairs={{0,16},{8,24},{16,0},{24,8},{1,17},{9,25},{17,1},{25,9},{2,18},{10... | collective-permute-start | bytes 688136 | tf_op jit(solution)/shard_map/ppermute | solution.py:440
  157.1 1.9 %collective-permute-start.31 = (bf16[2,4,32,896]{3,2,1,0:T(8,128)(2,1)S(1)}, bf16[2,4,32,896]{3,2,1,0:T(8,128)(2,1)S(1)}, u32[]{:S(2)}, u32[]{:S(2)}) collective-permute-start(bf16[2,4,32,896]{3,2,1,0:T(8,128)(2,1)S(1)} %join.3), channel_id=1, source_target_pairs={{0,8},{8,0},{16,24},{24,16},{1,9},{9,1},{17,25},{25,17},{2,10},{10... | collective-permute-start | bytes 1376264 | tf_op jit(solution)/shard_map/ppermute | solution.py:440
  159.5 6.8 %collective-permute-start.34 = (f32[128,128]{1,0:T(8,128)S(1)}, f32[128,128]{1,0:T(8,128)S(1)}, u32[]{:S(2)}, u32[]{:S(2)}) collective-permute-start(f32[128,128]{1,0:T(8,128)S(1)} %get-tuple-element.34.refs_0_), channel_id=1, source_target_pairs={{0,6},{1,7},{2,4},{3,5},{4,2},{5,3},{6,0},{7,1},{8,14},{9,15},{10,... | collective-permute-start | bytes 196616 | tf_op jit(solution)/shard_map/ppermute | solution.py:440
  161.3 7.0 %collective-permute-start.33 = (f32[128,128]{1,0:T(8,128)S(1)}, f32[128,128]{1,0:T(8,128)S(1)}, u32[]{:S(2)}, u32[]{:S(2)}) collective-permute-start(f32[128,128]{1,0:T(8,128)S(1)} %get-tuple-element.34.refs_0_), channel_id=1, source_target_pairs={{0,4},{1,5},{2,6},{3,7},{4,0},{5,1},{6,2},{7,3},{8,12},{9,13},{10,... | collective-permute-start | bytes 196616 | tf_op jit(solution)/shard_map/ppermute | solution.py:440
  161.3 7.0 %collective-permute-start.32 = (f32[128,128]{1,0:T(8,128)S(1)}, f32[128,128]{1,0:T(8,128)S(1)}, u32[]{:S(2)}, u32[]{:S(2)}) collective-permute-start(f32[128,128]{1,0:T(8,128)S(1)} %get-tuple-element.34.refs_0_), channel_id=1, source_target_pairs={{0,2},{1,3},{2,0},{3,1},{4,6},{5,7},{6,4},{7,5},{8,10},{9,11},{10,... | collective-permute-start | bytes 196616 | tf_op jit(solution)/shard_map/ppermute | solution.py:440
  168.3 4.3 %collective-permute-start.35 = (f32[128,128]{1,0:T(8,128)S(1)}, f32[128,128]{1,0:T(8,128)S(1)}, u32[]{:S(2)}, u32[]{:S(2)}) collective-permute-start(f32[128,128]{1,0:T(8,128)S(1)} %add.1.one_ref), channel_id=1, source_target_pairs={{0,1},{1,0},{2,3},{3,2},{4,5},{5,4},{6,7},{7,6},{8,9},{9,8},{10,11... | collective-permute-start | bytes 196616 | tf_op jit(solution)/shard_map/ppermute | solution.py:440

commit v4 on v3

--- a/solution.py
+++ b/solution.py
@@ -304,7 +304,11 @@
             for at in range(tasks):
                 whole[down, at * each : (at + 1) * each] = in_ref[place, at]
             panel_ref[down, :] = in_ref[place, partner("task", 0)]
-    gram_ref[...] = lax.dot_general(whole[...], whole[...], ROWS_BY_ROWS, preferred_element_type=F32)
+    gram = lax.dot_general(whole[...], whole[...], ROWS_BY_ROWS, preferred_element_type=F32)
+    half = gram.shape[0] // 2
+    gram_ref[:half] = gram[:half]
+    gram_ref[half:, :half] = gram[half : half + half // 2, half:]
+    gram_ref[half:, half:] = gram[half + half // 2 :, half:]
 
 
 def left(blocks, groups, after):
@@ -314,7 +318,7 @@
         functools.partial(left_kernel, groups),
         "left",
         blocks,
-        [shape_of((size, size), F32), shape_of((size, each), BF16)],
+        [shape_of((size // 4 * 3, size), F32), shape_of((size, each), BF16)],
         [pltpu.VMEM((size, tasks * each), BF16)],
         idle=[after],
     )
@@ -393,7 +397,12 @@
 def finish_kernel(across, one_ref, other_ref, panel_ref, wide_ref, lower_ref, right_ref, out_ref, made, sems):
     size, cols = wide_ref.shape
     lower = lower_ref[...]
-    gram = square(square(lower, one_ref[...] + other_ref[...]), lower.T)
+    packed = one_ref[...] + other_ref[...]
+    half = size // 2
+    corner = jnp.concatenate([packed[half:, :half], packed[half:, half:]], axis=0)
+    below = jnp.concatenate([packed[:half, half:].T, corner], axis=1)
+    raw = jnp.concatenate([packed[:half], below], axis=0)
+    gram = square(square(lower, raw), lower.T)
     diagonal = jnp.where(eye_of(size), gram, 0.0)
     down = jnp.sqrt(jnp.sum(diagonal, axis=1, keepdims=True))
     over = jnp.sqrt(jnp.sum(diagonal, axis=0, keepdims=True))

time: 182 us -> 181 us (level)
  transfers between devices with their start and end apart: 36 -> 36, of which waited for: 24 -> 23; matrix products, arithmetic and copies ran while one was open for 0% -> 0% of each run, Pallas kernels for 26% -> 26%
where the time goes in v4:
time: 181 us
  Pallas kernels  90.6 us (50%)
  starting transfers between devices  49.2 us (27%)
  waiting for transfers between devices  30.4 us (17%)
  local copies, waits for them, and re-layouts  10.4 us (6%)
    pallas_call x46, Pallas kernels, call(): pl.pallas_call(kernel, out_shape=tuple(shapes), in_specs=specs, out_specs...  81.3 us
    ppermute x36, starting transfers between devices, send(): return lax.ppermute(piece, axis, [(at, at ^ mask) for at in range(count)])  49.2 us
    ppermute x36, waiting for transfers between devices, send(): return lax.ppermute(piece, axis, [(at, at ^ mask) for at in range(count)])  30.4 us
    unnamed x4, local copies, waits for them, and re-layouts  10.4 us
    pallas_call x1, Pallas kernels, finish(): pl.pallas_call(functools.partial(finish_kernel, across), out_shape=shape_...  9.36 us
  transfers between devices with their start and end apart: 36, of which 23 were waited for; matrix products, arithmetic and copies ran while one was open for 0% of the time, Pallas kernels for 26%

profile of v4, /device:TPU:0, one launch (start us, length us, event | category | flops | bytes accessed | tf_op | source)
XLA Modules:
  0.0 181.0 jit_solution(11823449826495211509)
XLA Ops:
  0.0 9.3 %copy-done = bf16[1,3584,4096]{2,1,0:T(8,128)(2,1)S(1)} copy-done((bf16[1,3584,4096]{2,1,0:T(8,128)(2,1)S(1)}, bf16[1,3584,4096]{2,1,0:T(8,128)(2,1)}, u32[]{:S(2)}) %copy-start) | copy-done | bytes 29360152
  10.4 8.3 %first.1 = (bf16[32,3584]{1,0:T(8,128)(2,1)S(1)}, bf16[32,128]{1,0:T(8,128)(2,1)S(1)}) custom-call(bf16[3584,4096]{1,0:T(8,128)(2,1)S(1)} %bitcast.5, f32[32,4096]{1,0:T(8,128)S(1)} %bitcast.46), custom_call_target="tpu_custom_call" | custom-call | flops 11274289152 | bytes 1000000 | tf_op jit(solution)/shard_map/first/pallas_call | solution.py:31
  18.7 1.4 backs.16.refs_0_
  20.1 5.1 %collective-permute-start = (bf16[32,1152]{1,0:T(8,128)(2,1)S(1)}, bf16[32,1152]{1,0:T(8,128)(2,1)S(1)}, u32[]{:S(2)}, u32[]{:S(2)}) collective-permute-start(bf16[32,1152]{1,0:T(8,128)(2,1)S(1)} %backs.16.refs_0_), channel_id=1, source_target_pairs={{0,6},{1,7},{2,4},{3,5},{4,2},{5,3},{6,0},{7,1},{8,14},{9,15},{10,... | collective-permute-start | bytes 221192 | tf_op jit(solution)/shard_map/ppermute | solution.py:449
  25.1 1.3 backs.17.refs_0_
  26.5 1.4 backs.18.refs_0_
  28.4 1.3 backs.19.refs_0_
  29.8 2.2 %collective-permute-done.2.refs_0_ = bf16[32,1152]{1,0:T(8,128)(2,1)S(1)} collective-permute-done((bf16[32,1152]{1,0:T(8,128)(2,1)S(1)}, bf16[32,1152]{1,0:T(8,128)(2,1)S(1)}, u32[]{:S(2)}, u32[]{:S(2)}) %collective-permute-start.2) | collective-permute-done | bytes 73760 | tf_op jit(solution)/shard_map/ppermute | solution.py:449
  32.9 1.5 collective-permute-start.3
  34.4 2.8 %collective-permute-done.3.other_ref = bf16[32,1152]{1,0:T(8,128)(2,1)S(1)} collective-permute-done((bf16[32,1152]{1,0:T(8,128)(2,1)S(1)}, bf16[32,1152]{1,0:T(8,128)(2,1)S(1)}, u32[]{:S(2)}, u32[]{:S(2)}) %collective-permute-start.3) | collective-permute-done | bytes 73760 | tf_op jit(solution)/shard_map/ppermute | solution.py:449
  38.3 3.8 %collective-permute-start.5 = (bf16[32,1024]{1,0:T(8,128)(2,1)S(1)}, bf16[32,1024]{1,0:T(8,128)(2,1)S(1)}, u32[]{:S(2)}, u32[]{:S(2)}) collective-permute-start(bf16[32,1024]{1,0:T(8,128)(2,1)S(1)} %settle.4.refs_0_), channel_id=1, source_target_pairs={{0,6},{1,7},{2,4},{3,5},{4,2},{5,3},{6,0},{7,1},{8,14},{9,15},{10,... | collective-permute-start | bytes 196616 | tf_op jit(solution)/shard_map/ppermute | solution.py:449
  42.8 4.6 %images.8.refs_2_ = f32[32,3584]{1,0:T(8,128)S(1)} custom-call(bf16[3584,4096]{1,0:T(8,128)(2,1)S(1)} %bitcast.13, bf16[32,1024]{1,0:T(8,128)(2,1)S(1)} %settle.4.refs_0_, bf16[32,1024]{1,0:T(8,128)(2,1)S(1)} %collective-permute-done.6.refs_1_), custom_call_target="tpu_custom_call" | custom-call | flops 5637144576 | bytes 1000000 | tf_op jit(solution)/shard_map/images/pallas_call | solution.py:31
  47.4 5.0 %images.9 = (bf16[32,3584]{1,0:T(8,128)(2,1)S(1)}, bf16[32,128]{1,0:T(8,128)(2,1)S(1)}) custom-call(bf16[3584,4096]{1,0:T(8,128)(2,1)S(1)} %bitcast.14, bf16[32,1024]{1,0:T(8,128)(2,1)S(1)} %collective-permute-done.4.refs_0_, bf16[32,1024]{1,0:T(8,128)(2,1)S(1)} %collective-permute-done.5.refs_1_, f32[32,3584]{1,0:T(8,128)S(1)} %images.8.refs_2_), custom_call_target="tpu_custom_call" | custom-call | flops 5637144576 | bytes 1000000 | tf_op jit(solution)/shard_map/images/pallas_call | solution.py:31
  52.4 1.4 backs.20.refs_0_
  53.8 2.8 %collective-permute-start.7 = (bf16[32,1152]{1,0:T(8,128)(2,1)S(1)}, bf16[32,1152]{1,0:T(8,128)(2,1)S(1)}, u32[]{:S(2)}, u32[]{:S(2)}) collective-permute-start(bf16[32,1152]{1,0:T(8,128)(2,1)S(1)} %backs.20.refs_0_), channel_id=1, source_target_pairs={{0,6},{1,7},{2,4},{3,5},{4,2},{5,3},{6,0},{7,1},{8,14},{9,15},{10,... | collective-permute-start | bytes 221192 | tf_op jit(solution)/shard_map/ppermute | solution.py:449
  56.6 1.3 backs.21.refs_0_
  58.0 1.4 backs.22.refs_0_
  59.3 1.6 collective-permute-start.8
  60.9 1.3 backs.23.refs_0_
  62.3 1.2 collective-permute-done.9.refs_0_
  64.4 1.5 collective-permute-start.10
  65.9 2.8 %collective-permute-done.10.other_ref = bf16[32,1152]{1,0:T(8,128)(2,1)S(1)} collective-permute-done((bf16[32,1152]{1,0:T(8,128)(2,1)S(1)}, bf16[32,1152]{1,0:T(8,128)(2,1)S(1)}, u32[]{:S(2)}, u32[]{:S(2)}) %collective-permute-start.10) | collective-permute-done | bytes 73760 | tf_op jit(solution)/shard_map/ppermute | solution.py:449
  69.7 1.1 collective-permute-start.13
  70.8 2.8 %collective-permute-start.12 = (bf16[32,1024]{1,0:T(8,128)(2,1)S(1)}, bf16[32,1024]{1,0:T(8,128)(2,1)S(1)}, u32[]{:S(2)}, u32[]{:S(2)}) collective-permute-start(bf16[32,1024]{1,0:T(8,128)(2,1)S(1)} %settle.5.refs_0_), channel_id=1, source_target_pairs={{0,6},{1,7},{2,4},{3,5},{4,2},{5,3},{6,0},{7,1},{8,14},{9,15},{10,... | collective-permute-start | bytes 196616 | tf_op jit(solution)/shard_map/ppermute | solution.py:449
  74.1 4.6 %images.10.refs_2_ = f32[32,3584]{1,0:T(8,128)S(1)} custom-call(bf16[3584,4096]{1,0:T(8,128)(2,1)S(1)} %bitcast.22, bf16[32,1024]{1,0:T(8,128)(2,1)S(1)} %settle.5.refs_0_, bf16[32,1024]{1,0:T(8,128)(2,1)S(1)} %collective-permute-done.13.refs_1_), custom_call_target="tpu_custom_call" | custom-call | flops 5637144576 | bytes 1000000 | tf_op jit(solution)/shard_map/images/pallas_call | solution.py:31
  78.8 4.8 %images.11 = (bf16[32,3584]{1,0:T(8,128)(2,1)S(1)}, bf16[32,128]{1,0:T(8,128)(2,1)S(1)}) custom-call(bf16[3584,4096]{1,0:T(8,128)(2,1)S(1)} %bitcast.23, bf16[32,1024]{1,0:T(8,128)(2,1)S(1)} %collective-permute-done.11.refs_0_, bf16[32,1024]{1,0:T(8,128)(2,1)S(1)} %collective-permute-done.12.refs_1_, f32[32,3584]{1,0:T(8,128)S(1)} %images.10.refs_2_), custom_call_target="tpu_custom_call" | custom-call | flops 5637144576 | bytes 1000000 | tf_op jit(solution)/shard_map/images/pallas_call | solution.py:31
  83.7 1.4 backs.24.refs_0_
  85.0 2.3 %collective-permute-start.14 = (bf16[32,1152]{1,0:T(8,128)(2,1)S(1)}, bf16[32,1152]{1,0:T(8,128)(2,1)S(1)}, u32[]{:S(2)}, u32[]{:S(2)}) collective-permute-start(bf16[32,1152]{1,0:T(8,128)(2,1)S(1)} %backs.24.refs_0_), channel_id=1, source_target_pairs={{0,6},{1,7},{2,4},{3,5},{4,2},{5,3},{6,0},{7,1},{8,14},{9,15},{10,... | collective-permute-start | bytes 221192 | tf_op jit(solution)/shard_map/ppermute | solution.py:449
  87.3 1.3 backs.25.refs_0_
  88.9 1.3 backs.26.refs_0_
  90.2 2.0 %collective-permute-start.15 = (bf16[32,1152]{1,0:T(8,128)(2,1)S(1)}, bf16[32,1152]{1,0:T(8,128)(2,1)S(1)}, u32[]{:S(2)}, u32[]{:S(2)}) collective-permute-start(bf16[32,1152]{1,0:T(8,128)(2,1)S(1)} %backs.26.refs_0_), channel_id=1, source_target_pairs={{0,2},{1,3},{2,0},{3,1},{4,6},{5,7},{6,4},{7,5},{8,10},{9,11},{10,... | collective-permute-start | bytes 221192 | tf_op jit(solution)/shard_map/ppermute | solution.py:449
  92.2 1.3 backs.27.refs_0_
  93.5 1.4 collective-permute-done.16.refs_0_
  95.8 1.6 collective-permute-start.17
  97.3 2.8 %collective-permute-done.17.other_ref = bf16[32,1152]{1,0:T(8,128)(2,1)S(1)} collective-permute-done((bf16[32,1152]{1,0:T(8,128)(2,1)S(1)}, bf16[32,1152]{1,0:T(8,128)(2,1)S(1)}, u32[]{:S(2)}, u32[]{:S(2)}) %collective-permute-start.17) | collective-permute-done | bytes 73760 | tf_op jit(solution)/shard_map/ppermute | solution.py:449
  101.1 1.5 collective-permute-start.20
  102.7 1.7 collective-permute-start.19
  105.5 4.6 %images.12.refs_2_ = f32[32,3584]{1,0:T(8,128)S(1)} custom-call(bf16[3584,4096]{1,0:T(8,128)(2,1)S(1)} %bitcast.31, bf16[32,1024]{1,0:T(8,128)(2,1)S(1)} %settle.6.refs_0_, bf16[32,1024]{1,0:T(8,128)(2,1)S(1)} %collective-permute-done.20.refs_1_), custom_call_target="tpu_custom_call" | custom-call | flops 5637144576 | bytes 1000000 | tf_op jit(solution)/shard_map/images/pallas_call | solution.py:31
  110.1 5.0 %images.13 = (bf16[32,3584]{1,0:T(8,128)(2,1)S(1)}, bf16[32,128]{1,0:T(8,128)(2,1)S(1)}) custom-call(bf16[3584,4096]{1,0:T(8,128)(2,1)S(1)} %bitcast.32, bf16[32,1024]{1,0:T(8,128)(2,1)S(1)} %collective-permute-done.18.refs_0_, bf16[32,1024]{1,0:T(8,128)(2,1)S(1)} %collective-permute-done.19.refs_1_, f32[32,3584]{1,0:T(8,128)S(1)} %images.12.refs_2_), custom_call_target="tpu_custom_call" | custom-call | flops 5637144576 | bytes 1000000 | tf_op jit(solution)/shard_map/images/pallas_call | solution.py:31
  115.1 1.4 backs.28.refs_0_
  116.5 2.0 %collective-permute-start.21 = (bf16[32,1152]{1,0:T(8,128)(2,1)S(1)}, bf16[32,1152]{1,0:T(8,128)(2,1)S(1)}, u32[]{:S(2)}, u32[]{:S(2)}) collective-permute-start(bf16[32,1152]{1,0:T(8,128)(2,1)S(1)} %backs.28.refs_0_), channel_id=1, source_target_pairs={{0,6},{1,7},{2,4},{3,5},{4,2},{5,3},{6,0},{7,1},{8,14},{9,15},{10,... | collective-permute-start | bytes 221192 | tf_op jit(solution)/shard_map/ppermute | solution.py:449
  118.5 1.3 backs.29.refs_0_
  119.8 1.1 collective-permute-start.23
  120.9 1.3 backs.30.refs_0_
  122.2 1.4 collective-permute-start.22
  123.6 1.3 backs.31.refs_0_
  124.9 3.0 %collective-permute-done.23.refs_0_ = bf16[32,1152]{1,0:T(8,128)(2,1)S(1)} collective-permute-done((bf16[32,1152]{1,0:T(8,128)(2,1)S(1)}, bf16[32,1152]{1,0:T(8,128)(2,1)S(1)}, u32[]{:S(2)}, u32[]{:S(2)}) %collective-permute-start.23) | collective-permute-done | bytes 73760 | tf_op jit(solution)/shard_map/ppermute | solution.py:449
  128.2 1.5 collective-permute-start.24
  129.7 2.9 %collective-permute-done.24.other_ref = bf16[32,1152]{1,0:T(8,128)(2,1)S(1)} collective-permute-done((bf16[32,1152]{1,0:T(8,128)(2,1)S(1)}, bf16[32,1152]{1,0:T(8,128)(2,1)S(1)}, u32[]{:S(2)}, u32[]{:S(2)}) %collective-permute-start.24) | collective-permute-done | bytes 73760 | tf_op jit(solution)/shard_map/ppermute | solution.py:449
  133.6 1.9 %collective-permute-start.26 = (bf16[32,1024]{1,0:T(8,128)(2,1)S(1)}, bf16[32,1024]{1,0:T(8,128)(2,1)S(1)}, u32[]{:S(2)}, u32[]{:S(2)}) collective-permute-start(bf16[32,1024]{1,0:T(8,128)(2,1)S(1)} %settle.7.refs_0_), channel_id=1, source_target_pairs={{0,6},{1,7},{2,4},{3,5},{4,2},{5,3},{6,0},{7,1},{8,14},{9,15},{10,... | collective-permute-start | bytes 196616 | tf_op jit(solution)/shard_map/ppermute | solution.py:449
  135.5 1.6 collective-permute-start.25
  137.9 4.6 %images.14.refs_2_.refs_4_ = f32[32,3584]{1,0:T(8,128)S(1)} custom-call(bf16[3584,4096]{1,0:T(8,128)(2,1)S(1)} %bitcast.40, bf16[32,1024]{1,0:T(8,128)(2,1)S(1)} %settle.7.refs_0_, bf16[32,1024]{1,0:T(8,128)(2,1)S(1)} %collective-permute-done.27.refs_1_), custom_call_target="tpu_custom_call" | custom-call | flops 5637144576 | bytes 1000000 | tf_op jit(solution)/shard_map/images/pallas_call | solution.py:31
  142.5 1.5 collective-permute-start.29
  144.0 4.6 %images.15.refs_2_ = bf16[4,32,896]{2,1,0:T(8,128)(2,1)S(1)} custom-call(bf16[3584,4096]{1,0:T(8,128)(2,1)S(1)} %bitcast.42, bf16[32,1024]{1,0:T(8,128)(2,1)S(1)} %collective-permute-done.25.refs_0_.refs_2_, bf16[32,1024]{1,0:T(8,128)(2,1)S(1)} %collective-permute-done.26.refs_1_.refs_3_, f32[32,3584]{1,0:T(8,128)S(1)} %images.14.refs_2_.refs_4_), custom_call_target="tpu_custom_call" | custom-call | flops 5637144576 | bytes 1000000 | tf_op jit(solution)/shard_map/images/pallas_call | solution.py:31
  149.1 1.5 collective-permute-start.28
  151.0 2.9 %right_first.1 = (bf16[128,4096]{1,0:T(8,128)(2,1)S(1)}, f32[128,128]{1,0:T(8,128)S(1)}, f32[128,128]{1,0:T(8,128)S(1)}) custom-call(bf16[1,32,4096]{2,1,0:T(8,128)(2,1)S(1)} %pack.1.refs_0_, bf16[1,32,4096]{2,1,0:T(8,128)(2,1)S(1)} %collective-permute-done.29.refs_1_, bf16[2,32,4096]{2,1,0:T(8,128)(2,1)S(1)} %collective-permute-done.30.refs_2_), custom_call_target="tpu_custom_call" | custom-call | flops 100000000 | bytes 1000000 | tf_op jit(solution)/shard_map/right_first/pallas_call | solution.py:31
  153.9 2.4 %right_begin.1 = (f32[128,128]{1,0:T(8,128)S(1)}, f32[128,128]{1,0:T(8,128)S(1)}) custom-call(f32[128,128]{1,0:T(8,128)S(1)} %get-tuple-element.30.gram_ref), custom_call_target="tpu_custom_call" | custom-call | flops 100000000 | bytes 1000000 | tf_op jit(solution)/shard_map/right_begin/pallas_call | solution.py:31
  159.6 1.8 collective-permute-start.34
  161.4 2.6 %collective-permute-start.32 = (f32[96,128]{1,0:T(8,128)S(1)}, f32[96,128]{1,0:T(8,128)S(1)}, u32[]{:S(2)}, u32[]{:S(2)}) collective-permute-start(f32[96,128]{1,0:T(8,128)S(1)} %get-tuple-element.34.refs_0_), channel_id=1, source_target_pairs={{0,2},{1,3},{2,0},{3,1},{4,6},{5,7},{6,4},{7,5},{8,10},{9,11},{10,... | collective-permute-start | bytes 147464 | tf_op jit(solution)/shard_map/ppermute | solution.py:449
  164.0 2.1 %right_end.1.refs_4_.right_ref = f32[128,128]{1,0:T(8,128)S(1)} custom-call(f32[128,128]{1,0:T(8,128)S(1)} %get-tuple-element.30.gram_ref, f32[128,128]{1,0:T(8,128)S(1)} %get-tuple-element.33.refs_3_.upper_ref, f32[128,128]{1,0:T(8,128)S(1)} %get-tuple-element.35.lower_ref, f32[128,128]{1,0:T(8,128)S(1)} %get-tuple-element.36.change_ref.lower_ref, ...), custom_call_target="tpu_custom_call" | custom-call | flops 100000000 | bytes 1000000 | tf_op jit(solution)/shard_map/right_end/pallas_call | solution.py:31
  166.1 1.2 collective-permute-done.33.refs_2_
  167.3 1.6 collective-permute-start.35
  168.8 2.6 %collective-permute-done.35.other_ref = f32[96,128]{1,0:T(8,128)S(1)} collective-permute-done((f32[96,128]{1,0:T(8,128)S(1)}, f32[96,128]{1,0:T(8,128)S(1)}, u32[]{:S(2)}, u32[]{:S(2)}) %collective-permute-start.35) | collective-permute-done | bytes 49184 | tf_op jit(solution)/shard_map/ppermute | solution.py:449
  171.4 9.4 %finish.1 = bf16[896,4096]{1,0:T(8,128)(2,1)} custom-call(f32[96,128]{1,0:T(8,128)S(1)} %add.1.one_ref, f32[96,128]{1,0:T(8,128)S(1)} %collective-permute-done.35.other_ref, bf16[128,896]{1,0:T(8,128)(2,1)S(1)} %get-tuple-element.37.panel_ref, bf16[128,4096]{1,0:T(8,128)(2,1)S(1)} %get-tuple-element.38.wide_ref, ...), custom_call_target="tpu_custom_call" | custom-call | tf_op jit(solution)/shard_map/finish/pallas_call | solution.py:434
  (59 shorter events, 16.2 us)
Async XLA Ops:
  0.0 9.4 %copy-start = (bf16[1,3584,4096]{2,1,0:T(8,128)(2,1)S(1)}, bf16[1,3584,4096]{2,1,0:T(8,128)(2,1)}, u32[]{:S(2)}) copy-start(bf16[1,3584,4096]{2,1,0:T(8,128)(2,1)} %param.2) | copy-start | bytes 88080384
  9.4 1.0 copy-start.1
  20.1 8.4 %collective-permute-start = (bf16[32,1152]{1,0:T(8,128)(2,1)S(1)}, bf16[32,1152]{1,0:T(8,128)(2,1)S(1)}, u32[]{:S(2)}, u32[]{:S(2)}) collective-permute-start(bf16[32,1152]{1,0:T(8,128)(2,1)S(1)} %backs.16.refs_0_), channel_id=1, source_target_pairs={{0,6},{1,7},{2,4},{3,5},{4,2},{5,3},{6,0},{7,1},{8,14},{9,15},{10,... | collective-permute-start | bytes 221192 | tf_op jit(solution)/shard_map/ppermute | solution.py:449
  26.5 5.5 %collective-permute-start.2 = (bf16[32,1152]{1,0:T(8,128)(2,1)S(1)}, bf16[32,1152]{1,0:T(8,128)(2,1)S(1)}, u32[]{:S(2)}, u32[]{:S(2)}) collective-permute-start(bf16[32,1152]{1,0:T(8,128)(2,1)S(1)} %backs.17.refs_0_), channel_id=1, source_target_pairs={{0,4},{1,5},{2,6},{3,7},{4,0},{5,1},{6,2},{7,3},{8,12},{9,13},{10,... | collective-permute-start | bytes 221192 | tf_op jit(solution)/shard_map/ppermute | solution.py:449
  27.8 4.9 %collective-permute-start.1 = (bf16[32,1152]{1,0:T(8,128)(2,1)S(1)}, bf16[32,1152]{1,0:T(8,128)(2,1)S(1)}, u32[]{:S(2)}, u32[]{:S(2)}) collective-permute-start(bf16[32,1152]{1,0:T(8,128)(2,1)S(1)} %backs.18.refs_0_), channel_id=1, source_target_pairs={{0,2},{1,3},{2,0},{3,1},{4,6},{5,7},{6,4},{7,5},{8,10},{9,11},{10,... | collective-permute-start | bytes 221192 | tf_op jit(solution)/shard_map/ppermute | solution.py:449
  32.9 4.4 %collective-permute-start.3 = (bf16[32,1152]{1,0:T(8,128)(2,1)S(1)}, bf16[32,1152]{1,0:T(8,128)(2,1)S(1)}, u32[]{:S(2)}, u32[]{:S(2)}) collective-permute-start(bf16[32,1152]{1,0:T(8,128)(2,1)S(1)} %combine.4.one_ref), channel_id=1, source_target_pairs={{0,1},{1,0},{2,3},{3,2},{4,5},{5,4},{6,7},{7,6},{8,9},{9,8},{10,11... | collective-permute-start | bytes 221192 | tf_op jit(solution)/shard_map/ppermute | solution.py:449
  38.2 4.6 %collective-permute-start.6 = (bf16[32,1024]{1,0:T(8,128)(2,1)S(1)}, bf16[32,1024]{1,0:T(8,128)(2,1)S(1)}, u32[]{:S(2)}, u32[]{:S(2)}) collective-permute-start(bf16[32,1024]{1,0:T(8,128)(2,1)S(1)} %settle.4.refs_0_), channel_id=1, source_target_pairs={{0,2},{1,3},{2,0},{3,1},{4,6},{5,7},{6,4},{7,5},{8,10},{9,11},{10,... | collective-permute-start | bytes 196616 | tf_op jit(solution)/shard_map/ppermute | solution.py:449
  38.3 9.1 %collective-permute-start.5 = (bf16[32,1024]{1,0:T(8,128)(2,1)S(1)}, bf16[32,1024]{1,0:T(8,128)(2,1)S(1)}, u32[]{:S(2)}, u32[]{:S(2)}) collective-permute-start(bf16[32,1024]{1,0:T(8,128)(2,1)S(1)} %settle.4.refs_0_), channel_id=1, source_target_pairs={{0,6},{1,7},{2,4},{3,5},{4,2},{5,3},{6,0},{7,1},{8,14},{9,15},{10,... | collective-permute-start | bytes 196616 | tf_op jit(solution)/shard_map/ppermute | solution.py:449
  42.2 5.3 %collective-permute-start.4 = (bf16[32,1024]{1,0:T(8,128)(2,1)S(1)}, bf16[32,1024]{1,0:T(8,128)(2,1)S(1)}, u32[]{:S(2)}, u32[]{:S(2)}) collective-permute-start(bf16[32,1024]{1,0:T(8,128)(2,1)S(1)} %settle.4.refs_0_), channel_id=1, source_target_pairs={{0,4},{1,5},{2,6},{3,7},{4,0},{5,1},{6,2},{7,3},{8,12},{9,13},{10,... | collective-permute-start | bytes 196616 | tf_op jit(solution)/shard_map/ppermute | solution.py:449
  53.8 7.1 %collective-permute-start.7 = (bf16[32,1152]{1,0:T(8,128)(2,1)S(1)}, bf16[32,1152]{1,0:T(8,128)(2,1)S(1)}, u32[]{:S(2)}, u32[]{:S(2)}) collective-permute-start(bf16[32,1152]{1,0:T(8,128)(2,1)S(1)} %backs.20.refs_0_), channel_id=1, source_target_pairs={{0,6},{1,7},{2,4},{3,5},{4,2},{5,3},{6,0},{7,1},{8,14},{9,15},{10,... | collective-permute-start | bytes 221192 | tf_op jit(solution)/shard_map/ppermute | solution.py:449
  58.0 5.5 %collective-permute-start.9 = (bf16[32,1152]{1,0:T(8,128)(2,1)S(1)}, bf16[32,1152]{1,0:T(8,128)(2,1)S(1)}, u32[]{:S(2)}, u32[]{:S(2)}) collective-permute-start(bf16[32,1152]{1,0:T(8,128)(2,1)S(1)} %backs.21.refs_0_), channel_id=1, source_target_pairs={{0,4},{1,5},{2,6},{3,7},{4,0},{5,1},{6,2},{7,3},{8,12},{9,13},{10,... | collective-permute-start | bytes 221192 | tf_op jit(solution)/shard_map/ppermute | solution.py:449
  59.3 4.9 %collective-permute-start.8 = (bf16[32,1152]{1,0:T(8,128)(2,1)S(1)}, bf16[32,1152]{1,0:T(8,128)(2,1)S(1)}, u32[]{:S(2)}, u32[]{:S(2)}) collective-permute-start(bf16[32,1152]{1,0:T(8,128)(2,1)S(1)} %backs.22.refs_0_), channel_id=1, source_target_pairs={{0,2},{1,3},{2,0},{3,1},{4,6},{5,7},{6,4},{7,5},{8,10},{9,11},{10,... | collective-permute-start | bytes 221192 | tf_op jit(solution)/shard_map/ppermute | solution.py:449
  64.4 4.4 %collective-permute-start.10 = (bf16[32,1152]{1,0:T(8,128)(2,1)S(1)}, bf16[32,1152]{1,0:T(8,128)(2,1)S(1)}, u32[]{:S(2)}, u32[]{:S(2)}) collective-permute-start(bf16[32,1152]{1,0:T(8,128)(2,1)S(1)} %combine.5.one_ref), channel_id=1, source_target_pairs={{0,1},{1,0},{2,3},{3,2},{4,5},{5,4},{6,7},{7,6},{8,9},{9,8},{10,11... | collective-permute-start | bytes 221192 | tf_op jit(solution)/shard_map/ppermute | solution.py:449
  69.7 4.3 %collective-permute-start.13 = (bf16[32,1024]{1,0:T(8,128)(2,1)S(1)}, bf16[32,1024]{1,0:T(8,128)(2,1)S(1)}, u32[]{:S(2)}, u32[]{:S(2)}) collective-permute-start(bf16[32,1024]{1,0:T(8,128)(2,1)S(1)} %settle.5.refs_0_), channel_id=1, source_target_pairs={{0,2},{1,3},{2,0},{3,1},{4,6},{5,7},{6,4},{7,5},{8,10},{9,11},{10,... | collective-permute-start | bytes 196616 | tf_op jit(solution)/shard_map/ppermute | solution.py:449
  70.8 7.8 %collective-permute-start.12 = (bf16[32,1024]{1,0:T(8,128)(2,1)S(1)}, bf16[32,1024]{1,0:T(8,128)(2,1)S(1)}, u32[]{:S(2)}, u32[]{:S(2)}) collective-permute-start(bf16[32,1024]{1,0:T(8,128)(2,1)S(1)} %settle.5.refs_0_), channel_id=1, source_target_pairs={{0,6},{1,7},{2,4},{3,5},{4,2},{5,3},{6,0},{7,1},{8,14},{9,15},{10,... | collective-permute-start | bytes 196616 | tf_op jit(solution)/shard_map/ppermute | solution.py:449
  73.7 5.2 %collective-permute-start.11 = (bf16[32,1024]{1,0:T(8,128)(2,1)S(1)}, bf16[32,1024]{1,0:T(8,128)(2,1)S(1)}, u32[]{:S(2)}, u32[]{:S(2)}) collective-permute-start(bf16[32,1024]{1,0:T(8,128)(2,1)S(1)} %settle.5.refs_0_), channel_id=1, source_target_pairs={{0,4},{1,5},{2,6},{3,7},{4,0},{5,1},{6,2},{7,3},{8,12},{9,13},{10,... | collective-permute-start | bytes 196616 | tf_op jit(solution)/shard_map/ppermute | solution.py:449
  85.0 7.1 %collective-permute-start.14 = (bf16[32,1152]{1,0:T(8,128)(2,1)S(1)}, bf16[32,1152]{1,0:T(8,128)(2,1)S(1)}, u32[]{:S(2)}, u32[]{:S(2)}) collective-permute-start(bf16[32,1152]{1,0:T(8,128)(2,1)S(1)} %backs.24.refs_0_), channel_id=1, source_target_pairs={{0,6},{1,7},{2,4},{3,5},{4,2},{5,3},{6,0},{7,1},{8,14},{9,15},{10,... | collective-permute-start | bytes 221192 | tf_op jit(solution)/shard_map/ppermute | solution.py:449
  88.7 6.2 %collective-permute-start.16 = (bf16[32,1152]{1,0:T(8,128)(2,1)S(1)}, bf16[32,1152]{1,0:T(8,128)(2,1)S(1)}, u32[]{:S(2)}, u32[]{:S(2)}) collective-permute-start(bf16[32,1152]{1,0:T(8,128)(2,1)S(1)} %backs.25.refs_0_), channel_id=1, source_target_pairs={{0,4},{1,5},{2,6},{3,7},{4,0},{5,1},{6,2},{7,3},{8,12},{9,13},{10,... | collective-permute-start | bytes 221192 | tf_op jit(solution)/shard_map/ppermute | solution.py:449
  90.2 5.4 %collective-permute-start.15 = (bf16[32,1152]{1,0:T(8,128)(2,1)S(1)}, bf16[32,1152]{1,0:T(8,128)(2,1)S(1)}, u32[]{:S(2)}, u32[]{:S(2)}) collective-permute-start(bf16[32,1152]{1,0:T(8,128)(2,1)S(1)} %backs.26.refs_0_), channel_id=1, source_target_pairs={{0,2},{1,3},{2,0},{3,1},{4,6},{5,7},{6,4},{7,5},{8,10},{9,11},{10,... | collective-permute-start | bytes 221192 | tf_op jit(solution)/shard_map/ppermute | solution.py:449
  95.8 4.4 %collective-permute-start.17 = (bf16[32,1152]{1,0:T(8,128)(2,1)S(1)}, bf16[32,1152]{1,0:T(8,128)(2,1)S(1)}, u32[]{:S(2)}, u32[]{:S(2)}) collective-permute-start(bf16[32,1152]{1,0:T(8,128)(2,1)S(1)} %combine.6.one_ref), channel_id=1, source_target_pairs={{0,1},{1,0},{2,3},{3,2},{4,5},{5,4},{6,7},{7,6},{8,9},{9,8},{10,11... | collective-permute-start | bytes 221192 | tf_op jit(solution)/shard_map/ppermute | solution.py:449
  101.1 4.3 %collective-permute-start.20 = (bf16[32,1024]{1,0:T(8,128)(2,1)S(1)}, bf16[32,1024]{1,0:T(8,128)(2,1)S(1)}, u32[]{:S(2)}, u32[]{:S(2)}) collective-permute-start(bf16[32,1024]{1,0:T(8,128)(2,1)S(1)} %settle.6.refs_0_), channel_id=1, source_target_pairs={{0,2},{1,3},{2,0},{3,1},{4,6},{5,7},{6,4},{7,5},{8,10},{9,11},{10,... | collective-permute-start | bytes 196616 | tf_op jit(solution)/shard_map/ppermute | solution.py:449
  102.7 7.4 %collective-permute-start.19 = (bf16[32,1024]{1,0:T(8,128)(2,1)S(1)}, bf16[32,1024]{1,0:T(8,128)(2,1)S(1)}, u32[]{:S(2)}, u32[]{:S(2)}) collective-permute-start(bf16[32,1024]{1,0:T(8,128)(2,1)S(1)} %settle.6.refs_0_), channel_id=1, source_target_pairs={{0,6},{1,7},{2,4},{3,5},{4,2},{5,3},{6,0},{7,1},{8,14},{9,15},{10,... | collective-permute-start | bytes 196616 | tf_op jit(solution)/shard_map/ppermute | solution.py:449
  104.4 5.7 %collective-permute-start.18 = (bf16[32,1024]{1,0:T(8,128)(2,1)S(1)}, bf16[32,1024]{1,0:T(8,128)(2,1)S(1)}, u32[]{:S(2)}, u32[]{:S(2)}) collective-permute-start(bf16[32,1024]{1,0:T(8,128)(2,1)S(1)} %settle.6.refs_0_), channel_id=1, source_target_pairs={{0,4},{1,5},{2,6},{3,7},{4,0},{5,1},{6,2},{7,3},{8,12},{9,13},{10,... | collective-permute-start | bytes 196616 | tf_op jit(solution)/shard_map/ppermute | solution.py:449
  116.5 7.1 %collective-permute-start.21 = (bf16[32,1152]{1,0:T(8,128)(2,1)S(1)}, bf16[32,1152]{1,0:T(8,128)(2,1)S(1)}, u32[]{:S(2)}, u32[]{:S(2)}) collective-permute-start(bf16[32,1152]{1,0:T(8,128)(2,1)S(1)} %backs.28.refs_0_), channel_id=1, source_target_pairs={{0,6},{1,7},{2,4},{3,5},{4,2},{5,3},{6,0},{7,1},{8,14},{9,15},{10,... | collective-permute-start | bytes 221192 | tf_op jit(solution)/shard_map/ppermute | solution.py:449
  119.8 8.2 %collective-permute-start.23 = (bf16[32,1152]{1,0:T(8,128)(2,1)S(1)}, bf16[32,1152]{1,0:T(8,128)(2,1)S(1)}, u32[]{:S(2)}, u32[]{:S(2)}) collective-permute-start(bf16[32,1152]{1,0:T(8,128)(2,1)S(1)} %backs.29.refs_0_), channel_id=1, source_target_pairs={{0,4},{1,5},{2,6},{3,7},{4,0},{5,1},{6,2},{7,3},{8,12},{9,13},{10,... | collective-permute-start | bytes 221192 | tf_op jit(solution)/shard_map/ppermute | solution.py:449
  122.2 5.8 %collective-permute-start.22 = (bf16[32,1152]{1,0:T(8,128)(2,1)S(1)}, bf16[32,1152]{1,0:T(8,128)(2,1)S(1)}, u32[]{:S(2)}, u32[]{:S(2)}) collective-permute-start(bf16[32,1152]{1,0:T(8,128)(2,1)S(1)} %backs.30.refs_0_), channel_id=1, source_target_pairs={{0,2},{1,3},{2,0},{3,1},{4,6},{5,7},{6,4},{7,5},{8,10},{9,11},{10,... | collective-permute-start | bytes 221192 | tf_op jit(solution)/shard_map/ppermute | solution.py:449
  128.2 4.4 %collective-permute-start.24 = (bf16[32,1152]{1,0:T(8,128)(2,1)S(1)}, bf16[32,1152]{1,0:T(8,128)(2,1)S(1)}, u32[]{:S(2)}, u32[]{:S(2)}) collective-permute-start(bf16[32,1152]{1,0:T(8,128)(2,1)S(1)} %combine.7.one_ref), channel_id=1, source_target_pairs={{0,1},{1,0},{2,3},{3,2},{4,5},{5,4},{6,7},{7,6},{8,9},{9,8},{10,11... | collective-permute-start | bytes 221192 | tf_op jit(solution)/shard_map/ppermute | solution.py:449
  133.6 4.3 %collective-permute-start.27 = (bf16[32,1024]{1,0:T(8,128)(2,1)S(1)}, bf16[32,1024]{1,0:T(8,128)(2,1)S(1)}, u32[]{:S(2)}, u32[]{:S(2)}) collective-permute-start(bf16[32,1024]{1,0:T(8,128)(2,1)S(1)} %settle.7.refs_0_), channel_id=1, source_target_pairs={{0,2},{1,3},{2,0},{3,1},{4,6},{5,7},{6,4},{7,5},{8,10},{9,11},{10,... | collective-permute-start | bytes 196616 | tf_op jit(solution)/shard_map/ppermute | solution.py:449
  133.6 8.8 %collective-permute-start.26 = (bf16[32,1024]{1,0:T(8,128)(2,1)S(1)}, bf16[32,1024]{1,0:T(8,128)(2,1)S(1)}, u32[]{:S(2)}, u32[]{:S(2)}) collective-permute-start(bf16[32,1024]{1,0:T(8,128)(2,1)S(1)} %settle.7.refs_0_), channel_id=1, source_target_pairs={{0,6},{1,7},{2,4},{3,5},{4,2},{5,3},{6,0},{7,1},{8,14},{9,15},{10,... | collective-permute-start | bytes 196616 | tf_op jit(solution)/shard_map/ppermute | solution.py:449
  135.5 7.0 %collective-permute-start.25 = (bf16[32,1024]{1,0:T(8,128)(2,1)S(1)}, bf16[32,1024]{1,0:T(8,128)(2,1)S(1)}, u32[]{:S(2)}, u32[]{:S(2)}) collective-permute-start(bf16[32,1024]{1,0:T(8,128)(2,1)S(1)} %settle.7.refs_0_), channel_id=1, source_target_pairs={{0,4},{1,5},{2,6},{3,7},{4,0},{5,1},{6,2},{7,3},{8,12},{9,13},{10,... | collective-permute-start | bytes 196616 | tf_op jit(solution)/shard_map/ppermute | solution.py:449
  142.5 6.4 %collective-permute-start.29 = (bf16[1,32,4096]{2,1,0:T(8,128)(2,1)S(1)}, bf16[1,32,4096]{2,1,0:T(8,128)(2,1)S(1)}, u32[]{:S(2)}, u32[]{:S(2)}) collective-permute-start(bf16[1,32,4096]{2,1,0:T(8,128)(2,1)S(1)} %pack.1.refs_0_), channel_id=1, source_target_pairs={{0,16},{8,24},{16,0},{24,8},{1,17},{9,25},{17,1},{25,9},{2,18},{10... | collective-permute-start | bytes 786440 | tf_op jit(solution)/shard_map/ppermute | solution.py:449
  149.0 2.0 %collective-permute-start.30 = (bf16[2,32,4096]{2,1,0:T(8,128)(2,1)S(1)}, bf16[2,32,4096]{2,1,0:T(8,128)(2,1)S(1)}, u32[]{:S(2)}, u32[]{:S(2)}) collective-permute-start(bf16[2,32,4096]{2,1,0:T(8,128)(2,1)S(1)} %join.2), channel_id=1, source_target_pairs={{0,8},{8,0},{16,24},{24,16},{1,9},{9,1},{17,25},{25,17},{2,10},{10... | collective-permute-start | bytes 1572872 | tf_op jit(solution)/shard_map/ppermute | solution.py:449
  149.1 8.0 %collective-permute-start.28 = (bf16[1,4,32,896]{3,2,1,0:T(8,128)(2,1)S(1)}, bf16[1,4,32,896]{3,2,1,0:T(8,128)(2,1)S(1)}, u32[]{:S(2)}, u32[]{:S(2)}) collective-permute-start(bf16[1,4,32,896]{3,2,1,0:T(8,128)(2,1)S(1)} %bitcast.43), channel_id=1, source_target_pairs={{0,16},{8,24},{16,0},{24,8},{1,17},{9,25},{17,1},{25,9},{2,18},{10... | collective-permute-start | bytes 688136 | tf_op jit(solution)/shard_map/ppermute | solution.py:449
  157.1 1.9 %collective-permute-start.31 = (bf16[2,4,32,896]{3,2,1,0:T(8,128)(2,1)S(1)}, bf16[2,4,32,896]{3,2,1,0:T(8,128)(2,1)S(1)}, u32[]{:S(2)}, u32[]{:S(2)}) collective-permute-start(bf16[2,4,32,896]{3,2,1,0:T(8,128)(2,1)S(1)} %join.3), channel_id=1, source_target_pairs={{0,8},{8,0},{16,24},{24,16},{1,9},{9,1},{17,25},{25,17},{2,10},{10... | collective-permute-start | bytes 1376264 | tf_op jit(solution)/shard_map/ppermute | solution.py:449
  159.6 6.5 %collective-permute-start.34 = (f32[96,128]{1,0:T(8,128)S(1)}, f32[96,128]{1,0:T(8,128)S(1)}, u32[]{:S(2)}, u32[]{:S(2)}) collective-permute-start(f32[96,128]{1,0:T(8,128)S(1)} %get-tuple-element.34.refs_0_), channel_id=1, source_target_pairs={{0,6},{1,7},{2,4},{3,5},{4,2},{5,3},{6,0},{7,1},{8,14},{9,15},{10,... | collective-permute-start | bytes 147464 | tf_op jit(solution)/shard_map/ppermute | solution.py:449
  161.4 5.9 %collective-permute-start.33 = (f32[96,128]{1,0:T(8,128)S(1)}, f32[96,128]{1,0:T(8,128)S(1)}, u32[]{:S(2)}, u32[]{:S(2)}) collective-permute-start(f32[96,128]{1,0:T(8,128)S(1)} %get-tuple-element.34.refs_0_), channel_id=1, source_target_pairs={{0,4},{1,5},{2,6},{3,7},{4,0},{5,1},{6,2},{7,3},{8,12},{9,13},{10,... | collective-permute-start | bytes 147464 | tf_op jit(solution)/shard_map/ppermute | solution.py:449
  161.4 5.9 %collective-permute-start.32 = (f32[96,128]{1,0:T(8,128)S(1)}, f32[96,128]{1,0:T(8,128)S(1)}, u32[]{:S(2)}, u32[]{:S(2)}) collective-permute-start(f32[96,128]{1,0:T(8,128)S(1)} %get-tuple-element.34.refs_0_), channel_id=1, source_target_pairs={{0,2},{1,3},{2,0},{3,1},{4,6},{5,7},{6,4},{7,5},{8,10},{9,11},{10,... | collective-permute-start | bytes 147464 | tf_op jit(solution)/shard_map/ppermute | solution.py:449
  167.3 4.2 %collective-permute-start.35 = (f32[96,128]{1,0:T(8,128)S(1)}, f32[96,128]{1,0:T(8,128)S(1)}, u32[]{:S(2)}, u32[]{:S(2)}) collective-permute-start(f32[96,128]{1,0:T(8,128)S(1)} %add.1.one_ref), channel_id=1, source_target_pairs={{0,1},{1,0},{2,3},{3,2},{4,5},{5,4},{6,7},{7,6},{8,9},{9,8},{10,11... | collective-permute-start | bytes 147464 | tf_op jit(solution)/shard_map/ppermute | solution.py:449

commit v5 on v4

--- a/solution.py
+++ b/solution.py
@@ -57,10 +57,16 @@
     return jnp.concatenate([pieces[at] for at in order], axis=axis)
 
 
+def spread_left(value):
+    return spread(value, (0, 0, 1, 0, 2, 1), 1)
+
+
+def spread_right(value):
+    return spread(value, (0, 1, 0, 2, 0, 1), 0)
+
+
 def square(left, right):
-    return jnp.dot(
-        spread(left, (0, 0, 1, 0, 2, 1), 1), spread(right, (0, 1, 0, 2, 0, 1), 0), preferred_element_type=F32
-    )
+    return jnp.dot(spread_left(left), spread_right(right), preferred_element_type=F32)
 
 
 def eye_of(size):
@@ -122,8 +128,11 @@
     return pl.ds(pl.multiple_of(index * size, size), size)
 
 
-def first_kernel(tall, d_ref, x_ref, out_ref, gram_ref, wide):
-    wide[...] = x_ref[...].astype(BF16)
+def first_kernel(tall, d_ref, x_ref, out_ref, gram_ref, start, wide, sem):
+    copy = pltpu.make_async_copy(x_ref, start, sem)
+    copy.start()
+    copy.wait()
+    wide[...] = start[...].astype(BF16)
 
     def body(at, carry):
         rows = block_at(at, tall)
@@ -141,10 +150,11 @@
     return call(
         functools.partial(first_kernel, tall_of(rows, 1792, 896, 512, 256, 128)),
         "first",
-        [start],
+        [],
         [shape_of((rank, rows), BF16), shape_of((rank, LANES), BF16)],
-        [pltpu.VMEM((rank, cols), BF16)],
+        [pltpu.VMEM((rank, cols), F32), pltpu.VMEM((rank, cols), BF16), pltpu.SemaphoreType.DMA],
         held=held,
+        idle=[start],
         flops=2 * rows * cols * 384,
     )
 
@@ -345,8 +355,13 @@
 
     def step(_, state):
         upper, lower = state
-        middle = 0.5 * (3.0 * identity - square(lower, upper))
-        both = square(middle, jnp.concatenate([upper, lower], axis=1))
+        right = spread_right(upper)
+        middle = 0.5 * (3.0 * identity - jnp.dot(spread_left(lower), right, preferred_element_type=F32))
+        both = jnp.dot(
+            spread_left(middle),
+            jnp.concatenate([right, spread_right(lower)], axis=1),
+            preferred_element_type=F32,
+        )
         return both[:, :size], both[:, size:]
 
     return lax.fori_loop(0, count, step, state)
@@ -469,7 +484,7 @@
     count = len(masks)
     order = (*reversed(masks[1:]), 0)
     held = pltpu.with_memory_space_constraint(task_delta[0], pltpu.VMEM)
-    panel, gram = first(held, start_block[0].T)
+    panel, gram = first(held, pltpu.with_memory_space_constraint(start_block[0].T, pltpu.HBM))
     for step in range(ITERS):
         last = step == ITERS - 1
         received, after = {}, []

time: 181 us -> 181 us (level)
    unnamed x4 -> x2, local copies, waits for them, and re-layouts: 10.4 us -> 9.35 us
where the time goes in v5:
time: 181 us
  Pallas kernels  91.7 us (51%)
  starting transfers between devices  49.3 us (27%)
  waiting for transfers between devices  30.3 us (17%)
  local copies, waits for them, and re-layouts  9.35 us (5%)
    pallas_call x46, Pallas kernels, call(): pl.pallas_call(kernel, out_shape=tuple(shapes), in_specs=specs, out_specs...  82.4 us
    ppermute x36, starting transfers between devices, send(): return lax.ppermute(piece, axis, [(at, at ^ mask) for at in range(count)])  49.3 us
    ppermute x36, waiting for transfers between devices, send(): return lax.ppermute(piece, axis, [(at, at ^ mask) for at in range(count)])  30.3 us
    pallas_call x1, Pallas kernels, finish(): pl.pallas_call(functools.partial(finish_kernel, across), out_shape=shape_...  9.36 us
    unnamed x2, local copies, waits for them, and re-layouts  9.35 us
  transfers between devices with their start and end apart: 36, of which 23 were waited for; matrix products, arithmetic and copies ran while one was open for 0% of the time, Pallas kernels for 26%

profile of v5, /device:TPU:0, one launch (start us, length us, event | category | flops | bytes accessed | tf_op | source)
XLA Modules:
  0.0 181.0 jit_solution(15135127886460056862)
XLA Ops:
  0.0 9.3 %copy-done = bf16[1,3584,4096]{2,1,0:T(8,128)(2,1)S(1)} copy-done((bf16[1,3584,4096]{2,1,0:T(8,128)(2,1)S(1)}, bf16[1,3584,4096]{2,1,0:T(8,128)(2,1)}, u32[]{:S(2)}) %copy-start) | copy-done | bytes 29360152
  9.4 9.4 %first.1 = (bf16[32,3584]{1,0:T(8,128)(2,1)S(1)}, bf16[32,128]{1,0:T(8,128)(2,1)S(1)}) custom-call(bf16[3584,4096]{1,0:T(8,128)(2,1)S(1)} %bitcast.5, f32[32,4096]{1,0:T(8,128)} %bitcast.46), custom_call_target="tpu_custom_call" | custom-call | flops 11274289152 | bytes 1000000 | tf_op jit(solution)/shard_map/first/pallas_call | solution.py:31
  18.7 1.4 backs.16.refs_0_
  20.1 5.1 %collective-permute-start = (bf16[32,1152]{1,0:T(8,128)(2,1)S(1)}, bf16[32,1152]{1,0:T(8,128)(2,1)S(1)}, u32[]{:S(2)}, u32[]{:S(2)}) collective-permute-start(bf16[32,1152]{1,0:T(8,128)(2,1)S(1)} %backs.16.refs_0_), channel_id=1, source_target_pairs={{0,6},{1,7},{2,4},{3,5},{4,2},{5,3},{6,0},{7,1},{8,14},{9,15},{10,... | collective-permute-start | bytes 221192 | tf_op jit(solution)/shard_map/ppermute | solution.py:464
  25.1 1.3 backs.17.refs_0_
  26.5 1.4 backs.18.refs_0_
  28.4 1.3 backs.19.refs_0_
  29.8 2.2 %collective-permute-done.2.refs_0_ = bf16[32,1152]{1,0:T(8,128)(2,1)S(1)} collective-permute-done((bf16[32,1152]{1,0:T(8,128)(2,1)S(1)}, bf16[32,1152]{1,0:T(8,128)(2,1)S(1)}, u32[]{:S(2)}, u32[]{:S(2)}) %collective-permute-start.2) | collective-permute-done | bytes 73760 | tf_op jit(solution)/shard_map/ppermute | solution.py:464
  32.9 1.5 collective-permute-start.3
  34.4 2.8 %collective-permute-done.3.other_ref = bf16[32,1152]{1,0:T(8,128)(2,1)S(1)} collective-permute-done((bf16[32,1152]{1,0:T(8,128)(2,1)S(1)}, bf16[32,1152]{1,0:T(8,128)(2,1)S(1)}, u32[]{:S(2)}, u32[]{:S(2)}) %collective-permute-start.3) | collective-permute-done | bytes 73760 | tf_op jit(solution)/shard_map/ppermute | solution.py:464
  38.4 3.8 %collective-permute-start.5 = (bf16[32,1024]{1,0:T(8,128)(2,1)S(1)}, bf16[32,1024]{1,0:T(8,128)(2,1)S(1)}, u32[]{:S(2)}, u32[]{:S(2)}) collective-permute-start(bf16[32,1024]{1,0:T(8,128)(2,1)S(1)} %settle.4.refs_0_), channel_id=1, source_target_pairs={{0,6},{1,7},{2,4},{3,5},{4,2},{5,3},{6,0},{7,1},{8,14},{9,15},{10,... | collective-permute-start | bytes 196616 | tf_op jit(solution)/shard_map/ppermute | solution.py:464
  42.9 4.6 %images.8.refs_2_ = f32[32,3584]{1,0:T(8,128)S(1)} custom-call(bf16[3584,4096]{1,0:T(8,128)(2,1)S(1)} %bitcast.13, bf16[32,1024]{1,0:T(8,128)(2,1)S(1)} %settle.4.refs_0_, bf16[32,1024]{1,0:T(8,128)(2,1)S(1)} %collective-permute-done.6.refs_1_), custom_call_target="tpu_custom_call" | custom-call | flops 5637144576 | bytes 1000000 | tf_op jit(solution)/shard_map/images/pallas_call | solution.py:31
  47.5 5.0 %images.9 = (bf16[32,3584]{1,0:T(8,128)(2,1)S(1)}, bf16[32,128]{1,0:T(8,128)(2,1)S(1)}) custom-call(bf16[3584,4096]{1,0:T(8,128)(2,1)S(1)} %bitcast.14, bf16[32,1024]{1,0:T(8,128)(2,1)S(1)} %collective-permute-done.4.refs_0_, bf16[32,1024]{1,0:T(8,128)(2,1)S(1)} %collective-permute-done.5.refs_1_, f32[32,3584]{1,0:T(8,128)S(1)} %images.8.refs_2_), custom_call_target="tpu_custom_call" | custom-call | flops 5637144576 | bytes 1000000 | tf_op jit(solution)/shard_map/images/pallas_call | solution.py:31
  52.4 1.4 backs.20.refs_0_
  53.8 2.8 %collective-permute-start.7 = (bf16[32,1152]{1,0:T(8,128)(2,1)S(1)}, bf16[32,1152]{1,0:T(8,128)(2,1)S(1)}, u32[]{:S(2)}, u32[]{:S(2)}) collective-permute-start(bf16[32,1152]{1,0:T(8,128)(2,1)S(1)} %backs.20.refs_0_), channel_id=1, source_target_pairs={{0,6},{1,7},{2,4},{3,5},{4,2},{5,3},{6,0},{7,1},{8,14},{9,15},{10,... | collective-permute-start | bytes 221192 | tf_op jit(solution)/shard_map/ppermute | solution.py:464
  56.6 1.3 backs.21.refs_0_
  58.0 1.4 backs.22.refs_0_
  59.3 1.6 collective-permute-start.8
  60.9 1.3 backs.23.refs_0_
  62.3 1.2 collective-permute-done.9.refs_0_
  64.4 1.5 collective-permute-start.10
  66.0 2.8 %collective-permute-done.10.other_ref = bf16[32,1152]{1,0:T(8,128)(2,1)S(1)} collective-permute-done((bf16[32,1152]{1,0:T(8,128)(2,1)S(1)}, bf16[32,1152]{1,0:T(8,128)(2,1)S(1)}, u32[]{:S(2)}, u32[]{:S(2)}) %collective-permute-start.10) | collective-permute-done | bytes 73760 | tf_op jit(solution)/shard_map/ppermute | solution.py:464
  69.8 1.1 collective-permute-start.13
  70.9 2.8 %collective-permute-start.12 = (bf16[32,1024]{1,0:T(8,128)(2,1)S(1)}, bf16[32,1024]{1,0:T(8,128)(2,1)S(1)}, u32[]{:S(2)}, u32[]{:S(2)}) collective-permute-start(bf16[32,1024]{1,0:T(8,128)(2,1)S(1)} %settle.5.refs_0_), channel_id=1, source_target_pairs={{0,6},{1,7},{2,4},{3,5},{4,2},{5,3},{6,0},{7,1},{8,14},{9,15},{10,... | collective-permute-start | bytes 196616 | tf_op jit(solution)/shard_map/ppermute | solution.py:464
  74.1 4.6 %images.10.refs_2_ = f32[32,3584]{1,0:T(8,128)S(1)} custom-call(bf16[3584,4096]{1,0:T(8,128)(2,1)S(1)} %bitcast.22, bf16[32,1024]{1,0:T(8,128)(2,1)S(1)} %settle.5.refs_0_, bf16[32,1024]{1,0:T(8,128)(2,1)S(1)} %collective-permute-done.13.refs_1_), custom_call_target="tpu_custom_call" | custom-call | flops 5637144576 | bytes 1000000 | tf_op jit(solution)/shard_map/images/pallas_call | solution.py:31
  78.8 4.8 %images.11 = (bf16[32,3584]{1,0:T(8,128)(2,1)S(1)}, bf16[32,128]{1,0:T(8,128)(2,1)S(1)}) custom-call(bf16[3584,4096]{1,0:T(8,128)(2,1)S(1)} %bitcast.23, bf16[32,1024]{1,0:T(8,128)(2,1)S(1)} %collective-permute-done.11.refs_0_, bf16[32,1024]{1,0:T(8,128)(2,1)S(1)} %collective-permute-done.12.refs_1_, f32[32,3584]{1,0:T(8,128)S(1)} %images.10.refs_2_), custom_call_target="tpu_custom_call" | custom-call | flops 5637144576 | bytes 1000000 | tf_op jit(solution)/shard_map/images/pallas_call | solution.py:31
  83.7 1.4 backs.24.refs_0_
  85.0 2.3 %collective-permute-start.14 = (bf16[32,1152]{1,0:T(8,128)(2,1)S(1)}, bf16[32,1152]{1,0:T(8,128)(2,1)S(1)}, u32[]{:S(2)}, u32[]{:S(2)}) collective-permute-start(bf16[32,1152]{1,0:T(8,128)(2,1)S(1)} %backs.24.refs_0_), channel_id=1, source_target_pairs={{0,6},{1,7},{2,4},{3,5},{4,2},{5,3},{6,0},{7,1},{8,14},{9,15},{10,... | collective-permute-start | bytes 221192 | tf_op jit(solution)/shard_map/ppermute | solution.py:464
  87.4 1.3 backs.25.refs_0_
  88.9 1.3 backs.26.refs_0_
  90.2 1.9 %collective-permute-start.15 = (bf16[32,1152]{1,0:T(8,128)(2,1)S(1)}, bf16[32,1152]{1,0:T(8,128)(2,1)S(1)}, u32[]{:S(2)}, u32[]{:S(2)}) collective-permute-start(bf16[32,1152]{1,0:T(8,128)(2,1)S(1)} %backs.26.refs_0_), channel_id=1, source_target_pairs={{0,2},{1,3},{2,0},{3,1},{4,6},{5,7},{6,4},{7,5},{8,10},{9,11},{10,... | collective-permute-start | bytes 221192 | tf_op jit(solution)/shard_map/ppermute | solution.py:464
  92.2 1.3 backs.27.refs_0_
  93.5 1.4 collective-permute-done.16.refs_0_
  95.8 1.6 collective-permute-start.17
  97.4 2.8 %collective-permute-done.17.other_ref = bf16[32,1152]{1,0:T(8,128)(2,1)S(1)} collective-permute-done((bf16[32,1152]{1,0:T(8,128)(2,1)S(1)}, bf16[32,1152]{1,0:T(8,128)(2,1)S(1)}, u32[]{:S(2)}, u32[]{:S(2)}) %collective-permute-start.17) | collective-permute-done | bytes 73760 | tf_op jit(solution)/shard_map/ppermute | solution.py:464
  101.2 1.5 collective-permute-start.20
  102.7 1.7 collective-permute-start.19
  105.5 4.6 %images.12.refs_2_ = f32[32,3584]{1,0:T(8,128)S(1)} custom-call(bf16[3584,4096]{1,0:T(8,128)(2,1)S(1)} %bitcast.31, bf16[32,1024]{1,0:T(8,128)(2,1)S(1)} %settle.6.refs_0_, bf16[32,1024]{1,0:T(8,128)(2,1)S(1)} %collective-permute-done.20.refs_1_), custom_call_target="tpu_custom_call" | custom-call | flops 5637144576 | bytes 1000000 | tf_op jit(solution)/shard_map/images/pallas_call | solution.py:31
  110.1 5.0 %images.13 = (bf16[32,3584]{1,0:T(8,128)(2,1)S(1)}, bf16[32,128]{1,0:T(8,128)(2,1)S(1)}) custom-call(bf16[3584,4096]{1,0:T(8,128)(2,1)S(1)} %bitcast.32, bf16[32,1024]{1,0:T(8,128)(2,1)S(1)} %collective-permute-done.18.refs_0_, bf16[32,1024]{1,0:T(8,128)(2,1)S(1)} %collective-permute-done.19.refs_1_, f32[32,3584]{1,0:T(8,128)S(1)} %images.12.refs_2_), custom_call_target="tpu_custom_call" | custom-call | flops 5637144576 | bytes 1000000 | tf_op jit(solution)/shard_map/images/pallas_call | solution.py:31
  115.1 1.4 backs.28.refs_0_
  116.5 2.0 %collective-permute-start.21 = (bf16[32,1152]{1,0:T(8,128)(2,1)S(1)}, bf16[32,1152]{1,0:T(8,128)(2,1)S(1)}, u32[]{:S(2)}, u32[]{:S(2)}) collective-permute-start(bf16[32,1152]{1,0:T(8,128)(2,1)S(1)} %backs.28.refs_0_), channel_id=1, source_target_pairs={{0,6},{1,7},{2,4},{3,5},{4,2},{5,3},{6,0},{7,1},{8,14},{9,15},{10,... | collective-permute-start | bytes 221192 | tf_op jit(solution)/shard_map/ppermute | solution.py:464
  118.5 1.3 backs.29.refs_0_
  119.8 1.1 collective-permute-start.23
  120.9 1.3 backs.30.refs_0_
  122.3 1.4 collective-permute-start.22
  123.6 1.3 backs.31.refs_0_
  125.0 3.0 %collective-permute-done.23.refs_0_ = bf16[32,1152]{1,0:T(8,128)(2,1)S(1)} collective-permute-done((bf16[32,1152]{1,0:T(8,128)(2,1)S(1)}, bf16[32,1152]{1,0:T(8,128)(2,1)S(1)}, u32[]{:S(2)}, u32[]{:S(2)}) %collective-permute-start.23) | collective-permute-done | bytes 73760 | tf_op jit(solution)/shard_map/ppermute | solution.py:464
  128.2 1.5 collective-permute-start.24
  129.7 2.9 %collective-permute-done.24.other_ref = bf16[32,1152]{1,0:T(8,128)(2,1)S(1)} collective-permute-done((bf16[32,1152]{1,0:T(8,128)(2,1)S(1)}, bf16[32,1152]{1,0:T(8,128)(2,1)S(1)}, u32[]{:S(2)}, u32[]{:S(2)}) %collective-permute-start.24) | collective-permute-done | bytes 73760 | tf_op jit(solution)/shard_map/ppermute | solution.py:464
  133.7 1.9 %collective-permute-start.26 = (bf16[32,1024]{1,0:T(8,128)(2,1)S(1)}, bf16[32,1024]{1,0:T(8,128)(2,1)S(1)}, u32[]{:S(2)}, u32[]{:S(2)}) collective-permute-start(bf16[32,1024]{1,0:T(8,128)(2,1)S(1)} %settle.7.refs_0_), channel_id=1, source_target_pairs={{0,6},{1,7},{2,4},{3,5},{4,2},{5,3},{6,0},{7,1},{8,14},{9,15},{10,... | collective-permute-start | bytes 196616 | tf_op jit(solution)/shard_map/ppermute | solution.py:464
  135.5 1.6 collective-permute-start.25
  137.9 4.6 %images.14.refs_2_.refs_4_ = f32[32,3584]{1,0:T(8,128)S(1)} custom-call(bf16[3584,4096]{1,0:T(8,128)(2,1)S(1)} %bitcast.40, bf16[32,1024]{1,0:T(8,128)(2,1)S(1)} %settle.7.refs_0_, bf16[32,1024]{1,0:T(8,128)(2,1)S(1)} %collective-permute-done.27.refs_1_), custom_call_target="tpu_custom_call" | custom-call | flops 5637144576 | bytes 1000000 | tf_op jit(solution)/shard_map/images/pallas_call | solution.py:31
  142.5 1.6 collective-permute-start.29
  144.1 4.6 %images.15.refs_2_ = bf16[4,32,896]{2,1,0:T(8,128)(2,1)S(1)} custom-call(bf16[3584,4096]{1,0:T(8,128)(2,1)S(1)} %bitcast.42, bf16[32,1024]{1,0:T(8,128)(2,1)S(1)} %collective-permute-done.25.refs_0_.refs_2_, bf16[32,1024]{1,0:T(8,128)(2,1)S(1)} %collective-permute-done.26.refs_1_.refs_3_, f32[32,3584]{1,0:T(8,128)S(1)} %images.14.refs_2_.refs_4_), custom_call_target="tpu_custom_call" | custom-call | flops 5637144576 | bytes 1000000 | tf_op jit(solution)/shard_map/images/pallas_call | solution.py:31
  149.1 1.6 collective-permute-start.28
  151.0 2.9 %right_first.1 = (bf16[128,4096]{1,0:T(8,128)(2,1)S(1)}, f32[128,128]{1,0:T(8,128)S(1)}, f32[128,128]{1,0:T(8,128)S(1)}) custom-call(bf16[1,32,4096]{2,1,0:T(8,128)(2,1)S(1)} %pack.1.refs_0_, bf16[1,32,4096]{2,1,0:T(8,128)(2,1)S(1)} %collective-permute-done.29.refs_1_, bf16[2,32,4096]{2,1,0:T(8,128)(2,1)S(1)} %collective-permute-done.30.refs_2_), custom_call_target="tpu_custom_call" | custom-call | flops 100000000 | bytes 1000000 | tf_op jit(solution)/shard_map/right_first/pallas_call | solution.py:31
  153.9 2.4 %right_begin.1 = (f32[128,128]{1,0:T(8,128)S(1)}, f32[128,128]{1,0:T(8,128)S(1)}) custom-call(f32[128,128]{1,0:T(8,128)S(1)} %get-tuple-element.30.gram_ref), custom_call_target="tpu_custom_call" | custom-call | flops 100000000 | bytes 1000000 | tf_op jit(solution)/shard_map/right_begin/pallas_call | solution.py:31
  159.6 1.8 %collective-permute-start.34 = (f32[96,128]{1,0:T(8,128)S(1)}, f32[96,128]{1,0:T(8,128)S(1)}, u32[]{:S(2)}, u32[]{:S(2)}) collective-permute-start(f32[96,128]{1,0:T(8,128)S(1)} %get-tuple-element.34.refs_0_), channel_id=1, source_target_pairs={{0,6},{1,7},{2,4},{3,5},{4,2},{5,3},{6,0},{7,1},{8,14},{9,15},{10,... | collective-permute-start | bytes 147464 | tf_op jit(solution)/shard_map/ppermute | solution.py:464
  161.4 2.6 %collective-permute-start.32 = (f32[96,128]{1,0:T(8,128)S(1)}, f32[96,128]{1,0:T(8,128)S(1)}, u32[]{:S(2)}, u32[]{:S(2)}) collective-permute-start(f32[96,128]{1,0:T(8,128)S(1)} %get-tuple-element.34.refs_0_), channel_id=1, source_target_pairs={{0,2},{1,3},{2,0},{3,1},{4,6},{5,7},{6,4},{7,5},{8,10},{9,11},{10,... | collective-permute-start | bytes 147464 | tf_op jit(solution)/shard_map/ppermute | solution.py:464
  164.0 2.1 %right_end.1.refs_4_.right_ref = f32[128,128]{1,0:T(8,128)S(1)} custom-call(f32[128,128]{1,0:T(8,128)S(1)} %get-tuple-element.30.gram_ref, f32[128,128]{1,0:T(8,128)S(1)} %get-tuple-element.33.refs_3_.upper_ref, f32[128,128]{1,0:T(8,128)S(1)} %get-tuple-element.35.lower_ref, f32[128,128]{1,0:T(8,128)S(1)} %get-tuple-element.36.change_ref.lower_ref, ...), custom_call_target="tpu_custom_call" | custom-call | flops 100000000 | bytes 1000000 | tf_op jit(solution)/shard_map/right_end/pallas_call | solution.py:31
  166.1 1.2 collective-permute-done.33.refs_2_
  167.3 1.5 collective-permute-start.35
  168.9 2.6 %collective-permute-done.35.other_ref = f32[96,128]{1,0:T(8,128)S(1)} collective-permute-done((f32[96,128]{1,0:T(8,128)S(1)}, f32[96,128]{1,0:T(8,128)S(1)}, u32[]{:S(2)}, u32[]{:S(2)}) %collective-permute-start.35) | collective-permute-done | bytes 49184 | tf_op jit(solution)/shard_map/ppermute | solution.py:464
  171.5 9.4 %finish.1 = bf16[896,4096]{1,0:T(8,128)(2,1)} custom-call(f32[96,128]{1,0:T(8,128)S(1)} %add.1.one_ref, f32[96,128]{1,0:T(8,128)S(1)} %collective-permute-done.35.other_ref, bf16[128,896]{1,0:T(8,128)(2,1)S(1)} %get-tuple-element.37.panel_ref, bf16[128,4096]{1,0:T(8,128)(2,1)S(1)} %get-tuple-element.38.wide_ref, ...), custom_call_target="tpu_custom_call" | custom-call | tf_op jit(solution)/shard_map/finish/pallas_call | solution.py:449
  (57 shorter events, 15.1 us)
Async XLA Ops:
  0.0 9.4 %copy-start = (bf16[1,3584,4096]{2,1,0:T(8,128)(2,1)S(1)}, bf16[1,3584,4096]{2,1,0:T(8,128)(2,1)}, u32[]{:S(2)}) copy-start(bf16[1,3584,4096]{2,1,0:T(8,128)(2,1)} %param.2) | copy-start | bytes 88080384
  20.1 8.4 %collective-permute-start = (bf16[32,1152]{1,0:T(8,128)(2,1)S(1)}, bf16[32,1152]{1,0:T(8,128)(2,1)S(1)}, u32[]{:S(2)}, u32[]{:S(2)}) collective-permute-start(bf16[32,1152]{1,0:T(8,128)(2,1)S(1)} %backs.16.refs_0_), channel_id=1, source_target_pairs={{0,6},{1,7},{2,4},{3,5},{4,2},{5,3},{6,0},{7,1},{8,14},{9,15},{10,... | collective-permute-start | bytes 221192 | tf_op jit(solution)/shard_map/ppermute | solution.py:464
  26.5 5.5 %collective-permute-start.2 = (bf16[32,1152]{1,0:T(8,128)(2,1)S(1)}, bf16[32,1152]{1,0:T(8,128)(2,1)S(1)}, u32[]{:S(2)}, u32[]{:S(2)}) collective-permute-start(bf16[32,1152]{1,0:T(8,128)(2,1)S(1)} %backs.17.refs_0_), channel_id=1, source_target_pairs={{0,4},{1,5},{2,6},{3,7},{4,0},{5,1},{6,2},{7,3},{8,12},{9,13},{10,... | collective-permute-start | bytes 221192 | tf_op jit(solution)/shard_map/ppermute | solution.py:464
  27.9 4.9 %collective-permute-start.1 = (bf16[32,1152]{1,0:T(8,128)(2,1)S(1)}, bf16[32,1152]{1,0:T(8,128)(2,1)S(1)}, u32[]{:S(2)}, u32[]{:S(2)}) collective-permute-start(bf16[32,1152]{1,0:T(8,128)(2,1)S(1)} %backs.18.refs_0_), channel_id=1, source_target_pairs={{0,2},{1,3},{2,0},{3,1},{4,6},{5,7},{6,4},{7,5},{8,10},{9,11},{10,... | collective-permute-start | bytes 221192 | tf_op jit(solution)/shard_map/ppermute | solution.py:464
  32.9 4.4 %collective-permute-start.3 = (bf16[32,1152]{1,0:T(8,128)(2,1)S(1)}, bf16[32,1152]{1,0:T(8,128)(2,1)S(1)}, u32[]{:S(2)}, u32[]{:S(2)}) collective-permute-start(bf16[32,1152]{1,0:T(8,128)(2,1)S(1)} %combine.4.one_ref), channel_id=1, source_target_pairs={{0,1},{1,0},{2,3},{3,2},{4,5},{5,4},{6,7},{7,6},{8,9},{9,8},{10,11... | collective-permute-start | bytes 221192 | tf_op jit(solution)/shard_map/ppermute | solution.py:464
  38.2 4.6 %collective-permute-start.6 = (bf16[32,1024]{1,0:T(8,128)(2,1)S(1)}, bf16[32,1024]{1,0:T(8,128)(2,1)S(1)}, u32[]{:S(2)}, u32[]{:S(2)}) collective-permute-start(bf16[32,1024]{1,0:T(8,128)(2,1)S(1)} %settle.4.refs_0_), channel_id=1, source_target_pairs={{0,2},{1,3},{2,0},{3,1},{4,6},{5,7},{6,4},{7,5},{8,10},{9,11},{10,... | collective-permute-start | bytes 196616 | tf_op jit(solution)/shard_map/ppermute | solution.py:464
  38.4 9.1 %collective-permute-start.5 = (bf16[32,1024]{1,0:T(8,128)(2,1)S(1)}, bf16[32,1024]{1,0:T(8,128)(2,1)S(1)}, u32[]{:S(2)}, u32[]{:S(2)}) collective-permute-start(bf16[32,1024]{1,0:T(8,128)(2,1)S(1)} %settle.4.refs_0_), channel_id=1, source_target_pairs={{0,6},{1,7},{2,4},{3,5},{4,2},{5,3},{6,0},{7,1},{8,14},{9,15},{10,... | collective-permute-start | bytes 196616 | tf_op jit(solution)/shard_map/ppermute | solution.py:464
  42.2 5.3 %collective-permute-start.4 = (bf16[32,1024]{1,0:T(8,128)(2,1)S(1)}, bf16[32,1024]{1,0:T(8,128)(2,1)S(1)}, u32[]{:S(2)}, u32[]{:S(2)}) collective-permute-start(bf16[32,1024]{1,0:T(8,128)(2,1)S(1)} %settle.4.refs_0_), channel_id=1, source_target_pairs={{0,4},{1,5},{2,6},{3,7},{4,0},{5,1},{6,2},{7,3},{8,12},{9,13},{10,... | collective-permute-start | bytes 196616 | tf_op jit(solution)/shard_map/ppermute | solution.py:464
  53.8 7.1 %collective-permute-start.7 = (bf16[32,1152]{1,0:T(8,128)(2,1)S(1)}, bf16[32,1152]{1,0:T(8,128)(2,1)S(1)}, u32[]{:S(2)}, u32[]{:S(2)}) collective-permute-start(bf16[32,1152]{1,0:T(8,128)(2,1)S(1)} %backs.20.refs_0_), channel_id=1, source_target_pairs={{0,6},{1,7},{2,4},{3,5},{4,2},{5,3},{6,0},{7,1},{8,14},{9,15},{10,... | collective-permute-start | bytes 221192 | tf_op jit(solution)/shard_map/ppermute | solution.py:464
  58.0 5.5 %collective-permute-start.9 = (bf16[32,1152]{1,0:T(8,128)(2,1)S(1)}, bf16[32,1152]{1,0:T(8,128)(2,1)S(1)}, u32[]{:S(2)}, u32[]{:S(2)}) collective-permute-start(bf16[32,1152]{1,0:T(8,128)(2,1)S(1)} %backs.21.refs_0_), channel_id=1, source_target_pairs={{0,4},{1,5},{2,6},{3,7},{4,0},{5,1},{6,2},{7,3},{8,12},{9,13},{10,... | collective-permute-start | bytes 221192 | tf_op jit(solution)/shard_map/ppermute | solution.py:464
  59.3 4.9 %collective-permute-start.8 = (bf16[32,1152]{1,0:T(8,128)(2,1)S(1)}, bf16[32,1152]{1,0:T(8,128)(2,1)S(1)}, u32[]{:S(2)}, u32[]{:S(2)}) collective-permute-start(bf16[32,1152]{1,0:T(8,128)(2,1)S(1)} %backs.22.refs_0_), channel_id=1, source_target_pairs={{0,2},{1,3},{2,0},{3,1},{4,6},{5,7},{6,4},{7,5},{8,10},{9,11},{10,... | collective-permute-start | bytes 221192 | tf_op jit(solution)/shard_map/ppermute | solution.py:464
  64.4 4.4 %collective-permute-start.10 = (bf16[32,1152]{1,0:T(8,128)(2,1)S(1)}, bf16[32,1152]{1,0:T(8,128)(2,1)S(1)}, u32[]{:S(2)}, u32[]{:S(2)}) collective-permute-start(bf16[32,1152]{1,0:T(8,128)(2,1)S(1)} %combine.5.one_ref), channel_id=1, source_target_pairs={{0,1},{1,0},{2,3},{3,2},{4,5},{5,4},{6,7},{7,6},{8,9},{9,8},{10,11... | collective-permute-start | bytes 221192 | tf_op jit(solution)/shard_map/ppermute | solution.py:464
  69.8 4.3 %collective-permute-start.13 = (bf16[32,1024]{1,0:T(8,128)(2,1)S(1)}, bf16[32,1024]{1,0:T(8,128)(2,1)S(1)}, u32[]{:S(2)}, u32[]{:S(2)}) collective-permute-start(bf16[32,1024]{1,0:T(8,128)(2,1)S(1)} %settle.5.refs_0_), channel_id=1, source_target_pairs={{0,2},{1,3},{2,0},{3,1},{4,6},{5,7},{6,4},{7,5},{8,10},{9,11},{10,... | collective-permute-start | bytes 196616 | tf_op jit(solution)/shard_map/ppermute | solution.py:464
  70.9 7.8 %collective-permute-start.12 = (bf16[32,1024]{1,0:T(8,128)(2,1)S(1)}, bf16[32,1024]{1,0:T(8,128)(2,1)S(1)}, u32[]{:S(2)}, u32[]{:S(2)}) collective-permute-start(bf16[32,1024]{1,0:T(8,128)(2,1)S(1)} %settle.5.refs_0_), channel_id=1, source_target_pairs={{0,6},{1,7},{2,4},{3,5},{4,2},{5,3},{6,0},{7,1},{8,14},{9,15},{10,... | collective-permute-start | bytes 196616 | tf_op jit(solution)/shard_map/ppermute | solution.py:464
  73.7 5.2 %collective-permute-start.11 = (bf16[32,1024]{1,0:T(8,128)(2,1)S(1)}, bf16[32,1024]{1,0:T(8,128)(2,1)S(1)}, u32[]{:S(2)}, u32[]{:S(2)}) collective-permute-start(bf16[32,1024]{1,0:T(8,128)(2,1)S(1)} %settle.5.refs_0_), channel_id=1, source_target_pairs={{0,4},{1,5},{2,6},{3,7},{4,0},{5,1},{6,2},{7,3},{8,12},{9,13},{10,... | collective-permute-start | bytes 196616 | tf_op jit(solution)/shard_map/ppermute | solution.py:464
  85.0 7.1 %collective-permute-start.14 = (bf16[32,1152]{1,0:T(8,128)(2,1)S(1)}, bf16[32,1152]{1,0:T(8,128)(2,1)S(1)}, u32[]{:S(2)}, u32[]{:S(2)}) collective-permute-start(bf16[32,1152]{1,0:T(8,128)(2,1)S(1)} %backs.24.refs_0_), channel_id=1, source_target_pairs={{0,6},{1,7},{2,4},{3,5},{4,2},{5,3},{6,0},{7,1},{8,14},{9,15},{10,... | collective-permute-start | bytes 221192 | tf_op jit(solution)/shard_map/ppermute | solution.py:464
  88.7 6.2 %collective-permute-start.16 = (bf16[32,1152]{1,0:T(8,128)(2,1)S(1)}, bf16[32,1152]{1,0:T(8,128)(2,1)S(1)}, u32[]{:S(2)}, u32[]{:S(2)}) collective-permute-start(bf16[32,1152]{1,0:T(8,128)(2,1)S(1)} %backs.25.refs_0_), channel_id=1, source_target_pairs={{0,4},{1,5},{2,6},{3,7},{4,0},{5,1},{6,2},{7,3},{8,12},{9,13},{10,... | collective-permute-start | bytes 221192 | tf_op jit(solution)/shard_map/ppermute | solution.py:464
  90.2 5.4 %collective-permute-start.15 = (bf16[32,1152]{1,0:T(8,128)(2,1)S(1)}, bf16[32,1152]{1,0:T(8,128)(2,1)S(1)}, u32[]{:S(2)}, u32[]{:S(2)}) collective-permute-start(bf16[32,1152]{1,0:T(8,128)(2,1)S(1)} %backs.26.refs_0_), channel_id=1, source_target_pairs={{0,2},{1,3},{2,0},{3,1},{4,6},{5,7},{6,4},{7,5},{8,10},{9,11},{10,... | collective-permute-start | bytes 221192 | tf_op jit(solution)/shard_map/ppermute | solution.py:464
  95.8 4.4 %collective-permute-start.17 = (bf16[32,1152]{1,0:T(8,128)(2,1)S(1)}, bf16[32,1152]{1,0:T(8,128)(2,1)S(1)}, u32[]{:S(2)}, u32[]{:S(2)}) collective-permute-start(bf16[32,1152]{1,0:T(8,128)(2,1)S(1)} %combine.6.one_ref), channel_id=1, source_target_pairs={{0,1},{1,0},{2,3},{3,2},{4,5},{5,4},{6,7},{7,6},{8,9},{9,8},{10,11... | collective-permute-start | bytes 221192 | tf_op jit(solution)/shard_map/ppermute | solution.py:464
  101.2 4.3 %collective-permute-start.20 = (bf16[32,1024]{1,0:T(8,128)(2,1)S(1)}, bf16[32,1024]{1,0:T(8,128)(2,1)S(1)}, u32[]{:S(2)}, u32[]{:S(2)}) collective-permute-start(bf16[32,1024]{1,0:T(8,128)(2,1)S(1)} %settle.6.refs_0_), channel_id=1, source_target_pairs={{0,2},{1,3},{2,0},{3,1},{4,6},{5,7},{6,4},{7,5},{8,10},{9,11},{10,... | collective-permute-start | bytes 196616 | tf_op jit(solution)/shard_map/ppermute | solution.py:464
  102.7 7.4 %collective-permute-start.19 = (bf16[32,1024]{1,0:T(8,128)(2,1)S(1)}, bf16[32,1024]{1,0:T(8,128)(2,1)S(1)}, u32[]{:S(2)}, u32[]{:S(2)}) collective-permute-start(bf16[32,1024]{1,0:T(8,128)(2,1)S(1)} %settle.6.refs_0_), channel_id=1, source_target_pairs={{0,6},{1,7},{2,4},{3,5},{4,2},{5,3},{6,0},{7,1},{8,14},{9,15},{10,... | collective-permute-start | bytes 196616 | tf_op jit(solution)/shard_map/ppermute | solution.py:464
  104.4 5.7 %collective-permute-start.18 = (bf16[32,1024]{1,0:T(8,128)(2,1)S(1)}, bf16[32,1024]{1,0:T(8,128)(2,1)S(1)}, u32[]{:S(2)}, u32[]{:S(2)}) collective-permute-start(bf16[32,1024]{1,0:T(8,128)(2,1)S(1)} %settle.6.refs_0_), channel_id=1, source_target_pairs={{0,4},{1,5},{2,6},{3,7},{4,0},{5,1},{6,2},{7,3},{8,12},{9,13},{10,... | collective-permute-start | bytes 196616 | tf_op jit(solution)/shard_map/ppermute | solution.py:464
  116.5 7.1 %collective-permute-start.21 = (bf16[32,1152]{1,0:T(8,128)(2,1)S(1)}, bf16[32,1152]{1,0:T(8,128)(2,1)S(1)}, u32[]{:S(2)}, u32[]{:S(2)}) collective-permute-start(bf16[32,1152]{1,0:T(8,128)(2,1)S(1)} %backs.28.refs_0_), channel_id=1, source_target_pairs={{0,6},{1,7},{2,4},{3,5},{4,2},{5,3},{6,0},{7,1},{8,14},{9,15},{10,... | collective-permute-start | bytes 221192 | tf_op jit(solution)/shard_map/ppermute | solution.py:464
  119.8 8.1 %collective-permute-start.23 = (bf16[32,1152]{1,0:T(8,128)(2,1)S(1)}, bf16[32,1152]{1,0:T(8,128)(2,1)S(1)}, u32[]{:S(2)}, u32[]{:S(2)}) collective-permute-start(bf16[32,1152]{1,0:T(8,128)(2,1)S(1)} %backs.29.refs_0_), channel_id=1, source_target_pairs={{0,4},{1,5},{2,6},{3,7},{4,0},{5,1},{6,2},{7,3},{8,12},{9,13},{10,... | collective-permute-start | bytes 221192 | tf_op jit(solution)/shard_map/ppermute | solution.py:464
  122.3 5.8 %collective-permute-start.22 = (bf16[32,1152]{1,0:T(8,128)(2,1)S(1)}, bf16[32,1152]{1,0:T(8,128)(2,1)S(1)}, u32[]{:S(2)}, u32[]{:S(2)}) collective-permute-start(bf16[32,1152]{1,0:T(8,128)(2,1)S(1)} %backs.30.refs_0_), channel_id=1, source_target_pairs={{0,2},{1,3},{2,0},{3,1},{4,6},{5,7},{6,4},{7,5},{8,10},{9,11},{10,... | collective-permute-start | bytes 221192 | tf_op jit(solution)/shard_map/ppermute | solution.py:464
  128.2 4.4 %collective-permute-start.24 = (bf16[32,1152]{1,0:T(8,128)(2,1)S(1)}, bf16[32,1152]{1,0:T(8,128)(2,1)S(1)}, u32[]{:S(2)}, u32[]{:S(2)}) collective-permute-start(bf16[32,1152]{1,0:T(8,128)(2,1)S(1)} %combine.7.one_ref), channel_id=1, source_target_pairs={{0,1},{1,0},{2,3},{3,2},{4,5},{5,4},{6,7},{7,6},{8,9},{9,8},{10,11... | collective-permute-start | bytes 221192 | tf_op jit(solution)/shard_map/ppermute | solution.py:464
  133.6 4.3 %collective-permute-start.27 = (bf16[32,1024]{1,0:T(8,128)(2,1)S(1)}, bf16[32,1024]{1,0:T(8,128)(2,1)S(1)}, u32[]{:S(2)}, u32[]{:S(2)}) collective-permute-start(bf16[32,1024]{1,0:T(8,128)(2,1)S(1)} %settle.7.refs_0_), channel_id=1, source_target_pairs={{0,2},{1,3},{2,0},{3,1},{4,6},{5,7},{6,4},{7,5},{8,10},{9,11},{10,... | collective-permute-start | bytes 196616 | tf_op jit(solution)/shard_map/ppermute | solution.py:464
  133.7 8.8 %collective-permute-start.26 = (bf16[32,1024]{1,0:T(8,128)(2,1)S(1)}, bf16[32,1024]{1,0:T(8,128)(2,1)S(1)}, u32[]{:S(2)}, u32[]{:S(2)}) collective-permute-start(bf16[32,1024]{1,0:T(8,128)(2,1)S(1)} %settle.7.refs_0_), channel_id=1, source_target_pairs={{0,6},{1,7},{2,4},{3,5},{4,2},{5,3},{6,0},{7,1},{8,14},{9,15},{10,... | collective-permute-start | bytes 196616 | tf_op jit(solution)/shard_map/ppermute | solution.py:464
  135.5 6.9 %collective-permute-start.25 = (bf16[32,1024]{1,0:T(8,128)(2,1)S(1)}, bf16[32,1024]{1,0:T(8,128)(2,1)S(1)}, u32[]{:S(2)}, u32[]{:S(2)}) collective-permute-start(bf16[32,1024]{1,0:T(8,128)(2,1)S(1)} %settle.7.refs_0_), channel_id=1, source_target_pairs={{0,4},{1,5},{2,6},{3,7},{4,0},{5,1},{6,2},{7,3},{8,12},{9,13},{10,... | collective-permute-start | bytes 196616 | tf_op jit(solution)/shard_map/ppermute | solution.py:464
  142.5 6.4 %collective-permute-start.29 = (bf16[1,32,4096]{2,1,0:T(8,128)(2,1)S(1)}, bf16[1,32,4096]{2,1,0:T(8,128)(2,1)S(1)}, u32[]{:S(2)}, u32[]{:S(2)}) collective-permute-start(bf16[1,32,4096]{2,1,0:T(8,128)(2,1)S(1)} %pack.1.refs_0_), channel_id=1, source_target_pairs={{0,16},{8,24},{16,0},{24,8},{1,17},{9,25},{17,1},{25,9},{2,18},{10... | collective-permute-start | bytes 786440 | tf_op jit(solution)/shard_map/ppermute | solution.py:464
  149.0 2.0 %collective-permute-start.30 = (bf16[2,32,4096]{2,1,0:T(8,128)(2,1)S(1)}, bf16[2,32,4096]{2,1,0:T(8,128)(2,1)S(1)}, u32[]{:S(2)}, u32[]{:S(2)}) collective-permute-start(bf16[2,32,4096]{2,1,0:T(8,128)(2,1)S(1)} %join.2), channel_id=1, source_target_pairs={{0,8},{8,0},{16,24},{24,16},{1,9},{9,1},{17,25},{25,17},{2,10},{10... | collective-permute-start | bytes 1572872 | tf_op jit(solution)/shard_map/ppermute | solution.py:464
  149.1 8.0 %collective-permute-start.28 = (bf16[1,4,32,896]{3,2,1,0:T(8,128)(2,1)S(1)}, bf16[1,4,32,896]{3,2,1,0:T(8,128)(2,1)S(1)}, u32[]{:S(2)}, u32[]{:S(2)}) collective-permute-start(bf16[1,4,32,896]{3,2,1,0:T(8,128)(2,1)S(1)} %bitcast.43), channel_id=1, source_target_pairs={{0,16},{8,24},{16,0},{24,8},{1,17},{9,25},{17,1},{25,9},{2,18},{10... | collective-permute-start | bytes 688136 | tf_op jit(solution)/shard_map/ppermute | solution.py:464
  157.1 1.9 %collective-permute-start.31 = (bf16[2,4,32,896]{3,2,1,0:T(8,128)(2,1)S(1)}, bf16[2,4,32,896]{3,2,1,0:T(8,128)(2,1)S(1)}, u32[]{:S(2)}, u32[]{:S(2)}) collective-permute-start(bf16[2,4,32,896]{3,2,1,0:T(8,128)(2,1)S(1)} %join.3), channel_id=1, source_target_pairs={{0,8},{8,0},{16,24},{24,16},{1,9},{9,1},{17,25},{25,17},{2,10},{10... | collective-permute-start | bytes 1376264 | tf_op jit(solution)/shard_map/ppermute | solution.py:464
  159.6 6.5 %collective-permute-start.34 = (f32[96,128]{1,0:T(8,128)S(1)}, f32[96,128]{1,0:T(8,128)S(1)}, u32[]{:S(2)}, u32[]{:S(2)}) collective-permute-start(f32[96,128]{1,0:T(8,128)S(1)} %get-tuple-element.34.refs_0_), channel_id=1, source_target_pairs={{0,6},{1,7},{2,4},{3,5},{4,2},{5,3},{6,0},{7,1},{8,14},{9,15},{10,... | collective-permute-start | bytes 147464 | tf_op jit(solution)/shard_map/ppermute | solution.py:464
  161.4 5.9 %collective-permute-start.33 = (f32[96,128]{1,0:T(8,128)S(1)}, f32[96,128]{1,0:T(8,128)S(1)}, u32[]{:S(2)}, u32[]{:S(2)}) collective-permute-start(f32[96,128]{1,0:T(8,128)S(1)} %get-tuple-element.34.refs_0_), channel_id=1, source_target_pairs={{0,4},{1,5},{2,6},{3,7},{4,0},{5,1},{6,2},{7,3},{8,12},{9,13},{10,... | collective-permute-start | bytes 147464 | tf_op jit(solution)/shard_map/ppermute | solution.py:464
  161.4 5.9 %collective-permute-start.32 = (f32[96,128]{1,0:T(8,128)S(1)}, f32[96,128]{1,0:T(8,128)S(1)}, u32[]{:S(2)}, u32[]{:S(2)}) collective-permute-start(f32[96,128]{1,0:T(8,128)S(1)} %get-tuple-element.34.refs_0_), channel_id=1, source_target_pairs={{0,2},{1,3},{2,0},{3,1},{4,6},{5,7},{6,4},{7,5},{8,10},{9,11},{10,... | collective-permute-start | bytes 147464 | tf_op jit(solution)/shard_map/ppermute | solution.py:464
  167.3 4.2 %collective-permute-start.35 = (f32[96,128]{1,0:T(8,128)S(1)}, f32[96,128]{1,0:T(8,128)S(1)}, u32[]{:S(2)}, u32[]{:S(2)}) collective-permute-start(f32[96,128]{1,0:T(8,128)S(1)} %add.1.one_ref), channel_id=1, source_target_pairs={{0,1},{1,0},{2,3},{3,2},{4,5},{5,4},{6,7},{7,6},{8,9},{9,8},{10,11... | collective-permute-start | bytes 147464 | tf_op jit(solution)/shard_map/ppermute | solution.py:464
